TPU v7x, 128 devices: a whole 4x4x4 slice. The times are simulated.
128 devices in a mesh: dp: 8 (over x, y_lo), fsdp: 16 (over z, y_hi, core).
Axes of the slice: x: 4, y: 4 (y_hi: 2, y_lo: 2; y = y_hi * 2 + y_lo), z: 4, core: 2. Of those that a mesh axis runs over, the one named last changes fastest.
Arguments:
- activations: bfloat16 [16384, 8192], P(('dp', 'fsdp')), may hold values from -6 to 6
- out_grads: bfloat16 [16384, 28672], P(('dp', 'fsdp')), may hold values from -6 to 6
- act_signs: int32 [8192], replicated, may hold values 0 or 1
- grad_signs: int32 [28672], replicated, may hold values 0 or 1
- act_picks: int32 [2048], replicated, may hold values from 0 to 8191
- grad_picks: int32 [2048], replicated, may hold values from 0 to 28671
- gradient: bfloat16 [8192, 28672], P('dp', 'fsdp'), may hold values from -1100 to 1100, as said below
- damped_act: float32 [8192], P('dp'), may hold values from 0.25 to 2
- damped_grad: float32 [28672], P('fsdp'), may hold values from 0.25 to 2
- panel_act: bfloat16 [8192, 128], P(('dp', 'fsdp')), may hold values from -0.3125 to 0.3125
- panel_grad: bfloat16 [28672, 128], P(('fsdp', 'dp')), may hold values from -0.25 to 0.25
- core_act: float32 [128, 128], replicated, may hold values from -1 to 1, as said below
- core_grad: float32 [128, 128], replicated, may hold values from -1 to 1, as said below
Outputs:
- factor_act: float32 [8192, 2048], P(('fsdp', 'dp'))
- factor_grad: float32 [28672, 2048], P(('fsdp', 'dp'))
- update: float32 [8192, 28672], P('dp', 'fsdp')
Inputs may be any that keep to these rules, and one draw needn't show every extreme that they name: `gradient`: A real matrix. `core_act`: Symmetric. `core_grad`: Symmetric.
All inputs are finite; a program needn't handle non-finite values.
Results may differ from a plain program's by a relative error of at most 0.02.
Values may be sent and summed in bfloat16 or wider, within the bound.
No kernel may reach another device: no remote copies, remote signals or barrier semaphores. Data moves between devices by JAX's collectives and lax.ppermute only.
A program may use at most 128 MiB of HBM per device.

v0:
```python
import functools
import jax
import jax.numpy as jnp
import numpy as np
from jax import lax
from jax.experimental import pallas as pl
from jax.experimental.pallas import tpu as pltpu
from jax.sharding import Mesh
from jax.sharding import PartitionSpec as P

BF = jnp.bfloat16
F32 = jnp.float32
HB = 4096
INNER = 256
OUTER = HB // INNER
ROOM = 60 << 20


def hadamard_table(length):
    table = np.ones((1, 1), np.float32)
    while table.shape[0] < length:
        table = np.block([[table, table], [table, -table]])
    return jnp.asarray(table, BF)


def sketch_kernel(picks, x_ref, sign_ref, table_ref, out_ref, inner, spread, rows):
    block = pl.program_id(0)
    signs = (2 * sign_ref[...] - 1).astype(F32).astype(BF)
    for q in range(OUTER):
        cols = slice(q * INNER, (q + 1) * INNER)
        signed = table_ref[...] * signs[:, cols]
        inner[q] = lax.dot_general(
            signed, x_ref[:, cols], (((1,), (1,)), ((), ())), preferred_element_type=F32
        )

    strip = 8

    def mix(j, carry):
        at = pl.ds(pl.multiple_of(j * strip, strip), strip)
        parts = [inner[q, at, :] for q in range(OUTER)]
        half = 1
        while half < OUTER:
            for low in range(OUTER):
                if low & half == 0:
                    a, b = parts[low], parts[low | half]
                    parts[low], parts[low | half] = a + b, a - b
            half *= 2
        for p in range(OUTER):
            to = pl.multiple_of(block * HB + p * INNER + j * strip, strip)
            spread[pl.ds(to, strip), :] = parts[p]
        return carry

    lax.fori_loop(0, INNER // strip, mix, 0, unroll=2)

    @pl.when(block == pl.num_programs(0) - 1)
    def _():
        count = rows.shape[0]
        group = 16

        def take(i, carry):
            base = pl.multiple_of(i * group, group)
            for k in range(group):
                rows[pl.ds(base + k, 1), :] = spread[pl.ds(picks[base + k], 1), :]
            return carry

        lax.fori_loop(0, count // group, take, 0)
        out_ref[...] = rows[...].T.astype(BF)


def sketch(matrix, signs, picks, table):
    tokens, width = matrix.shape
    count = picks.shape[0]
    return pl.pallas_call(
        sketch_kernel,
        grid_spec=pltpu.PrefetchScalarGridSpec(
            num_scalar_prefetch=1,
            grid=(width // HB,),
            in_specs=[
                pl.BlockSpec((tokens, HB), lambda b, p: (0, b)),
                pl.BlockSpec((1, HB), lambda b, p: (0, b)),
                pl.BlockSpec((INNER, INNER), lambda b, p: (0, 0)),
            ],
            out_specs=pl.BlockSpec((tokens, count), lambda b, p: (0, 0)),
            scratch_shapes=[
                pltpu.VMEM((OUTER, INNER, tokens), F32),
                pltpu.VMEM((width, tokens), F32),
                pltpu.VMEM((count, tokens), F32),
            ],
        ),
        out_shape=jax.ShapeDtypeStruct((tokens, count), BF),
        compiler_params=pltpu.CompilerParams(vmem_limit_bytes=ROOM),
        cost_estimate=pl.CostEstimate(
            flops=4 * tokens * width * INNER, bytes_accessed=2 * tokens * (width + count), transcendentals=0
        ),
        name="sketch",
    )(picks, matrix, signs[None, :], table)


def turn_kernel(shifts, coords, grad_ref, *refs):
    outs, turned = refs[:-1], refs[-1]
    yhi = pl.program_id(1)
    x, y, core = coords[0], coords[1], coords[3]
    wide = grad_ref.shape[1] // 2
    own = wide // 8
    part = own // 2
    turned[...] = grad_ref[...].T
    for j in range(len(shifts)):

        @pl.when(pl.program_id(0) == j)
        def _(j=j):
            for away in range(2):
                for dx in range(4):
                    for ylo in range(2):
                        dy = (2 * yhi + ylo - y) & 3
                        at = (core ^ away) * wide + ((x + dx) & 3) * (2 * own) + ylo * own
                        at = pl.multiple_of(at, 16)
                        out = outs[2 * j + away]
                        out[dx * 4 + dy] = turned[pl.ds(at, part), :]
                        out[16 + dy * 4 + dx] = turned[pl.ds(at + part, part), :]


def turn(coords, grads, shifts):
    tokens = grads.shape[0]
    wide = grads.shape[1] // 8
    part = wide // 32
    first, last = shifts[0], shifts[-1]

    def slab(i, j, c):
        return (0, ((c[2] + jnp.where(i == 0, first, last)) & 3) * 2 + j)

    count = 2 * len(shifts)
    outs = pl.pallas_call(
        functools.partial(turn_kernel, shifts),
        grid_spec=pltpu.PrefetchScalarGridSpec(
            num_scalar_prefetch=1,
            grid=(len(shifts), 2),
            in_specs=[pl.BlockSpec((tokens, wide), slab)],
            out_specs=[pl.BlockSpec((32, part, tokens), lambda i, j, c: (0, 0, 0))] * count,
            scratch_shapes=[pltpu.VMEM((wide, tokens), BF)],
        ),
        out_shape=[jax.ShapeDtypeStruct((32, part, tokens), BF)] * count,
        compiler_params=pltpu.CompilerParams(vmem_limit_bytes=ROOM),
        cost_estimate=pl.CostEstimate(
            flops=0, bytes_accessed=4 * tokens * 2 * len(shifts) * wide, transcendentals=0
        ),
        name="turn",
    )(coords, grads)
    return [o.reshape(-1, tokens) for o in outs]


def turn_act_kernel(act_ref, out_ref, turned):
    z, yhi = pl.program_id(0), pl.program_id(1)
    slim = act_ref.shape[1] // 2
    small = slim // 8
    turned[...] = act_ref[...].T
    for ylo in range(2):
        for side in range(2):
            for xp in range(4):
                at = side * slim + xp * (2 * small) + ylo * small
                out_ref[ylo * 4 + yhi * 2 + side, xp * 4 + z] = turned[at : at + small, :]


def turn_act(acts):
    tokens = acts.shape[0]
    slim = acts.shape[1] // 8
    small = slim // 16
    return pl.pallas_call(
        turn_act_kernel,
        grid=(4, 2),
        in_specs=[pl.BlockSpec((tokens, slim), lambda i, j: (0, i * 2 + j))],
        out_specs=pl.BlockSpec((8, 16, small, tokens), lambda i, j: (0, 0, 0, 0)),
        out_shape=jax.ShapeDtypeStruct((8, 16, small, tokens), BF),
        scratch_shapes=[pltpu.VMEM((slim, tokens), BF)],
        compiler_params=pltpu.CompilerParams(vmem_limit_bytes=ROOM),
        cost_estimate=pl.CostEstimate(
            flops=0, bytes_accessed=4 * tokens * 8 * slim, transcendentals=0
        ),
        name="turn_act",
    )(acts)


def part_kernel(scale, split, coords, *refs):
    rows, given, outs = refs[0:8], refs[8:16], refs[16:]
    total = None
    for d in range(0, 8, 2):
        block = jnp.concatenate([rows[d][...], rows[d + 1][...]], axis=1)
        keys = jnp.concatenate([given[d][...], given[d + 1][...]], axis=0)
        term = jnp.dot(block, keys, preferred_element_type=F32)
        total = term if total is None else total + term
    total = (total * scale).astype(BF)
    if split == 0:
        outs[0][...] = total
        return
    each = total.shape[0] // split
    for j in range(len(outs) // split):

        @pl.when(pl.program_id(0) == j)
        def _(j=j):
            for k in range(split):
                outs[j * split + k][...] = total[k * each : (k + 1) * each]


def part_product(coords, rows, row_specs, keys, key_specs, scale, tile, steps, split):
    tokens, width = rows[0].shape[-1], keys[0].shape[-1]
    if split:
        each, count = tile // split, steps * split
        out_spec = pl.BlockSpec((each, width), lambda i, c: (0, 0))
    else:
        each, count = tile * steps, 1
        out_spec = pl.BlockSpec((tile, width), lambda i, c: (i, 0))
    return pl.pallas_call(
        functools.partial(part_kernel, scale, split),
        grid_spec=pltpu.PrefetchScalarGridSpec(
            num_scalar_prefetch=1,
            grid=(steps,),
            in_specs=row_specs + key_specs,
            out_specs=[out_spec] * count,
        ),
        out_shape=[jax.ShapeDtypeStruct((each, width), BF)] * count,
        compiler_params=pltpu.CompilerParams(vmem_limit_bytes=ROOM),
        cost_estimate=pl.CostEstimate(
            flops=2 * steps * tile * 8 * tokens * width,
            bytes_accessed=2 * (steps * tile * (8 * tokens + width) + 8 * tokens * width),
            transcendentals=0,
        ),
        name="part_product",
    )(coords, *rows, *keys)


def part_grad(coords, rows, keys, scale, tiles, split=1):
    tile, tokens = rows[0].shape[0] // 8, rows[0].shape[1]
    width = keys.shape[-1]

    def at(i):
        place = tiles[0]
        for j in range(1, len(tiles)):
            place = jnp.where(i >= j, tiles[j], place)
        return place

    def member(d, c):
        return ((c[2] - d // 2) & 3) * 2 + (c[3] ^ (d % 2))

    row_spec = pl.BlockSpec((tile, tokens), lambda i, c: (at(i), 0))
    key_specs = [
        pl.BlockSpec((None, tokens, width), lambda i, c, d=d: (member(d, c), 0, 0))
        for d in range(8)
    ]
    return part_product(
        coords, rows, [row_spec] * 8, [keys] * 8, key_specs, scale, tile, len(tiles), split
    )


def part_act(coords, rows, keys, sibling, scale):
    tile, tokens = rows.shape[1] // 4, rows.shape[2]
    width = sibling.shape[-1]

    def member(d, away, c):
        y = (c[1] - d) & 3
        return (y & 1) * 4 + (y >> 1) * 2 + (c[3] ^ away)

    row_specs = [
        pl.BlockSpec((None, tile, tokens), lambda i, c, d=d, a=a: (member(d, a, c), i, 0))
        for a in range(2)
        for d in range(4)
    ]
    key_specs = [pl.BlockSpec((tokens, width), lambda i, c: (0, 0))] * 4
    key_specs += [pl.BlockSpec((tokens, width), lambda i, c, d=d: (d, 0)) for d in range(4)]
    return part_product(
        coords, [rows] * 8, row_specs, [*keys, *([sibling] * 4)], key_specs, scale, tile, 4, 0
    )[0]


def add_kernel(*refs):
    count = len(refs) // 3
    for j in range(count):
        base, term, out = refs[j], refs[count + j], refs[2 * count + j]
        out[...] = (base[...].astype(F32) + term[...].astype(F32)).astype(BF)


def add_terms(bases, terms):
    rows, width = terms[0].shape
    block = rows // 2
    count = len(bases)
    spec = pl.BlockSpec((block, width), lambda i: (i, 0))
    return pl.pallas_call(
        add_kernel,
        grid=(2,),
        in_specs=[spec] * (2 * count),
        out_specs=[spec] * count,
        out_shape=[jax.ShapeDtypeStruct(b.shape, BF) for b in bases],
        compiler_params=pltpu.CompilerParams(vmem_limit_bytes=ROOM),
        cost_estimate=pl.CostEstimate(
            flops=count * rows * width, bytes_accessed=6 * count * rows * width, transcendentals=0
        ),
        name="add_terms",
    )(*bases, *terms)


def merge_kernel(*refs):
    count = len(refs) // 9
    ins, outs = refs[: 5 * count], refs[5 * count :]
    for p in range(count):
        here, *halves = [r[...].astype(F32) for r in ins[5 * p : 5 * p + 5]]
        half = here.shape[0] // 2
        total = [here[:half] + halves[0] + halves[2], here[half:] + halves[1] + halves[3]]
        block = half // 2
        outs[4 * p][...] = total[0][:block]
        outs[4 * p + 1][...] = total[0][block:].astype(BF)
        outs[4 * p + 2][...] = total[1][:block].astype(BF)
        outs[4 * p + 3][...] = total[1][block:].astype(BF)


def merge(groups):
    rows, width = groups[0][0].shape
    block, cols = rows // 4, width // 4
    count = len(groups)
    outs = pl.pallas_call(
        merge_kernel,
        grid=(4,),
        in_specs=(
            [pl.BlockSpec((rows, cols), lambda i: (0, i))]
            + [pl.BlockSpec((rows // 2, cols), lambda i: (0, i))] * 4
        )
        * count,
        out_specs=[pl.BlockSpec((block, cols), lambda i: (0, i))] * (4 * count),
        out_shape=(
            [jax.ShapeDtypeStruct((block, width), F32)]
            + [jax.ShapeDtypeStruct((block, width), BF)] * 3
        )
        * count,
        compiler_params=pltpu.CompilerParams(vmem_limit_bytes=ROOM),
        cost_estimate=pl.CostEstimate(
            flops=2 * count * rows * width,
            bytes_accessed=9 * count * rows * width,
            transcendentals=0,
        ),
        name="merge",
    )(*[a for g in groups for a in g])
    return [outs[4 * p : 4 * p + 4] for p in range(count)]


def finish_kernel(*refs):
    out = refs[-1]
    block = refs[0].shape[0]
    for part in range(2):
        own, *got = refs[4 * part : 4 * part + 4]
        total = own[...]
        for g in got:
            total = total + g[...].astype(F32)
        out[part * block : (part + 1) * block] = total


def finish(first, second):
    rows, width = first[0].shape
    cols = width // 2
    return pl.pallas_call(
        finish_kernel,
        grid=(2,),
        in_specs=[pl.BlockSpec((rows, cols), lambda i: (0, i))] * 8,
        out_specs=pl.BlockSpec((2 * rows, cols), lambda i: (0, i)),
        out_shape=jax.ShapeDtypeStruct((2 * rows, width), F32),
        cost_estimate=pl.CostEstimate(
            flops=6 * rows * width, bytes_accessed=28 * rows * width, transcendentals=0
        ),
        compiler_params=pltpu.CompilerParams(vmem_limit_bytes=ROOM),
        name="finish",
    )(*first, *second)


AXES = ("x", "ylo", "z", "yhi", "core")
GROUP = ("z", "yhi", "core")
DATA = ("x", "ylo")
RING_Y = ("ylo", "yhi")
AROUND_Y = ("ylo", "yhi", "core")
ALONG_Z = ("z", "core")
epsilon = 1e-06
clip_rms = 1.0


def shift(array, axis, step):
    if axis == "y":
        spot = lambda y: (y % 2) * 2 + y // 2
        return lax.ppermute(
            array, RING_Y, [(spot(y), spot((y + step) % 4)) for y in range(4)]
        )
    return lax.ppermute(array, axis, [(i, (i + step) % 4) for i in range(4)])


def swap(array):
    return lax.ppermute(array, "core", [(0, 1), (1, 0)])


def send(array, step, away):
    pairs = [(2 * z + c, 2 * ((z + step) % 4) + (c ^ away)) for z in range(4) for c in range(2)]
    return lax.ppermute(array, ALONG_Z, pairs)


def phase(*values):
    return lax.optimization_barrier(values)


def contract_rows(first_block, second_block):
    return lax.dot_general(
        first_block, second_block, (((0,), (0,)), ((), ())), preferred_element_type=F32
    )


def split_parts(matrix):
    high_part = matrix.astype(BF)
    low_part = (matrix - high_part.astype(F32)).astype(BF)
    return high_part, low_part


def expand_rows(panel, core_product):
    high_part, low_part = split_parts(core_product)
    return jnp.dot(panel, high_part, preferred_element_type=F32) + jnp.dot(
        panel, low_part, preferred_element_type=F32
    )


def expand_cols(core_product, panel):
    high_part, low_part = split_parts(core_product)
    dims = (((1,), (1,)), ((), ()))
    return lax.dot_general(
        high_part, panel, dims, preferred_element_type=F32
    ) + lax.dot_general(low_part, panel, dims, preferred_element_type=F32)


def share(block, axes, n):
    copies = jnp.broadcast_to(block[None], (n,) + block.shape)
    return lax.all_to_all(copies, axes, 0, 0, tiled=True)


def deal(blocks, axes):
    return lax.all_to_all(blocks, axes, 0, 0, tiled=True).astype(F32).sum(0)


def local(
    activations,
    out_grads,
    act_signs,
    grad_signs,
    act_picks,
    grad_picks,
    gradient,
    damped_act,
    damped_grad,
    panel_act,
    panel_grad,
    core_act,
    core_grad,
):
    y = lax.axis_index("yhi") * 2 + lax.axis_index("ylo")
    coords = jnp.stack(
        [lax.axis_index("x"), y, lax.axis_index("z"), lax.axis_index("core")]
    ).astype(jnp.int32)
    token_scale = 1.0 / (activations.shape[0] * lax.axis_size(AXES))
    table = hadamard_table(INNER)
    n_data, n_group = lax.axis_size(DATA), lax.axis_size(GROUP)
    rows, cols = gradient.shape
    rank = panel_act.shape[1]
    inv_act = 1.0 / damped_act
    inv_grad = 1.0 / damped_grad

    rows_act = share(panel_act, GROUP, n_group).reshape(rows, rank)
    sketch_act = sketch(activations, act_signs, act_picks, table)
    for_y = turn_act(activations)
    here, here_away, two, two_away = turn(coords, out_grads, (0, 2))
    (rows_act, two, two_away, here_away, sketch_act, for_y, coords, gradient, grad_picks) = phase(
        rows_act, two, two_away, here_away, sketch_act, for_y, coords, gradient, grad_picks
    )

    got = [send(two, 2, 0), send(two_away, 2, 1)]
    keys_y = [sketch_act] + [shift(sketch_act, "y", d) for d in (1, 2, 3)]
    rows_y = lax.all_to_all(for_y, AROUND_Y, 0, 0, tiled=True).reshape(8, -1, for_y.shape[-1])
    one, one_away, three, three_away = turn(coords, out_grads, (1, 3))
    sketch_grad = sketch(out_grads, grad_signs, grad_picks, table)
    scaled_act = (rows_act * inv_act[:, None]).astype(BF)
    left_part = contract_rows(scaled_act, gradient).astype(BF)
    left_part = left_part.reshape(n_data, rank // n_data, cols)
    panel = jnp.broadcast_to(panel_grad.reshape(1, -1, cols), (n_data, rank // n_data, cols))
    mixed = jnp.concatenate([left_part, panel], axis=1)
    (got, one, one_away, three, three_away, rows_y, mixed, sketch_grad, keys_y, scaled_act) = phase(
        got, one, one_away, three, three_away, rows_y, mixed, sketch_grad, keys_y, scaled_act
    )
    got_two, got_two_away = got

    keys_z = lax.all_gather(sketch_grad, ALONG_Z, axis=0)
    got = [send(one, 1, 0), send(three, 3, 0), send(here_away, 0, 1)]
    both = jnp.concatenate(keys_y, axis=0)
    mixed = lax.all_to_all(mixed, DATA, 0, 0, tiled=True)
    (got, one_away, three_away, both, mixed) = phase(got, one_away, three_away, both, mixed)
    got_one, got_three, got_here_away = got
    left_sum = mixed[:, : rank // n_data].astype(F32).sum(0).astype(BF)
    keys_sib = swap(both)
    (left_sum, mixed, keys_sib, one_away, three_away) = phase(
        left_sum, mixed, keys_sib, one_away, three_away
    )

    got = [send(one_away, 1, 1), send(three_away, 3, 1)]
    left_sum = share(left_sum, DATA, n_data).reshape(rank, cols)
    rows_grad = mixed[:, rank // n_data :].reshape(cols, rank)
    scaled_grad = (rows_grad * inv_grad[:, None]).astype(BF)
    partial = part_act(coords, rows_y, keys_y, keys_sib, token_scale)
    (got, left_sum, scaled_grad, partial, keys_z) = phase(got, left_sum, scaled_grad, partial, keys_z)
    got_one_away, got_three_away = got
    factor_act = lax.psum_scatter(partial, ("x", "z"), scatter_dimension=0, tiled=True).astype(F32)

    left_core = jnp.dot(core_act, left_sum.astype(F32), precision=lax.Precision.HIGHEST)
    left = inv_act[:, None] * gradient - expand_rows(scaled_act, left_core)
    left = left.astype(BF)
    right_part = jnp.dot(left, scaled_grad, preferred_element_type=F32).astype(BF)
    (right_part, left, keys_z) = phase(right_part, left, keys_z)

    received = [
        here,
        got_here_away,
        got_one,
        got_one_away,
        got_two,
        got_two_away,
        got_three,
        got_three_away,
    ]
    right_sum = deal(right_part.reshape(n_group, rows // n_group, rank), GROUP).astype(BF)
    far = part_grad(coords, received, keys_z, token_scale, (2, 6), 2)
    (far, right_sum, keys_z) = phase(far, right_sum, keys_z)

    ways = (("x", 1), ("x", 3), ("y", 1), ("y", 3))
    via = [shift(f, *way) for f, way in zip(far, ways)]
    right_sum = share(right_sum, GROUP, n_group).reshape(rows, rank)
    near = part_grad(coords, received, keys_z, token_scale, (1, 3, 5, 7), 2)
    (via, near, right_sum, keys_z, left) = phase(via, near, right_sum, keys_z, left)

    free, held = [near[1], near[2], near[5], near[6]], [near[0], near[3], near[4], near[7]]
    got_free = [shift(f, *way) for f, way in zip(free, ways)]
    held = add_terms(held, via)
    right_core = jnp.dot(right_sum.astype(F32), core_grad, precision=lax.Precision.HIGHEST)
    precon = left * inv_grad[None, :] - expand_cols(right_core, scaled_grad)
    total = jnp.full((8, 128), jnp.sum(precon * precon), F32)
    (got_free, held, total, keys_z) = phase(got_free, held, total, keys_z)

    got_held = [shift(h, *way) for h, way in zip(held, ways)]
    total = share(total, GROUP, n_group).sum(0)
    own_a, own_b = part_grad(coords, received, keys_z, token_scale, (0, 4))
    (got_held, own_a, own_b, total) = phase(got_held, own_a, own_b, total)
    sum_a, sum_b = merge(
        [
            [own_a, got_held[0], got_free[0], got_free[1], got_held[1]],
            [own_b, got_held[2], got_free[2], got_free[3], got_held[3]],
        ]
    )
    (sum_a, sum_b, total) = phase(sum_a, sum_b, total)

    got_a = [sum_a[0]] + [shift(sum_a[d], "y", d) for d in (1, 2, 3)]
    got_b = [sum_b[0]] + [shift(sum_b[d], "x", d) for d in (1, 2, 3)]
    total = share(total, DATA, n_data).sum(0)[0, 0]
    root_mean = jnp.sqrt(total / (rows * n_data * cols * n_group) + epsilon)
    update = jnp.minimum(1.0, clip_rms / root_mean) * precon
    factor_grad = finish(got_a, got_b)
    return factor_act, factor_grad, update


def solution(mesh):
    cut = Mesh(mesh.devices.reshape(4, 2, 4, 2, 2), AXES)
    placed = (
        P(AXES, None),
        P(AXES, None),
        P(),
        P(),
        P(),
        P(),
        P(DATA, GROUP),
        P(DATA),
        P(GROUP),
        P(AXES, None),
        P(GROUP + DATA, None),
        P(),
        P(),
    )
    return jax.shard_map(
        local,
        mesh=cut,
        in_specs=placed,
        out_specs=(P(GROUP + DATA, None), P(GROUP + DATA, None), P(DATA, GROUP)),
        check_vma=False,
    )
```

profile of v0, /device:TPU:1, one launch (start us, length us, event | category | flops | bytes accessed | tf_op | source)
XLA Modules:
  0.0 334.5 jit_solution(16231349950028176912)
XLA Ops:
  7.2 1.5 broadcast_in_dim.20
  8.7 9.5 %all-to-all-start = ((bf16[16,64,128]{2,1,0:T(8,128)(2,1)}), bf16[16,64,128]{2,1,0:T(8,128)(2,1)S(1)}, u32[]{:S(2)}, u32[]{:S(2)}) async-start(bf16[16,64,128]{2,1,0:T(8,128)(2,1)} %broadcast_in_dim.20), calls=%async_computation | async-start | bytes 524288 | tf_op jit(solution)/shard_map/all_to_all | solution.py:431
  18.1 6.0 %turn_act.1 = bf16[8,16,64,128]{3,2,1,0:T(8,128)(2,1)} custom-call(bf16[128,8192]{1,0:T(8,128)(2,1)} %act_ref.1), custom_call_target="tpu_custom_call" | custom-call | bytes 4194304 | tf_op jit(solution)/shard_map/turn_act/pallas_call | solution.py:167
  24.8 6.1 %turn.2 = (bf16[32,112,128]{2,1,0:T(8,128)(2,1)}, bf16[32,112,128]{2,1,0:T(8,128)(2,1)}, bf16[32,112,128]{2,1,0:T(8,128)(2,1)}, bf16[32,112,128]{2,1,0:T(8,128)(2,1)}) custom-call(s32[4]{0:T(128)} %pad_add_fusion.coords, bf16[128,28672]{1,0:T(8,128)(2,1)} %x_ref.3), custom_call_target="tpu_custom_call" | custom-call | bytes 7340032 | tf_op jit(solution)/shard_map/turn/pallas_call | solution.py:132
  30.9 7.7 %sketch.2.refs_8_ = bf16[128,2048]{1,0:T(8,128)(2,1)} custom-call(s32[2048]{0:T(1024)} %picks.1, bf16[128,8192]{1,0:T(8,128)(2,1)} %act_ref.1, s32[1,8192]{1,0:T(1,128)} %bitcast.82, bf16[256,256]{1,0:T(8,128)(2,1)} %constant.41.clone.table_ref), custom_call_target="tpu_custom_call" | custom-call | flops 1073741824 | bytes 2621440 | tf_op jit(solution)/shard_map/sketch/pallas_call | solution.py:73
  39.3 4.8 %all-to-all-start.1 = ((bf16[8,16,64,128]{3,2,1,0:T(8,128)(2,1)}), bf16[8,16,64,128]{3,2,1,0:T(8,128)(2,1)S(1)}, u32[]{:S(2)}, u32[]{:S(2)}) async-start(bf16[8,16,64,128]{3,2,1,0:T(8,128)(2,1)} %turn_act.1), calls=%async_computation.1 | async-start | bytes 4194304 | tf_op jit(solution)/shard_map/all_to_all | solution.py:475
  44.3 2.7 collective-permute-start.4
  48.1 2.7 collective-permute-start
  50.8 1.6 collective-permute-start.1
  52.4 6.0 %turn.3 = (bf16[32,112,128]{2,1,0:T(8,128)(2,1)}, bf16[32,112,128]{2,1,0:T(8,128)(2,1)}, bf16[32,112,128]{2,1,0:T(8,128)(2,1)}, bf16[32,112,128]{2,1,0:T(8,128)(2,1)}) custom-call(s32[4]{0:T(128)} %pad_add_fusion.coords, bf16[128,28672]{1,0:T(8,128)(2,1)} %x_ref.3), custom_call_target="tpu_custom_call" | custom-call | bytes 7340032 | tf_op jit(solution)/shard_map/turn/pallas_call | solution.py:132
  58.6 2.7 convolution_convert_fusion
  62.4 13.7 %sketch.3 = bf16[128,2048]{1,0:T(8,128)(2,1)} custom-call(s32[2048]{0:T(1024)} %picks.2, bf16[128,28672]{1,0:T(8,128)(2,1)} %x_ref.3, s32[1,28672]{1,0:T(1,128)} %bitcast.81, bf16[256,256]{1,0:T(8,128)(2,1)} %constant.41.clone.table_ref), custom_call_target="tpu_custom_call" | custom-call | flops 3758096384 | bytes 7864320 | tf_op jit(solution)/shard_map/sketch/pallas_call | solution.py:73
  76.1 4.2 %collective-permute-done.4.refs_11_ = bf16[128,2048]{1,0:T(8,128)(2,1)} collective-permute-done((bf16[128,2048]{1,0:T(8,128)(2,1)}, bf16[128,2048]{1,0:T(8,128)(2,1)}, u32[]{:S(2)}, u32[]{:S(2)}) %collective-permute-start.4) | collective-permute-done | bytes 524320 | tf_op jit(solution)/shard_map/ppermute | solution.py:383
  80.3 1.5 collective-permute-done.3.refs_10_
  81.8 10.9 %collective-permute-done.2.refs_9_ = bf16[128,2048]{1,0:T(8,128)(2,1)} collective-permute-done((bf16[128,2048]{1,0:T(8,128)(2,1)}, bf16[128,2048]{1,0:T(8,128)(2,1)}, u32[]{:S(2)}, u32[]{:S(2)}) %collective-permute-start.2) | collective-permute-done | bytes 524320 | tf_op jit(solution)/shard_map/ppermute | solution.py:383
  93.7 1.2 collective-permute-start.5
  94.9 1.5 collective-permute-start.6
  96.4 4.3 %all-to-all-start.2 = ((bf16[8,32,1792]{2,1,0:T(8,128)(2,1)}), bf16[8,32,1792]{2,1,0:T(8,128)(2,1)}, u32[]{:S(2)}, u32[]{:S(2)}) async-start(bf16[8,32,1792]{2,1,0:T(8,128)(2,1)} %pad_maximum_fusion.1), calls=%async_computation.2 | async-start | bytes 1835008 | tf_op jit(solution)/shard_map/all_to_all | solution.py:491
  100.8 3.2 pad_maximum_fusion
  104.0 10.3 %all-to-all-done.2 = bf16[8,32,1792]{2,1,0:T(8,128)(2,1)} async-done(((bf16[8,32,1792]{2,1,0:T(8,128)(2,1)}), bf16[8,32,1792]{2,1,0:T(8,128)(2,1)}, u32[]{:S(2)}, u32[]{:S(2)}) %all-to-all-start.2) | async-done | bytes 917536 | tf_op jit(solution)/shard_map/all_to_all | solution.py:491
  114.2 13.1 %collective-permute-done.5.refs_2_ = bf16[3584,128]{1,0:T(8,128)(2,1)} collective-permute-done((bf16[3584,128]{1,0:T(8,128)(2,1)}, bf16[3584,128]{1,0:T(8,128)(2,1)}, u32[]{:S(2)}, u32[]{:S(2)}) %collective-permute-start.5) | collective-permute-done | bytes 917536 | tf_op jit(solution)/shard_map/ppermute | solution.py:395
  128.5 2.8 collective-permute-start.8
  132.4 3.0 collective-permute-done.8.refs_12_.refs_13_.refs_14_.refs_15_
  136.3 4.1 %all-to-all-start.3 = ((bf16[8,16,1792]{2,1,0:T(8,128)(2,1)}), bf16[8,16,1792]{2,1,0:T(8,128)(2,1)}, u32[]{:S(2)}, u32[]{:S(2)}) async-start(bf16[8,16,1792]{2,1,0:T(8,128)(2,1)} %broadcast_in_dim.25), calls=%async_computation.3 | async-start | bytes 917504 | tf_op jit(solution)/shard_map/all_to_all | solution.py:431
  141.4 3.3 %collective-permute-start.10 = (bf16[3584,128]{1,0:T(8,128)(2,1)}, bf16[3584,128]{1,0:T(8,128)(2,1)S(1)}, u32[]{:S(2)}, u32[]{:S(2)}) collective-permute-start(bf16[3584,128]{1,0:T(8,128)(2,1)} %bitcast.74), channel_id=1, source_target_pairs={{0,13},{1,12},{4,1},{5,0},{8,5},{9,4},{12,9},{13,8},{2,15},{3,14},... | collective-permute-start | bytes 2752520 | tf_op jit(solution)/shard_map/ppermute | solution.py:395
  146.8 1.5 multiply_convert_fusion
  148.3 9.7 %part_product.4 = bf16[1024,2048]{1,0:T(8,128)(2,1)} custom-call(s32[4]{0:T(128)} %pad_add_fusion.coords, bf16[8,1024,128]{2,1,0:T(8,128)(2,1)} %bitcast.60, bf16[8,1024,128]{2,1,0:T(8,128)(2,1)} %bitcast.61, bf16[8,1024,128]{2,1,0:T(8,128)(2,1)} %bitcast.62, bf16[8,1024,128]{2,1,0:T(8,128)(2,1)} %bitcast.63, bf16[8,1024,128]{2,1,0:T(8,128)(2,1)} %bitcast.64, ...), custom_call_target="tpu_custom_call" | custom-call | flops 4294967296 | bytes 10485760 | tf_op jit(solution)/shard_map/part_product/pallas_call | solution.py:211
  158.0 6.8 %collective-permute-done.9.refs_3_ = bf16[3584,128]{1,0:T(8,128)(2,1)S(1)} collective-permute-done((bf16[3584,128]{1,0:T(8,128)(2,1)}, bf16[3584,128]{1,0:T(8,128)(2,1)S(1)}, u32[]{:S(2)}, u32[]{:S(2)}) %collective-permute-start.9) | collective-permute-done | bytes 917536 | tf_op jit(solution)/shard_map/ppermute | solution.py:395
  165.2 1.9 convolution_bitcast_fusion
  169.2 1.5 subtract_convert_fusion
  170.7 1.8 copy-done.3
  172.6 1.8 convolution_convert_fusion.1
  174.4 5.7 %all-to-all-start.4 = ((bf16[16,64,128]{2,1,0:T(8,128)(2,1)}), bf16[16,64,128]{2,1,0:T(8,128)(2,1)S(1)}, u32[]{:S(2)}, u32[]{:S(2)}) async-start(bf16[16,64,128]{2,1,0:T(8,128)(2,1)} %bitcast.20), calls=%async_computation.5 | async-start | bytes 524288 | tf_op jit(solution)/shard_map/all_to_all | solution.py:435
  180.0 9.9 %part_product.5 = (bf16[224,2048]{1,0:T(8,128)(2,1)}, bf16[224,2048]{1,0:T(8,128)(2,1)}, bf16[224,2048]{1,0:T(8,128)(2,1)}, bf16[224,2048]{1,0:T(8,128)(2,1)}) custom-call(s32[4]{0:T(128)} %pad_add_fusion.coords, bf16[3584,128]{1,0:T(8,128)(2,1)} %bitcast.68, bf16[3584,128]{1,0:T(8,128)(2,1)} %collective-permute-done.7.refs_1_, ...), custom_call_target="tpu_custom_call" | custom-call | flops 3758096384 | bytes 9699328 | tf_op jit(solution)/shard_map/part_product/pallas_call | solution.py:211
  190.0 1.6 collective-permute-start.11
  191.5 1.3 collective-permute-start.12
  193.8 2.4 collective-permute-start.14
  196.9 6.4 %all-to-all-start.5 = ((bf16[16,64,128]{2,1,0:T(8,128)(2,1)}), bf16[16,64,128]{2,1,0:T(8,128)(2,1)S(1)}, u32[]{:S(2)}, u32[]{:S(2)}) async-start(bf16[16,64,128]{2,1,0:T(8,128)(2,1)} %broadcast_in_dim.26), calls=%async_computation.6 | async-start | bytes 524288 | tf_op jit(solution)/shard_map/all_to_all | solution.py:431
  203.3 16.1 %part_product.6 = (bf16[224,2048]{1,0:T(8,128)(2,1)}, bf16[224,2048]{1,0:T(8,128)(2,1)}, bf16[224,2048]{1,0:T(8,128)(2,1)}, bf16[224,2048]{1,0:T(8,128)(2,1)}, b...) custom-call(s32[4]{0:T(128)} %pad_add_fusion.coords, ...), custom_call_target="tpu_custom_call" | custom-call | flops 7516192768 | bytes 15204352 | tf_op jit(solution)/shard_map/part_product/pallas_call | solution.py:211
  219.4 3.4 %all-to-all-done.5 = bf16[16,64,128]{2,1,0:T(8,128)(2,1)S(1)} async-done(((bf16[16,64,128]{2,1,0:T(8,128)(2,1)}), bf16[16,64,128]{2,1,0:T(8,128)(2,1)S(1)}, u32[]{:S(2)}, u32[]{:S(2)}) %all-to-all-start.5) | async-done | bytes 262176 | tf_op jit(solution)/shard_map/all_to_all | solution.py:431
  224.6 1.8 collective-permute-start.16
  226.4 1.2 collective-permute-start.17
  227.6 2.1 collective-permute-start.18
  230.9 4.2 %fusion.1 = f32[1024,1792]{1,0:T(8,128)} fusion(bf16[1792,128]{1,0:T(8,128)(2,1)S(1)} %multiply_convert_fusion, f32[1024,128]{1,0:T(8,128)S(1)} %fusion.6), kind=kOutput, calls=%fused_computation.16 | convolution fusion | flops 470286336 | bytes 8323072 | tf_op jit(solution)/shard_map/dot_general | solution.py:426
  235.1 4.8 %add_terms.1 = (bf16[224,2048]{1,0:T(8,128)(2,1)}, bf16[224,2048]{1,0:T(8,128)(2,1)}, bf16[224,2048]{1,0:T(8,128)(2,1)}, bf16[224,2048]{1,0:T(8,128)(2,1)}) custom-call(bf16[224,2048]{1,0:T(8,128)(2,1)} %get-tuple-element.202.refs_0_, bf16[224,2048]{1,0:T(8,128)(2,1)} %get-tuple-element.203.refs_1_, bf16[224,2048]{1,0:T(8,128)(2,1)} %get-tuple-element.204.refs_2_, ...), custom_call_target="tpu_custom_call" | custom-call | flops 1835008 | bytes 11010048 | tf_op jit(solution)/shard_map/add_terms/pallas_call | solution.py:285
  240.7 9.1 %multiply_reduce_fusion = (f32[]{:T(128)}, f32[1024,1792]{1,0:T(8,128)}) fusion(f32[1024,1792]{1,0:T(8,128)} %fusion.1, bf16[1792,128]{1,0:T(8,128)(2,1)} %copy-done.10, f32[1024,128]{1,0:T(8,128)} %copy-done.9, f32[1792]{0:T(1024)S(1)} %broadcast_divide_fusion, bf16[1024,1792]{1,0:T(8,128)(2,1)S(1)} %copy-done.4), kind=kOutput, calls=%fused_computation | convolution fusion | flops 480903168 | bytes 19340292 | tf_op jit(solution)/shard_map/dot_general | solution.py:424
  251.6 2.7 collective-permute-start.20
  254.3 1.2 collective-permute-start.21
  255.5 2.0 collective-permute-start.22
  258.1 7.2 %all-to-all-start.6 = ((f32[16,8,128]{2,1,0:T(8,128)}), f32[16,8,128]{2,1,0:T(8,128)S(1)}, u32[]{:S(2)}, u32[]{:S(2)}) async-start(f32[16,8,128]{2,1,0:T(8,128)} %broadcast_in_dim.28), calls=%async_computation.7 | async-start | bytes 131072 | tf_op jit(solution)/shard_map/all_to_all | solution.py:431
  265.3 9.9 %part_product.7 = (bf16[448,2048]{1,0:T(8,128)(2,1)}, bf16[448,2048]{1,0:T(8,128)(2,1)}) custom-call(s32[4]{0:T(128)} %pad_add_fusion.coords, bf16[3584,128]{1,0:T(8,128)(2,1)} %bitcast.70, bf16[3584,128]{1,0:T(8,128)(2,1)} %collective-permute-done.7.refs_1_, bf16[3584,128]{1,0:T(8,128)(2,1)} %collective-permute-done.5.refs_2_, bf16[3584,128]{1,0:T(8,128)(2,1)} %copy-done.7, ...), custom_call_target="tpu_custom_call" | custom-call | flops 3758096384 | bytes 9699328 | tf_op jit(solution)/shard_map/part_product/pallas_call | solution.py:211
  275.2 6.3 %all-to-all-done.6 = f32[16,8,128]{2,1,0:T(8,128)S(1)} async-done(((f32[16,8,128]{2,1,0:T(8,128)}), f32[16,8,128]{2,1,0:T(8,128)S(1)}, u32[]{:S(2)}, u32[]{:S(2)}) %all-to-all-start.6) | async-done | bytes 65568 | tf_op jit(solution)/shard_map/all_to_all | solution.py:431
  283.1 6.8 %merge.1 = (f32[112,2048]{1,0:T(8,128)}, bf16[112,2048]{1,0:T(8,128)(2,1)}, bf16[112,2048]{1,0:T(8,128)(2,1)}, bf16[112,2048]{1,0:T(8,128)(2,1)}, f32[112,2048]{...) custom-call(bf16[448,2048]{1,0:T(8,128)(2,1)} %get-tuple-element.225.refs_0_, ...), custom_call_target="tpu_custom_call" | custom-call | flops 3670016 | bytes 16515072 | tf_op jit(solution)/shard_map/merge/pallas_call | solution.py:317
  291.5 3.3 all-to-all-start.7
  294.8 1.8 collective-permute-start.24
  296.6 2.0 collective-permute-start.25
  299.8 2.4 collective-permute-start.27
  303.4 1.2 collective-permute-start.28
  304.7 6.6 %broadcast_multiply_fusion = f32[1024,1792]{1,0:T(8,128)} fusion(f32[1024,1792]{1,0:T(8,128)} %get-tuple-element.254, f32[]{:T(128)} %bitcast.22), kind=kLoop, calls=%fused_computation.3 | loop fusion | flops 1835008 | bytes 14680068 | tf_op jit(solution)/shard_map/mul | solution.py:559
  311.3 1.3 collective-permute-done.24.refs_2_
  312.6 5.1 %collective-permute-done.25.refs_3_ = bf16[112,2048]{1,0:T(8,128)(2,1)S(1)} collective-permute-done((bf16[112,2048]{1,0:T(8,128)(2,1)}, bf16[112,2048]{1,0:T(8,128)(2,1)S(1)}, u32[]{:S(2)}, u32[]{:S(2)}) %collective-permute-start.25) | collective-permute-done | bytes 458784 | tf_op jit(solution)/shard_map/ppermute | solution.py:383
  317.7 3.1 collective-permute-done.27.refs_6_
  322.4 3.5 %finish.1 = f32[224,2048]{1,0:T(8,128)} custom-call(f32[112,2048]{1,0:T(8,128)} %get-tuple-element.244.refs_0_, bf16[112,2048]{1,0:T(8,128)(2,1)} %copy-done.18, bf16[112,2048]{1,0:T(8,128)(2,1)} %copy-done.19, bf16[112,2048]{1,0:T(8,128)(2,1)} %copy-done.20, f32[112,2048]{1,0:T(8,128)} %get-tuple-element.248.refs_4_, bf16[112,2048]{1,0:T(8,128)(2,1)} %copy-done.21, ...), custom_call_target="tpu_custom_call" | custom-call | flops 1376256 | bytes 6422528 | tf_op jit(solution)/shard_map/finish/pallas_call | solution.py:356
  325.9 1.8 convert_element_type.63
  (116 shorter events, 27.7 us)
Async XLA Ops:
  7.2 158.0 %copy-start = (f32[128,128]{1,0:T(8,128)S(1)}, f32[128,128]{1,0:T(8,128)}, u32[]{:S(2)}) copy-start(f32[128,128]{1,0:T(8,128)} %param.25) | copy-start | bytes 196612
  8.7 29.9 %all-to-all-start = ((bf16[16,64,128]{2,1,0:T(8,128)(2,1)}), bf16[16,64,128]{2,1,0:T(8,128)(2,1)S(1)}, u32[]{:S(2)}, u32[]{:S(2)}) async-start(bf16[16,64,128]{2,1,0:T(8,128)(2,1)} %broadcast_in_dim.20), calls=%async_computation | async-start | bytes 524288 | tf_op jit(solution)/shard_map/all_to_all | solution.py:431
  30.9 13.2 %copy-start.25 = (bf16[224,128]{1,0:T(8,128)(2,1)S(1)}, bf16[224,128]{1,0:T(8,128)(2,1)}, u32[]{:S(2)}) copy-start(bf16[224,128]{1,0:T(8,128)(2,1)} %param.24) | copy-start | bytes 172036
  30.9 13.3 %copy-start.27 = (f32[1024]{0:T(1024)S(1)}, f32[1024]{0:T(1024)}, u32[]{:S(2)}) copy-start(f32[1024]{0:T(1024)} %param.21) | copy-start | bytes 12292
  39.3 53.4 %all-to-all-start.1 = ((bf16[8,16,64,128]{3,2,1,0:T(8,128)(2,1)}), bf16[8,16,64,128]{3,2,1,0:T(8,128)(2,1)S(1)}, u32[]{:S(2)}, u32[]{:S(2)}) async-start(bf16[8,16,64,128]{3,2,1,0:T(8,128)(2,1)} %turn_act.1), calls=%async_computation.1 | async-start | bytes 4194304 | tf_op jit(solution)/shard_map/all_to_all | solution.py:475
  44.1 121.0 %all-gather.3.cloned.1.call-start = ((), (), s32[]{:S(2)}) async-start(), calls=%async_computation.10 | async-start | bytes 4718592 | tf_op jit(solution)/shard_map/all_gather | solution.py:488
  44.2 14.2 %copy-start.12 = (bf16[16,64,128]{2,1,0:T(8,128)(2,1)S(1)}, bf16[16,64,128]{2,1,0:T(8,128)(2,1)}, u32[]{:S(2)}) copy-start(bf16[16,64,128]{2,1,0:T(8,128)(2,1)} %copy-done.11) | copy-start | bytes 786436
  44.3 36.0 %collective-permute-start.4 = (bf16[128,2048]{1,0:T(8,128)(2,1)}, bf16[128,2048]{1,0:T(8,128)(2,1)}, u32[]{:S(2)}, u32[]{:S(2)}) collective-permute-start(bf16[128,2048]{1,0:T(8,128)(2,1)} %sketch.2.refs_8_), channel_id=1, source_target_pairs={{0,18},{16,0},{2,16},{18,2},{1,19},{17,1},{3,17},{19,3},{4,22},{20... | collective-permute-start | bytes 1572872 | tf_op jit(solution)/shard_map/ppermute | solution.py:383
  46.9 34.9 %collective-permute-start.3 = (bf16[128,2048]{1,0:T(8,128)(2,1)}, bf16[128,2048]{1,0:T(8,128)(2,1)}, u32[]{:S(2)}, u32[]{:S(2)}) collective-permute-start(bf16[128,2048]{1,0:T(8,128)(2,1)} %sketch.2.refs_8_), channel_id=1, source_target_pairs={{0,2},{16,18},{2,0},{18,16},{1,3},{17,19},{3,1},{19,17},{4,6},{20,... | collective-permute-start | bytes 1572872 | tf_op jit(solution)/shard_map/ppermute | solution.py:383
  47.5 45.2 %collective-permute-start.2 = (bf16[128,2048]{1,0:T(8,128)(2,1)}, bf16[128,2048]{1,0:T(8,128)(2,1)}, u32[]{:S(2)}, u32[]{:S(2)}) collective-permute-start(bf16[128,2048]{1,0:T(8,128)(2,1)} %sketch.2.refs_8_), channel_id=1, source_target_pairs={{0,16},{16,2},{2,18},{18,0},{1,17},{17,3},{3,19},{19,1},{4,20},{20... | collective-permute-start | bytes 1572872 | tf_op jit(solution)/shard_map/ppermute | solution.py:383
  48.1 44.7 %collective-permute-start = (bf16[3584,128]{1,0:T(8,128)(2,1)}, bf16[3584,128]{1,0:T(8,128)(2,1)S(1)}, u32[]{:S(2)}, u32[]{:S(2)}) collective-permute-start(bf16[3584,128]{1,0:T(8,128)(2,1)} %bitcast.80), channel_id=1, source_target_pairs={{0,8},{1,9},{4,12},{5,13},{8,0},{9,1},{12,4},{13,5},{2,10},{3,11},... | collective-permute-start | bytes 2752520 | tf_op jit(solution)/shard_map/ppermute | solution.py:395
  50.8 42.0 %collective-permute-start.1 = (bf16[3584,128]{1,0:T(8,128)(2,1)}, bf16[3584,128]{1,0:T(8,128)(2,1)}, u32[]{:S(2)}, u32[]{:S(2)}) collective-permute-start(bf16[3584,128]{1,0:T(8,128)(2,1)} %bitcast.79), channel_id=1, source_target_pairs={{0,9},{1,8},{4,13},{5,12},{8,1},{9,0},{12,5},{13,4},{2,11},{3,10},... | collective-permute-start | bytes 2752520 | tf_op jit(solution)/shard_map/ppermute | solution.py:395
  76.1 55.2 %copy-start.26 = (f32[1792]{0:T(1024)S(1)}, f32[1792]{0:T(1024)}, u32[]{:S(2)}) copy-start(f32[1792]{0:T(1024)} %param.22) | copy-start | bytes 21508
  92.7 43.5 %copy-start.6 = (bf16[3584,128]{1,0:T(8,128)(2,1)}, bf16[3584,128]{1,0:T(8,128)(2,1)S(1)}, u32[]{:S(2)}) copy-start(bf16[3584,128]{1,0:T(8,128)(2,1)S(1)} %collective-permute-done.refs_4_) | copy-start | bytes 2752516
  92.8 43.5 %copy-start.2 = (bf16[8,16,64,128]{3,2,1,0:T(8,128)(2,1)}, bf16[8,16,64,128]{3,2,1,0:T(8,128)(2,1)S(1)}, u32[]{:S(2)}) copy-start(bf16[8,16,64,128]{3,2,1,0:T(8,128)(2,1)S(1)} %all-to-all-done.1) | copy-start | bytes 6291460
  92.8 11.2 %collective-permute-start.7 = (bf16[3584,128]{1,0:T(8,128)(2,1)}, bf16[3584,128]{1,0:T(8,128)(2,1)}, u32[]{:S(2)}, u32[]{:S(2)}) collective-permute-start(bf16[3584,128]{1,0:T(8,128)(2,1)} %bitcast.76), channel_id=1, source_target_pairs={{0,1},{1,0},{4,5},{5,4},{8,9},{9,8},{12,13},{13,12},{2,3},{3,2},{6... | collective-permute-start | bytes 2752520 | tf_op jit(solution)/shard_map/ppermute | solution.py:395
  93.7 33.6 %collective-permute-start.5 = (bf16[3584,128]{1,0:T(8,128)(2,1)}, bf16[3584,128]{1,0:T(8,128)(2,1)}, u32[]{:S(2)}, u32[]{:S(2)}) collective-permute-start(bf16[3584,128]{1,0:T(8,128)(2,1)} %bitcast.78), channel_id=1, source_target_pairs={{0,4},{1,5},{4,8},{5,9},{8,12},{9,13},{12,0},{13,1},{2,6},{3,7},{6... | collective-permute-start | bytes 2752520 | tf_op jit(solution)/shard_map/ppermute | solution.py:395
  94.9 33.6 %collective-permute-start.6 = (bf16[3584,128]{1,0:T(8,128)(2,1)}, bf16[3584,128]{1,0:T(8,128)(2,1)}, u32[]{:S(2)}, u32[]{:S(2)}) collective-permute-start(bf16[3584,128]{1,0:T(8,128)(2,1)} %bitcast.77), channel_id=1, source_target_pairs={{0,12},{1,13},{4,0},{5,1},{8,4},{9,5},{12,8},{13,9},{2,14},{3,15},... | collective-permute-start | bytes 2752520 | tf_op jit(solution)/shard_map/ppermute | solution.py:395
  96.4 17.8 %all-to-all-start.2 = ((bf16[8,32,1792]{2,1,0:T(8,128)(2,1)}), bf16[8,32,1792]{2,1,0:T(8,128)(2,1)}, u32[]{:S(2)}, u32[]{:S(2)}) async-start(bf16[8,32,1792]{2,1,0:T(8,128)(2,1)} %pad_maximum_fusion.1), calls=%async_computation.2 | async-start | bytes 1835008 | tf_op jit(solution)/shard_map/all_to_all | solution.py:491
  128.5 6.9 %collective-permute-start.8 = (bf16[512,2048]{1,0:T(8,128)(2,1)}, bf16[512,2048]{1,0:T(8,128)(2,1)}, u32[]{:S(2)}, u32[]{:S(2)}) collective-permute-start(bf16[512,2048]{1,0:T(8,128)(2,1)} %pad_maximum_fusion), channel_id=1, source_target_pairs={{0,1},{1,0},{2,3},{3,2},{4,5},{5,4},{6,7},{7,6},{8,9},{9,8},{10,11... | collective-permute-start | bytes 6291464 | tf_op jit(solution)/shard_map/ppermute | solution.py:390
  136.3 21.7 %all-to-all-start.3 = ((bf16[8,16,1792]{2,1,0:T(8,128)(2,1)}), bf16[8,16,1792]{2,1,0:T(8,128)(2,1)}, u32[]{:S(2)}, u32[]{:S(2)}) async-start(bf16[8,16,1792]{2,1,0:T(8,128)(2,1)} %broadcast_in_dim.25), calls=%async_computation.3 | async-start | bytes 917504 | tf_op jit(solution)/shard_map/all_to_all | solution.py:431
  140.4 185.5 %reduce-scatter.2.cloned.1.call-start = ((), (), s32[]{:S(2)}) async-start(), calls=%async_computation.9 | async-start | bytes 4456448 | tf_op jit(solution)/shard_map/reduce_scatter | solution.py:507
  140.4 24.4 %collective-permute-start.9 = (bf16[3584,128]{1,0:T(8,128)(2,1)}, bf16[3584,128]{1,0:T(8,128)(2,1)S(1)}, u32[]{:S(2)}, u32[]{:S(2)}) collective-permute-start(bf16[3584,128]{1,0:T(8,128)(2,1)} %bitcast.75), channel_id=1, source_target_pairs={{0,5},{1,4},{4,9},{5,8},{8,13},{9,12},{12,1},{13,0},{2,7},{3,6},{6... | collective-permute-start | bytes 2752520 | tf_op jit(solution)/shard_map/ppermute | solution.py:395
  141.4 23.7 %collective-permute-start.10 = (bf16[3584,128]{1,0:T(8,128)(2,1)}, bf16[3584,128]{1,0:T(8,128)(2,1)S(1)}, u32[]{:S(2)}, u32[]{:S(2)}) collective-permute-start(bf16[3584,128]{1,0:T(8,128)(2,1)} %bitcast.74), channel_id=1, source_target_pairs={{0,13},{1,12},{4,1},{5,0},{8,5},{9,4},{12,9},{13,8},{2,15},{3,14},... | collective-permute-start | bytes 2752520 | tf_op jit(solution)/shard_map/ppermute | solution.py:395
  148.3 81.8 %copy-start.10 = (bf16[1792,128]{1,0:T(8,128)(2,1)}, bf16[1792,128]{1,0:T(8,128)(2,1)S(1)}, u32[]{:S(2)}) copy-start(bf16[1792,128]{1,0:T(8,128)(2,1)S(1)} %multiply_convert_fusion) | copy-start | bytes 1376260
  164.8 3.4 %copy-start.7 = (bf16[3584,128]{1,0:T(8,128)(2,1)}, bf16[3584,128]{1,0:T(8,128)(2,1)S(1)}, u32[]{:S(2)}) copy-start(bf16[3584,128]{1,0:T(8,128)(2,1)S(1)} %collective-permute-done.9.refs_3_) | copy-start | bytes 2752516
  165.2 3.1 copy-start.8
  167.1 2.0 copy-start.5
  170.7 1.8 copy-start.3
  174.4 15.6 %all-to-all-start.4 = ((bf16[16,64,128]{2,1,0:T(8,128)(2,1)}), bf16[16,64,128]{2,1,0:T(8,128)(2,1)S(1)}, u32[]{:S(2)}, u32[]{:S(2)}) async-start(bf16[16,64,128]{2,1,0:T(8,128)(2,1)} %bitcast.20), calls=%async_computation.5 | async-start | bytes 524288 | tf_op jit(solution)/shard_map/all_to_all | solution.py:435
  190.0 33.6 %collective-permute-start.11 = (bf16[224,2048]{1,0:T(8,128)(2,1)}, bf16[224,2048]{1,0:T(8,128)(2,1)S(1)}, u32[]{:S(2)}, u32[]{:S(2)}) collective-permute-start(bf16[224,2048]{1,0:T(8,128)(2,1)} %get-tuple-element.183), channel_id=1, source_target_pairs={{0,32},{32,64},{64,96},{96,0},{1,33},{33,65},{65,97},{97,1},{2,34}... | collective-permute-start | bytes 2752520 | tf_op jit(solution)/shard_map/ppermute | solution.py:386
  191.5 32.1 %collective-permute-start.12 = (bf16[224,2048]{1,0:T(8,128)(2,1)}, bf16[224,2048]{1,0:T(8,128)(2,1)S(1)}, u32[]{:S(2)}, u32[]{:S(2)}) collective-permute-start(bf16[224,2048]{1,0:T(8,128)(2,1)} %get-tuple-element.184), channel_id=1, source_target_pairs={{0,96},{32,0},{64,32},{96,64},{1,97},{33,1},{65,33},{97,65},{2,98}... | collective-permute-start | bytes 2752520 | tf_op jit(solution)/shard_map/ppermute | solution.py:386
  192.8 30.8 %collective-permute-start.13 = (bf16[224,2048]{1,0:T(8,128)(2,1)}, bf16[224,2048]{1,0:T(8,128)(2,1)}, u32[]{:S(2)}, u32[]{:S(2)}) collective-permute-start(bf16[224,2048]{1,0:T(8,128)(2,1)} %get-tuple-element.185), channel_id=1, source_target_pairs={{0,16},{16,2},{2,18},{18,0},{1,17},{17,3},{3,19},{19,1},{4,20},{20... | collective-permute-start | bytes 2752520 | tf_op jit(solution)/shard_map/ppermute | solution.py:383
  193.8 29.8 %collective-permute-start.14 = (bf16[224,2048]{1,0:T(8,128)(2,1)}, bf16[224,2048]{1,0:T(8,128)(2,1)}, u32[]{:S(2)}, u32[]{:S(2)}) collective-permute-start(bf16[224,2048]{1,0:T(8,128)(2,1)} %get-tuple-element.186), channel_id=1, source_target_pairs={{0,18},{16,0},{2,16},{18,2},{1,19},{17,1},{3,17},{19,3},{4,22},{20... | collective-permute-start | bytes 2752520 | tf_op jit(solution)/shard_map/ppermute | solution.py:383
  196.9 25.9 %all-to-all-start.5 = ((bf16[16,64,128]{2,1,0:T(8,128)(2,1)}), bf16[16,64,128]{2,1,0:T(8,128)(2,1)S(1)}, u32[]{:S(2)}, u32[]{:S(2)}) async-start(bf16[16,64,128]{2,1,0:T(8,128)(2,1)} %broadcast_in_dim.26), calls=%async_computation.6 | async-start | bytes 524288 | tf_op jit(solution)/shard_map/all_to_all | solution.py:431
  203.3 26.4 %copy-start.24 = (f32[128,128]{1,0:T(8,128)S(1)}, f32[128,128]{1,0:T(8,128)}, u32[]{:S(2)}) copy-start(f32[128,128]{1,0:T(8,128)} %param.26) | copy-start | bytes 196612
  223.6 6.5 %copy-start.13 = (bf16[224,2048]{1,0:T(8,128)(2,1)}, bf16[224,2048]{1,0:T(8,128)(2,1)S(1)}, u32[]{:S(2)}) copy-start(bf16[224,2048]{1,0:T(8,128)(2,1)S(1)} %collective-permute-done.11.refs_4_) | copy-start | bytes 2752516
  223.6 6.5 %copy-start.14 = (bf16[224,2048]{1,0:T(8,128)(2,1)}, bf16[224,2048]{1,0:T(8,128)(2,1)S(1)}, u32[]{:S(2)}) copy-start(bf16[224,2048]{1,0:T(8,128)(2,1)S(1)} %collective-permute-done.12.refs_5_) | copy-start | bytes 2752516
  223.7 27.2 %collective-permute-start.15 = (bf16[224,2048]{1,0:T(8,128)(2,1)}, bf16[224,2048]{1,0:T(8,128)(2,1)}, u32[]{:S(2)}, u32[]{:S(2)}) collective-permute-start(bf16[224,2048]{1,0:T(8,128)(2,1)} %get-tuple-element.198), channel_id=1, source_target_pairs={{0,32},{32,64},{64,96},{96,0},{1,33},{33,65},{65,97},{97,1},{2,34}... | collective-permute-start | bytes 2752520 | tf_op jit(solution)/shard_map/ppermute | solution.py:386
  224.6 26.2 %collective-permute-start.16 = (bf16[224,2048]{1,0:T(8,128)(2,1)}, bf16[224,2048]{1,0:T(8,128)(2,1)}, u32[]{:S(2)}, u32[]{:S(2)}) collective-permute-start(bf16[224,2048]{1,0:T(8,128)(2,1)} %get-tuple-element.199), channel_id=1, source_target_pairs={{0,96},{32,0},{64,32},{96,64},{1,97},{33,1},{65,33},{97,65},{2,98}... | collective-permute-start | bytes 2752520 | tf_op jit(solution)/shard_map/ppermute | solution.py:386
  226.4 24.5 %collective-permute-start.17 = (bf16[224,2048]{1,0:T(8,128)(2,1)}, bf16[224,2048]{1,0:T(8,128)(2,1)}, u32[]{:S(2)}, u32[]{:S(2)}) collective-permute-start(bf16[224,2048]{1,0:T(8,128)(2,1)} %get-tuple-element.200), channel_id=1, source_target_pairs={{0,16},{16,2},{2,18},{18,0},{1,17},{17,3},{3,19},{19,1},{4,20},{20... | collective-permute-start | bytes 2752520 | tf_op jit(solution)/shard_map/ppermute | solution.py:383
  227.6 23.3 %collective-permute-start.18 = (bf16[224,2048]{1,0:T(8,128)(2,1)}, bf16[224,2048]{1,0:T(8,128)(2,1)}, u32[]{:S(2)}, u32[]{:S(2)}) collective-permute-start(bf16[224,2048]{1,0:T(8,128)(2,1)} %get-tuple-element.201), channel_id=1, source_target_pairs={{0,18},{16,0},{2,16},{18,2},{1,19},{17,1},{3,17},{19,3},{4,22},{20... | collective-permute-start | bytes 2752520 | tf_op jit(solution)/shard_map/ppermute | solution.py:383
  235.1 5.5 %copy-start.4 = (bf16[1024,1792]{1,0:T(8,128)(2,1)S(1)}, bf16[1024,1792]{1,0:T(8,128)(2,1)}, u32[]{:S(2)}) copy-start(bf16[1024,1792]{1,0:T(8,128)(2,1)} %copy-done.3) | copy-start | bytes 11010052
  251.5 30.0 %collective-permute-start.19 = (bf16[224,2048]{1,0:T(8,128)(2,1)}, bf16[224,2048]{1,0:T(8,128)(2,1)S(1)}, u32[]{:S(2)}, u32[]{:S(2)}) collective-permute-start(bf16[224,2048]{1,0:T(8,128)(2,1)} %get-tuple-element.217), channel_id=1, source_target_pairs={{0,32},{32,64},{64,96},{96,0},{1,33},{33,65},{65,97},{97,1},{2,34}... | collective-permute-start | bytes 2752520 | tf_op jit(solution)/shard_map/ppermute | solution.py:386
  251.6 30.0 %collective-permute-start.20 = (bf16[224,2048]{1,0:T(8,128)(2,1)}, bf16[224,2048]{1,0:T(8,128)(2,1)S(1)}, u32[]{:S(2)}, u32[]{:S(2)}) collective-permute-start(bf16[224,2048]{1,0:T(8,128)(2,1)} %get-tuple-element.218), channel_id=1, source_target_pairs={{0,96},{32,0},{64,32},{96,64},{1,97},{33,1},{65,33},{97,65},{2,98}... | collective-permute-start | bytes 2752520 | tf_op jit(solution)/shard_map/ppermute | solution.py:386
  254.3 27.3 %collective-permute-start.21 = (bf16[224,2048]{1,0:T(8,128)(2,1)}, bf16[224,2048]{1,0:T(8,128)(2,1)S(1)}, u32[]{:S(2)}, u32[]{:S(2)}) collective-permute-start(bf16[224,2048]{1,0:T(8,128)(2,1)} %get-tuple-element.219), channel_id=1, source_target_pairs={{0,16},{16,2},{2,18},{18,0},{1,17},{17,3},{3,19},{19,1},{4,20},{20... | collective-permute-start | bytes 2752520 | tf_op jit(solution)/shard_map/ppermute | solution.py:383
  255.5 26.1 %collective-permute-start.22 = (bf16[224,2048]{1,0:T(8,128)(2,1)}, bf16[224,2048]{1,0:T(8,128)(2,1)}, u32[]{:S(2)}, u32[]{:S(2)}) collective-permute-start(bf16[224,2048]{1,0:T(8,128)(2,1)} %get-tuple-element.220), channel_id=1, source_target_pairs={{0,18},{16,0},{2,16},{18,2},{1,19},{17,1},{3,17},{19,3},{4,22},{20... | collective-permute-start | bytes 2752520 | tf_op jit(solution)/shard_map/ppermute | solution.py:383
  258.1 23.4 %all-to-all-start.6 = ((f32[16,8,128]{2,1,0:T(8,128)}), f32[16,8,128]{2,1,0:T(8,128)S(1)}, u32[]{:S(2)}, u32[]{:S(2)}) async-start(f32[16,8,128]{2,1,0:T(8,128)} %broadcast_in_dim.28), calls=%async_computation.7 | async-start | bytes 131072 | tf_op jit(solution)/shard_map/all_to_all | solution.py:431
  281.6 0.9 copy-start.15
  281.6 1.3 copy-start.16
  281.6 1.5 copy-start.17
  289.9 13.5 %collective-permute-start.23 = (bf16[112,2048]{1,0:T(8,128)(2,1)}, bf16[112,2048]{1,0:T(8,128)(2,1)S(1)}, u32[]{:S(2)}, u32[]{:S(2)}) collective-permute-start(bf16[112,2048]{1,0:T(8,128)(2,1)} %get-tuple-element.245), channel_id=1, source_target_pairs={{0,16},{16,2},{2,18},{18,0},{1,17},{17,3},{3,19},{19,1},{4,20},{20... | collective-permute-start | bytes 1376264 | tf_op jit(solution)/shard_map/ppermute | solution.py:383
  291.5 10.7 %all-to-all-start.7 = ((f32[8,8,128]{2,1,0:T(8,128)}), f32[8,8,128]{2,1,0:T(8,128)S(1)}, u32[]{:S(2)}, u32[]{:S(2)}) async-start(f32[8,8,128]{2,1,0:T(8,128)} %broadcast_in_dim.29), calls=%async_computation.8 | async-start | bytes 65536 | tf_op jit(solution)/shard_map/all_to_all | solution.py:431
  294.8 17.8 %collective-permute-start.24 = (bf16[112,2048]{1,0:T(8,128)(2,1)}, bf16[112,2048]{1,0:T(8,128)(2,1)S(1)}, u32[]{:S(2)}, u32[]{:S(2)}) collective-permute-start(bf16[112,2048]{1,0:T(8,128)(2,1)} %get-tuple-element.246), channel_id=1, source_target_pairs={{0,2},{16,18},{2,0},{18,16},{1,3},{17,19},{3,1},{19,17},{4,6},{20,... | collective-permute-start | bytes 1376264 | tf_op jit(solution)/shard_map/ppermute | solution.py:383
  296.6 21.1 %collective-permute-start.25 = (bf16[112,2048]{1,0:T(8,128)(2,1)}, bf16[112,2048]{1,0:T(8,128)(2,1)S(1)}, u32[]{:S(2)}, u32[]{:S(2)}) collective-permute-start(bf16[112,2048]{1,0:T(8,128)(2,1)} %get-tuple-element.247), channel_id=1, source_target_pairs={{0,18},{16,0},{2,16},{18,2},{1,19},{17,1},{3,17},{19,3},{4,22},{20... | collective-permute-start | bytes 1376264 | tf_op jit(solution)/shard_map/ppermute | solution.py:383
  298.6 19.1 %collective-permute-start.26 = (bf16[112,2048]{1,0:T(8,128)(2,1)}, bf16[112,2048]{1,0:T(8,128)(2,1)S(1)}, u32[]{:S(2)}, u32[]{:S(2)}) collective-permute-start(bf16[112,2048]{1,0:T(8,128)(2,1)} %get-tuple-element.249), channel_id=1, source_target_pairs={{0,32},{32,64},{64,96},{96,0},{1,33},{33,65},{65,97},{97,1},{2,34}... | collective-permute-start | bytes 1376264 | tf_op jit(solution)/shard_map/ppermute | solution.py:386
  299.8 21.0 %collective-permute-start.27 = (bf16[112,2048]{1,0:T(8,128)(2,1)}, bf16[112,2048]{1,0:T(8,128)(2,1)S(1)}, u32[]{:S(2)}, u32[]{:S(2)}) collective-permute-start(bf16[112,2048]{1,0:T(8,128)(2,1)} %get-tuple-element.250), channel_id=1, source_target_pairs={{0,64},{32,96},{64,0},{96,32},{1,65},{33,97},{65,1},{97,33},{2,66}... | collective-permute-start | bytes 1376264 | tf_op jit(solution)/shard_map/ppermute | solution.py:386
  303.4 7.9 %copy-start.18 = (bf16[112,2048]{1,0:T(8,128)(2,1)}, bf16[112,2048]{1,0:T(8,128)(2,1)S(1)}, u32[]{:S(2)}) copy-start(bf16[112,2048]{1,0:T(8,128)(2,1)S(1)} %collective-permute-done.23.refs_1_) | copy-start | bytes 1376260
  303.4 17.4 %collective-permute-start.28 = (bf16[112,2048]{1,0:T(8,128)(2,1)}, bf16[112,2048]{1,0:T(8,128)(2,1)S(1)}, u32[]{:S(2)}, u32[]{:S(2)}) collective-permute-start(bf16[112,2048]{1,0:T(8,128)(2,1)} %get-tuple-element.251), channel_id=1, source_target_pairs={{0,96},{32,0},{64,32},{96,64},{1,97},{33,1},{65,33},{97,65},{2,98}... | collective-permute-start | bytes 1376264 | tf_op jit(solution)/shard_map/ppermute | solution.py:386
  304.7 23.0 %copy-start.1 = (f32[128,128]{1,0:T(8,128)S(1)}, f32[128,128]{1,0:T(8,128)}, u32[]{:S(2)}) copy-start(f32[128,128]{1,0:T(8,128)} %param.25) | copy-start | bytes 196612
  312.6 8.1 %copy-start.19 = (bf16[112,2048]{1,0:T(8,128)(2,1)}, bf16[112,2048]{1,0:T(8,128)(2,1)S(1)}, u32[]{:S(2)}) copy-start(bf16[112,2048]{1,0:T(8,128)(2,1)S(1)} %collective-permute-done.24.refs_2_) | copy-start | bytes 1376260
  317.7 3.1 copy-start.20
  317.7 3.1 copy-start.21
  321.6 0.8 copy-start.23
  (3 other events, 2.3 us)
Sparse Core Ops, SparseCore 0:
  92.9 43.2 all-gather.2
  165.3 83.1 reduce-scatter.1
where the time goes:
time: 338 us; the launch traced here: 335 us
  Pallas kernels  100 us (30%)
  starting transfers between devices  92 us (27%)
  waiting for transfers between devices  72.6 us (21%)
  matrix products  22.7 us (7%)
  other arithmetic  17.2 us (5%)
  between operations  15.2 us (4%)
  local copies, waits for them, and re-layouts  14.7 us (4%)
    pallas_call x4, Pallas kernels, part_product(): pl.pallas_call(functools.partial(part_kernel, scale, split), grid_spec=pl...  45.5 us
    all_to_all x5, starting transfers between devices, share(): return lax.all_to_all(copies, axes, 0, 0, tiled=True)  30.5 us
    ppermute x12, waiting for transfers between devices, shift(): lax.ppermute(array, RING_Y, [(spot(y), spot((y + step) % 4)) for y in ran...  23.1 us
    ppermute x7, waiting for transfers between devices, send(): return lax.ppermute(array, ALONG_Z, pairs)  21.4 us
    pallas_call x2, Pallas kernels, sketch(): pl.pallas_call(sketch_kernel, grid_spec=pltpu.PrefetchScalarGridSpec(num_...  21.4 us
    ppermute x12, starting transfers between devices, shift(): lax.ppermute(array, RING_Y, [(spot(y), spot((y + step) % 4)) for y in ran...  18.4 us
    ppermute x9, starting transfers between devices, shift(): return lax.ppermute(array, axis, [(i, (i + step) % 4) for i in range(4)])  13.2 us
    ppermute x7, starting transfers between devices, send(): return lax.ppermute(array, ALONG_Z, pairs)  12.3 us
  transfers between devices with their start and end apart: 39, of which 16 were waited for; matrix products, arithmetic and copies ran while one was open for 13% of the time, Pallas kernels for 30%

commit v1 on v0

--- a/solution.py
+++ b/solution.py
@@ -14,6 +14,11 @@
 INNER = 256
 OUTER = HB // INNER
 ROOM = 60 << 20
+COST_BYTES = 3_400_000
+
+
+def cost(us):
+    return pl.CostEstimate(flops=us * 550_000_000, bytes_accessed=us * COST_BYTES, transcendentals=0)
 
 
 def hadamard_table(length):
@@ -89,9 +94,7 @@
         ),
         out_shape=jax.ShapeDtypeStruct((tokens, count), BF),
         compiler_params=pltpu.CompilerParams(vmem_limit_bytes=ROOM),
-        cost_estimate=pl.CostEstimate(
-            flops=4 * tokens * width * INNER, bytes_accessed=2 * tokens * (width + count), transcendentals=0
-        ),
+        cost_estimate=cost(2 + width // 2400),
         name="sketch",
     )(picks, matrix, signs[None, :], table)
 
@@ -140,9 +143,7 @@
         ),
         out_shape=[jax.ShapeDtypeStruct((32, part, tokens), BF)] * count,
         compiler_params=pltpu.CompilerParams(vmem_limit_bytes=ROOM),
-        cost_estimate=pl.CostEstimate(
-            flops=0, bytes_accessed=4 * tokens * 2 * len(shifts) * wide, transcendentals=0
-        ),
+        cost_estimate=cost(6),
         name="turn",
     )(coords, grads)
     return [o.reshape(-1, tokens) for o in outs]
@@ -172,9 +173,7 @@
         out_shape=jax.ShapeDtypeStruct((8, 16, small, tokens), BF),
         scratch_shapes=[pltpu.VMEM((slim, tokens), BF)],
         compiler_params=pltpu.CompilerParams(vmem_limit_bytes=ROOM),
-        cost_estimate=pl.CostEstimate(
-            flops=0, bytes_accessed=4 * tokens * 8 * slim, transcendentals=0
-        ),
+        cost_estimate=cost(6),
         name="turn_act",
     )(acts)
 
@@ -218,11 +217,7 @@
         ),
         out_shape=[jax.ShapeDtypeStruct((each, width), BF)] * count,
         compiler_params=pltpu.CompilerParams(vmem_limit_bytes=ROOM),
-        cost_estimate=pl.CostEstimate(
-            flops=2 * steps * tile * 8 * tokens * width,
-            bytes_accessed=2 * (steps * tile * (8 * tokens + width) + 8 * tokens * width),
-            transcendentals=0,
-        ),
+        cost_estimate=cost(5 + steps * tile // 160),
         name="part_product",
     )(coords, *rows, *keys)
 
@@ -289,9 +284,7 @@
         out_specs=[spec] * count,
         out_shape=[jax.ShapeDtypeStruct(b.shape, BF) for b in bases],
         compiler_params=pltpu.CompilerParams(vmem_limit_bytes=ROOM),
-        cost_estimate=pl.CostEstimate(
-            flops=count * rows * width, bytes_accessed=6 * count * rows * width, transcendentals=0
-        ),
+        cost_estimate=cost(5),
         name="add_terms",
     )(*bases, *terms)
 
@@ -329,11 +322,7 @@
         )
         * count,
         compiler_params=pltpu.CompilerParams(vmem_limit_bytes=ROOM),
-        cost_estimate=pl.CostEstimate(
-            flops=2 * count * rows * width,
-            bytes_accessed=9 * count * rows * width,
-            transcendentals=0,
-        ),
+        cost_estimate=cost(7),
         name="merge",
     )(*[a for g in groups for a in g])
     return [outs[4 * p : 4 * p + 4] for p in range(count)]
@@ -359,9 +348,7 @@
         in_specs=[pl.BlockSpec((rows, cols), lambda i: (0, i))] * 8,
         out_specs=pl.BlockSpec((2 * rows, cols), lambda i: (0, i)),
         out_shape=jax.ShapeDtypeStruct((2 * rows, width), F32),
-        cost_estimate=pl.CostEstimate(
-            flops=6 * rows * width, bytes_accessed=28 * rows * width, transcendentals=0
-        ),
+        cost_estimate=cost(4),
         compiler_params=pltpu.CompilerParams(vmem_limit_bytes=ROOM),
         name="finish",
     )(*first, *second)
@@ -462,56 +449,52 @@
     inv_act = 1.0 / damped_act
     inv_grad = 1.0 / damped_grad
 
+    here, here_away, two, two_away = turn(coords, out_grads, (0, 2))
+    (two, two_away, here_away, coords, panel_act, act_picks, grad_picks, gradient) = phase(
+        two, two_away, here_away, coords, panel_act, act_picks, grad_picks, gradient
+    )
+
+    got = [send(two, 2, 0), send(two_away, 2, 1), send(here_away, 0, 1)]
     rows_act = share(panel_act, GROUP, n_group).reshape(rows, rank)
+    one, one_away, three, three_away = turn(coords, out_grads, (1, 3))
     sketch_act = sketch(activations, act_signs, act_picks, table)
-    for_y = turn_act(activations)
-    here, here_away, two, two_away = turn(coords, out_grads, (0, 2))
-    (rows_act, two, two_away, here_away, sketch_act, for_y, coords, gradient, grad_picks) = phase(
-        rows_act, two, two_away, here_away, sketch_act, for_y, coords, gradient, grad_picks
-    )
-
-    got = [send(two, 2, 0), send(two_away, 2, 1)]
-    keys_y = [sketch_act] + [shift(sketch_act, "y", d) for d in (1, 2, 3)]
-    rows_y = lax.all_to_all(for_y, AROUND_Y, 0, 0, tiled=True).reshape(8, -1, for_y.shape[-1])
-    one, one_away, three, three_away = turn(coords, out_grads, (1, 3))
     sketch_grad = sketch(out_grads, grad_signs, grad_picks, table)
     scaled_act = (rows_act * inv_act[:, None]).astype(BF)
     left_part = contract_rows(scaled_act, gradient).astype(BF)
     left_part = left_part.reshape(n_data, rank // n_data, cols)
     panel = jnp.broadcast_to(panel_grad.reshape(1, -1, cols), (n_data, rank // n_data, cols))
     mixed = jnp.concatenate([left_part, panel], axis=1)
-    (got, one, one_away, three, three_away, rows_y, mixed, sketch_grad, keys_y, scaled_act) = phase(
-        got, one, one_away, three, three_away, rows_y, mixed, sketch_grad, keys_y, scaled_act
-    )
-    got_two, got_two_away = got
+    (got, one, one_away, three, three_away, mixed, sketch_grad, sketch_act, scaled_act, activations) = phase(
+        got, one, one_away, three, three_away, mixed, sketch_grad, sketch_act, scaled_act, activations
+    )
+    got_two, got_two_away, got_here_away = got
 
     keys_z = lax.all_gather(sketch_grad, ALONG_Z, axis=0)
-    got = [send(one, 1, 0), send(three, 3, 0), send(here_away, 0, 1)]
-    both = jnp.concatenate(keys_y, axis=0)
+    got = [send(one, 1, 0), send(three, 3, 0), shift(sketch_act, "y", 2)]
     mixed = lax.all_to_all(mixed, DATA, 0, 0, tiled=True)
-    (got, one_away, three_away, both, mixed) = phase(got, one_away, three_away, both, mixed)
-    got_one, got_three, got_here_away = got
+    for_y = turn_act(activations)
+    (got, one_away, three_away, mixed, for_y, sketch_act) = phase(
+        got, one_away, three_away, mixed, for_y, sketch_act
+    )
+    got_one, got_three, keys_two = got
     left_sum = mixed[:, : rank // n_data].astype(F32).sum(0).astype(BF)
-    keys_sib = swap(both)
-    (left_sum, mixed, keys_sib, one_away, three_away) = phase(
-        left_sum, mixed, keys_sib, one_away, three_away
-    )
+    (left_sum, one_away, three_away, sketch_act) = phase(left_sum, one_away, three_away, sketch_act)
 
     got = [send(one_away, 1, 1), send(three_away, 3, 1)]
+    got += [shift(sketch_act, "y", 1), shift(sketch_act, "y", 3)]
     left_sum = share(left_sum, DATA, n_data).reshape(rank, cols)
     rows_grad = mixed[:, rank // n_data :].reshape(cols, rank)
     scaled_grad = (rows_grad * inv_grad[:, None]).astype(BF)
-    partial = part_act(coords, rows_y, keys_y, keys_sib, token_scale)
-    (got, left_sum, scaled_grad, partial, keys_z) = phase(got, left_sum, scaled_grad, partial, keys_z)
-    got_one_away, got_three_away = got
-    factor_act = lax.psum_scatter(partial, ("x", "z"), scatter_dimension=0, tiled=True).astype(F32)
-
     left_core = jnp.dot(core_act, left_sum.astype(F32), precision=lax.Precision.HIGHEST)
     left = inv_act[:, None] * gradient - expand_rows(scaled_act, left_core)
     left = left.astype(BF)
     right_part = jnp.dot(left, scaled_grad, preferred_element_type=F32).astype(BF)
-    (right_part, left, keys_z) = phase(right_part, left, keys_z)
-
+    (got, left, right_part, keys_z, sketch_act) = phase(got, left, right_part, keys_z, sketch_act)
+    got_one_away, got_three_away, keys_one, keys_three = got
+    keys_y = [sketch_act, keys_one, keys_two, keys_three]
+
+    rows_y = lax.all_to_all(for_y, AROUND_Y, 0, 0, tiled=True).reshape(8, -1, for_y.shape[-1])
+    both = jnp.concatenate(keys_y, axis=0)
     received = [
         here,
         got_here_away,
@@ -522,34 +505,40 @@
         got_three,
         got_three_away,
     ]
-    right_sum = deal(right_part.reshape(n_group, rows // n_group, rank), GROUP).astype(BF)
     far = part_grad(coords, received, keys_z, token_scale, (2, 6), 2)
-    (far, right_sum, keys_z) = phase(far, right_sum, keys_z)
+    (far, both, keys_z, rows_y) = phase(far, both, keys_z, rows_y)
 
     ways = (("x", 1), ("x", 3), ("y", 1), ("y", 3))
     via = [shift(f, *way) for f, way in zip(far, ways)]
-    right_sum = share(right_sum, GROUP, n_group).reshape(rows, rank)
+    right_sum = deal(right_part.reshape(n_group, rows // n_group, rank), GROUP).astype(BF)
+    keys_sib = swap(both)
     near = part_grad(coords, received, keys_z, token_scale, (1, 3, 5, 7), 2)
-    (via, near, right_sum, keys_z, left) = phase(via, near, right_sum, keys_z, left)
+    (via, near, right_sum, keys_z, keys_sib, rows_y) = phase(
+        via, near, right_sum, keys_z, keys_sib, rows_y
+    )
 
     free, held = [near[1], near[2], near[5], near[6]], [near[0], near[3], near[4], near[7]]
     got_free = [shift(f, *way) for f, way in zip(free, ways)]
     held = add_terms(held, via)
+    right_sum = share(right_sum, GROUP, n_group).reshape(rows, rank)
+    partial = part_act(coords, rows_y, keys_y, keys_sib, token_scale)
+    (got_free, held, right_sum, partial, left, keys_z) = phase(
+        got_free, held, right_sum, partial, left, keys_z
+    )
+    factor_act = lax.psum_scatter(partial, ("x", "z"), scatter_dimension=0, tiled=True).astype(F32)
+
+    got_held = [shift(h, *way) for h, way in zip(held, ways)]
     right_core = jnp.dot(right_sum.astype(F32), core_grad, precision=lax.Precision.HIGHEST)
     precon = left * inv_grad[None, :] - expand_cols(right_core, scaled_grad)
     total = jnp.full((8, 128), jnp.sum(precon * precon), F32)
-    (got_free, held, total, keys_z) = phase(got_free, held, total, keys_z)
-
-    got_held = [shift(h, *way) for h, way in zip(held, ways)]
-    total = share(total, GROUP, n_group).sum(0)
     own_a, own_b = part_grad(coords, received, keys_z, token_scale, (0, 4))
-    (got_held, own_a, own_b, total) = phase(got_held, own_a, own_b, total)
     sum_a, sum_b = merge(
         [
             [own_a, got_held[0], got_free[0], got_free[1], got_held[1]],
             [own_b, got_held[2], got_free[2], got_free[3], got_held[3]],
         ]
     )
+    total = share(total, GROUP, n_group).sum(0)
     (sum_a, sum_b, total) = phase(sum_a, sum_b, total)
 
     got_a = [sum_a[0]] + [shift(sum_a[d], "y", d) for d in (1, 2, 3)]

time: 338 us -> 309 us (0.914)
  waiting for transfers between devices: 72.6 us -> 55.4 us
  matrix products: 22.7 us -> 16.4 us
  local copies, waits for them, and re-layouts: 14.7 us -> 10.3 us
    ppermute x7, waiting for transfers between devices: 21.4 us -> 0.6 us  [send(): return lax.ppermute(array, ALONG_Z, pairs)]
    all_to_all x5, waiting for transfers between devices: 9.78 us -> 20.4 us  [share(): return lax.all_to_all(copies, axes, 0, 0, tiled=True)]
    all_to_all x1, waiting for transfers between devices: 10.3 us -> 0.01 us  [local(): mixed = lax.all_to_all(mixed, DATA, 0, 0, tiled=True)]
    reduce_scatter x1, waiting for transfers between devices: 0.01 us -> 5.69 us  [local(): lax.psum_scatter(partial, ('x', 'z'), scatter_dimension=0, tiled=True)]
    ppermute x12, waiting for transfers between devices: 23.1 us -> 18.8 us  [shift(): lax.ppermute(array, RING_Y, [(spot(y), spot((y + step) % 4)) for y in ran...]
    mul x1, other arithmetic: 6.64 us -> 10.5 us  [local(): update = jnp.minimum(1.0, clip_rms / root_mean) * precon]
    unnamed x56 -> x54, local copies, waits for them, and re-layouts: 8.09 us -> 5.37 us
  transfers between devices with their start and end apart: 39 -> 39, of which waited for: 16 -> 11; matrix products, arithmetic and copies ran while one was open for 13% -> 13% of each run, Pallas kernels for 30% -> 31%
where the time goes in v1:
time: 309 us; the launch traced here: 308 us
  Pallas kernels  100 us (32%)
  starting transfers between devices  90.2 us (29%)
  waiting for transfers between devices  55.4 us (18%)
  other arithmetic  19.9 us (6%)
  matrix products  16.4 us (5%)
  between operations  15.2 us (5%)
  local copies, waits for them, and re-layouts  10.3 us (3%)
    pallas_call x4, Pallas kernels, part_product(): pl.pallas_call(functools.partial(part_kernel, scale, split), grid_spec=pl...  45.3 us
    all_to_all x5, starting transfers between devices, share(): return lax.all_to_all(copies, axes, 0, 0, tiled=True)  27.8 us
    pallas_call x2, Pallas kernels, sketch(): pl.pallas_call(sketch_kernel, grid_spec=pltpu.PrefetchScalarGridSpec(num_...  21.4 us
    all_to_all x5, waiting for transfers between devices, share(): return lax.all_to_all(copies, axes, 0, 0, tiled=True)  20.4 us
    ppermute x12, waiting for transfers between devices, shift(): lax.ppermute(array, RING_Y, [(spot(y), spot((y + step) % 4)) for y in ran...  18.8 us
    ppermute x12, starting transfers between devices, shift(): lax.ppermute(array, RING_Y, [(spot(y), spot((y + step) % 4)) for y in ran...  17.6 us
    ppermute x7, starting transfers between devices, send(): return lax.ppermute(array, ALONG_Z, pairs)  15.4 us
    ppermute x9, starting transfers between devices, shift(): return lax.ppermute(array, axis, [(i, (i + step) % 4) for i in range(4)])  12.9 us
  transfers between devices with their start and end apart: 39, of which 11 were waited for; matrix products, arithmetic and copies ran while one was open for 13% of the time, Pallas kernels for 31%

profile of v1, /device:TPU:1, one launch (start us, length us, event | category | flops | bytes accessed | tf_op | source)
XLA Modules:
  0.0 307.6 jit_solution(17128760389158929188)
XLA Ops:
  7.8 6.2 %turn.2 = (bf16[32,112,128]{2,1,0:T(8,128)(2,1)}, bf16[32,112,128]{2,1,0:T(8,128)(2,1)}, bf16[32,112,128]{2,1,0:T(8,128)(2,1)}, bf16[32,112,128]{2,1,0:T(8,128)(2,1)}) custom-call(s32[4]{0:T(128)} %pad_add_fusion.coords, bf16[128,28672]{1,0:T(8,128)(2,1)} %x_ref.2), custom_call_target="tpu_custom_call" | custom-call | flops 3300000000 | bytes 20400000 | tf_op jit(solution)/shard_map/turn/pallas_call | solution.py:135
  14.0 4.4 %collective-permute-start = (bf16[3584,128]{1,0:T(8,128)(2,1)}, bf16[3584,128]{1,0:T(8,128)(2,1)S(1)}, u32[]{:S(2)}, u32[]{:S(2)}) collective-permute-start(bf16[3584,128]{1,0:T(8,128)(2,1)} %bitcast.81), channel_id=1, source_target_pairs={{0,8},{1,9},{4,12},{5,13},{8,0},{9,1},{12,4},{13,5},{2,10},{3,11},... | collective-permute-start | bytes 2752520 | tf_op jit(solution)/shard_map/ppermute | solution.py:382
  20.2 7.7 %all-to-all-start = ((bf16[16,64,128]{2,1,0:T(8,128)(2,1)}), bf16[16,64,128]{2,1,0:T(8,128)(2,1)S(1)}, u32[]{:S(2)}, u32[]{:S(2)}) async-start(bf16[16,64,128]{2,1,0:T(8,128)(2,1)} %broadcast_in_dim.16), calls=%async_computation | async-start | bytes 524288 | tf_op jit(solution)/shard_map/all_to_all | solution.py:418
  27.9 6.1 %turn.3 = (bf16[32,112,128]{2,1,0:T(8,128)(2,1)}, bf16[32,112,128]{2,1,0:T(8,128)(2,1)}, bf16[32,112,128]{2,1,0:T(8,128)(2,1)}, bf16[32,112,128]{2,1,0:T(8,128)(2,1)}) custom-call(s32[4]{0:T(128)} %pad_add_fusion.coords, bf16[128,28672]{1,0:T(8,128)(2,1)} %x_ref.2), custom_call_target="tpu_custom_call" | custom-call | flops 3300000000 | bytes 20400000 | tf_op jit(solution)/shard_map/turn/pallas_call | solution.py:135
  34.0 13.7 %sketch.2 = bf16[128,2048]{1,0:T(8,128)(2,1)} custom-call(s32[2048]{0:T(1024)} %picks, bf16[128,28672]{1,0:T(8,128)(2,1)} %x_ref.2, s32[1,28672]{1,0:T(1,128)} %bitcast.82, bf16[256,256]{1,0:T(8,128)(2,1)} %constant.41.clone.table_ref), custom_call_target="tpu_custom_call" | custom-call | flops 7150000128 | bytes 44200000 | tf_op jit(solution)/shard_map/sketch/pallas_call | solution.py:78
  47.7 7.7 %sketch.3.refs_8_ = bf16[128,2048]{1,0:T(8,128)(2,1)} custom-call(s32[2048]{0:T(1024)} %picks.1, bf16[128,8192]{1,0:T(8,128)(2,1)} %act_ref, s32[1,8192]{1,0:T(1,128)} %bitcast.83, bf16[256,256]{1,0:T(8,128)(2,1)} %constant.41.clone.table_ref), custom_call_target="tpu_custom_call" | custom-call | flops 2750000128 | bytes 17000000 | tf_op jit(solution)/shard_map/sketch/pallas_call | solution.py:78
  55.5 7.0 %all-to-all-done = bf16[16,64,128]{2,1,0:T(8,128)(2,1)S(1)} async-done(((bf16[16,64,128]{2,1,0:T(8,128)(2,1)}), bf16[16,64,128]{2,1,0:T(8,128)(2,1)S(1)}, u32[]{:S(2)}, u32[]{:S(2)}) %all-to-all-start) | async-done | bytes 262176 | tf_op jit(solution)/shard_map/all_to_all | solution.py:418
  62.8 2.7 convolution_convert_fusion
  65.6 1.0 pad_maximum_fusion.1
  67.2 2.2 collective-permute-start.4
  69.4 5.0 %all-to-all-start.1 = ((bf16[8,32,1792]{2,1,0:T(8,128)(2,1)}), bf16[8,32,1792]{2,1,0:T(8,128)(2,1)}, u32[]{:S(2)}, u32[]{:S(2)}) async-start(bf16[8,32,1792]{2,1,0:T(8,128)(2,1)} %pad_maximum_fusion.1), calls=%async_computation.1 | async-start | bytes 1835008 | tf_op jit(solution)/shard_map/all_to_all | solution.py:474
  74.4 2.6 collective-permute-start.5
  77.1 6.0 %turn_act.1 = bf16[8,16,64,128]{3,2,1,0:T(8,128)(2,1)} custom-call(bf16[128,8192]{1,0:T(8,128)(2,1)} %act_ref), custom_call_target="tpu_custom_call" | custom-call | flops 3300000000 | bytes 20400000 | tf_op jit(solution)/shard_map/turn_act/pallas_call | solution.py:168
  83.1 15.3 %collective-permute-done.5.refs_10_ = bf16[128,2048]{1,0:T(8,128)(2,1)} collective-permute-done((bf16[128,2048]{1,0:T(8,128)(2,1)}, bf16[128,2048]{1,0:T(8,128)(2,1)}, u32[]{:S(2)}, u32[]{:S(2)}) %collective-permute-start.5) | collective-permute-done | bytes 524320 | tf_op jit(solution)/shard_map/ppermute | solution.py:370
  98.9 1.3 slice_convert_fusion
  100.2 1.3 collective-permute-start.8
  101.5 1.7 collective-permute-start.9
  103.2 3.5 %collective-permute-start.6 = (bf16[3584,128]{1,0:T(8,128)(2,1)}, bf16[3584,128]{1,0:T(8,128)(2,1)S(1)}, u32[]{:S(2)}, u32[]{:S(2)}) collective-permute-start(bf16[3584,128]{1,0:T(8,128)(2,1)} %bitcast.76), channel_id=1, source_target_pairs={{0,5},{1,4},{4,9},{5,8},{8,13},{9,12},{12,1},{13,0},{2,7},{3,6},{6... | collective-permute-start | bytes 2752520 | tf_op jit(solution)/shard_map/ppermute | solution.py:382
  106.7 3.7 %collective-permute-start.7 = (bf16[3584,128]{1,0:T(8,128)(2,1)}, bf16[3584,128]{1,0:T(8,128)(2,1)}, u32[]{:S(2)}, u32[]{:S(2)}) collective-permute-start(bf16[3584,128]{1,0:T(8,128)(2,1)} %bitcast.75), channel_id=1, source_target_pairs={{0,13},{1,12},{4,1},{5,0},{8,5},{9,4},{12,9},{13,8},{2,15},{3,14},... | collective-permute-start | bytes 2752520 | tf_op jit(solution)/shard_map/ppermute | solution.py:382
  111.3 4.1 %all-to-all-start.2 = ((bf16[8,16,1792]{2,1,0:T(8,128)(2,1)}), bf16[8,16,1792]{2,1,0:T(8,128)(2,1)}, u32[]{:S(2)}, u32[]{:S(2)}) async-start(bf16[8,16,1792]{2,1,0:T(8,128)(2,1)} %broadcast_in_dim.21), calls=%async_computation.2 | async-start | bytes 917504 | tf_op jit(solution)/shard_map/all_to_all | solution.py:418
  115.5 1.1 multiply_convert_fusion
  116.5 7.9 %all-to-all-done.2 = bf16[8,16,1792]{2,1,0:T(8,128)(2,1)} async-done(((bf16[8,16,1792]{2,1,0:T(8,128)(2,1)}), bf16[8,16,1792]{2,1,0:T(8,128)(2,1)}, u32[]{:S(2)}, u32[]{:S(2)}) %all-to-all-start.2) | async-done | bytes 458784 | tf_op jit(solution)/shard_map/all_to_all | solution.py:418
  124.4 4.8 %all-to-all-start.3 = ((bf16[8,16,64,128]{3,2,1,0:T(8,128)(2,1)}), bf16[8,16,64,128]{3,2,1,0:T(8,128)(2,1)S(1)}, u32[]{:S(2)}, u32[]{:S(2)}) async-start(bf16[8,16,64,128]{3,2,1,0:T(8,128)(2,1)} %turn_act.1), calls=%async_computation.3 | async-start | bytes 4194304 | tf_op jit(solution)/shard_map/all_to_all | solution.py:496
  129.3 1.6 convolution_bitcast_fusion
  130.9 1.1 fusion.1
  132.9 1.5 subtract_convert_fusion
  134.5 1.8 copy-done.4
  136.3 1.8 convolution_convert_fusion.1
  138.2 3.4 %pad_maximum_fusion = bf16[512,2048]{1,0:T(8,128)(2,1)} fusion(bf16[128,2048]{1,0:T(8,128)(2,1)} %collective-permute-done.9.refs_11_, bf16[128,2048]{1,0:T(8,128)(2,1)} %collective-permute-done.5.refs_10_, bf16[128,2048]{1,0:T(8,128)(2,1)} %collective-permute-done.8.refs_9_, bf16[128,2048]{1,0:T(8,128)(2,1)} %sketch.3.refs_8_), kind=kLoop, calls=%fused_computation.6 | loop fusion | flops 8388608 | bytes 4194304 | tf_op jit(solution)/shard_map/concatenate | solution.py:497
  141.6 9.9 %part_product.4 = (bf16[224,2048]{1,0:T(8,128)(2,1)}, bf16[224,2048]{1,0:T(8,128)(2,1)}, bf16[224,2048]{1,0:T(8,128)(2,1)}, bf16[224,2048]{1,0:T(8,128)(2,1)}) custom-call(s32[4]{0:T(128)} %pad_add_fusion.coords, bf16[3584,128]{1,0:T(8,128)(2,1)} %bitcast.70, bf16[3584,128]{1,0:T(8,128)(2,1)} %copy-done.9, bf16[3584,128]{1,0:T(8,128)(2,1)} %collective-permute-done.3.refs_2_, ...), custom_call_target="tpu_custom_call" | custom-call | flops 5500000256 | bytes 34000000 | tf_op jit(solution)/shard_map/part_product/pallas_call | solution.py:210
  151.4 2.6 all-to-all-done.3
  154.1 2.1 collective-permute-start.14
  156.5 2.4 collective-permute-start.11
  158.8 2.7 collective-permute-start.13
  161.5 4.4 %all-to-all-start.4 = ((bf16[16,64,128]{2,1,0:T(8,128)(2,1)}), bf16[16,64,128]{2,1,0:T(8,128)(2,1)S(1)}, u32[]{:S(2)}, u32[]{:S(2)}) async-start(bf16[16,64,128]{2,1,0:T(8,128)(2,1)} %bitcast.20), calls=%async_computation.4 | async-start | bytes 524288 | tf_op jit(solution)/shard_map/all_to_all | solution.py:422
  166.0 15.8 %part_product.5 = (bf16[224,2048]{1,0:T(8,128)(2,1)}, bf16[224,2048]{1,0:T(8,128)(2,1)}, bf16[224,2048]{1,0:T(8,128)(2,1)}, bf16[224,2048]{1,0:T(8,128)(2,1)}, b...) custom-call(s32[4]{0:T(128)} %pad_add_fusion.coords, ...), custom_call_target="tpu_custom_call" | custom-call | flops 8800000000 | bytes 54400000 | tf_op jit(solution)/shard_map/part_product/pallas_call | solution.py:210
  181.8 2.6 all-to-all-done.4
  185.4 2.7 collective-permute-start.16
  188.1 1.5 collective-permute-start.17
  189.5 1.2 collective-permute-start.18
  191.5 5.1 %all-to-all-start.5 = ((bf16[16,64,128]{2,1,0:T(8,128)(2,1)}), bf16[16,64,128]{2,1,0:T(8,128)(2,1)S(1)}, u32[]{:S(2)}, u32[]{:S(2)}) async-start(bf16[16,64,128]{2,1,0:T(8,128)(2,1)} %broadcast_in_dim.22), calls=%async_computation.5 | async-start | bytes 524288 | tf_op jit(solution)/shard_map/all_to_all | solution.py:418
  196.6 9.7 %part_product.6 = bf16[1024,2048]{1,0:T(8,128)(2,1)} custom-call(s32[4]{0:T(128)} %pad_add_fusion.coords, bf16[8,1024,128]{2,1,0:T(8,128)(2,1)} %bitcast.62, bf16[8,1024,128]{2,1,0:T(8,128)(2,1)} %bitcast.63, bf16[8,1024,128]{2,1,0:T(8,128)(2,1)} %bitcast.64, bf16[8,1024,128]{2,1,0:T(8,128)(2,1)} %bitcast.65, bf16[8,1024,128]{2,1,0:T(8,128)(2,1)} %bitcast.66, ...), custom_call_target="tpu_custom_call" | custom-call | flops 6049999872 | bytes 37400000 | tf_op jit(solution)/shard_map/part_product/pallas_call | solution.py:210
  206.3 4.7 %add_terms.1 = (bf16[224,2048]{1,0:T(8,128)(2,1)}, bf16[224,2048]{1,0:T(8,128)(2,1)}, bf16[224,2048]{1,0:T(8,128)(2,1)}, bf16[224,2048]{1,0:T(8,128)(2,1)}) custom-call(bf16[224,2048]{1,0:T(8,128)(2,1)} %get-tuple-element.191.refs_0_, bf16[224,2048]{1,0:T(8,128)(2,1)} %get-tuple-element.192.refs_1_, bf16[224,2048]{1,0:T(8,128)(2,1)} %get-tuple-element.193.refs_2_, ...), custom_call_target="tpu_custom_call" | custom-call | flops 2750000128 | bytes 17000000 | tf_op jit(solution)/shard_map/add_terms/pallas_call | solution.py:280
  211.0 5.4 %all-to-all-done.5 = bf16[16,64,128]{2,1,0:T(8,128)(2,1)S(1)} async-done(((bf16[16,64,128]{2,1,0:T(8,128)(2,1)}), bf16[16,64,128]{2,1,0:T(8,128)(2,1)S(1)}, u32[]{:S(2)}, u32[]{:S(2)}) %all-to-all-start.5) | async-done | bytes 262176 | tf_op jit(solution)/shard_map/all_to_all | solution.py:418
  216.6 2.7 collective-permute-start.20
  220.1 1.8 collective-permute-start.22
  222.3 1.1 fusion.2
  224.4 6.1 %multiply_reduce_fusion = (f32[]{:T(128)}, f32[1024,1792]{1,0:T(8,128)}) fusion(f32[1024,1792]{1,0:T(8,128)S(1)} %fusion.2, f32[1792]{0:T(1024)S(1)} %broadcast_divide_fusion, bf16[1024,1792]{1,0:T(8,128)(2,1)S(1)} %copy-done.5, bf16[1792,128]{1,0:T(8,128)(2,1)S(1)} %copy-done.12, f32[1024,128]{1,0:T(8,128)S(1)} %fusion.8), kind=kOutput, calls=%fused_computation | convolution fusion | flops 480903168 | bytes 19340292 | tf_op jit(solution)/shard_map/dot_general | solution.py:411
  230.4 1.3 broadcast_in_dim_broadcast_in_dim_broadcast_in_dim.3
  231.7 5.5 %all-to-all-start.6 = ((f32[16,8,128]{2,1,0:T(8,128)}), f32[16,8,128]{2,1,0:T(8,128)S(1)}, u32[]{:S(2)}, u32[]{:S(2)}) async-start(f32[16,8,128]{2,1,0:T(8,128)} %broadcast_in_dim_broadcast_in_dim_broadcast_in_dim.3), calls=%async_computation.7 | async-start | bytes 131072 | tf_op jit(solution)/shard_map/all_to_all | solution.py:418
  237.2 9.9 %part_product.7 = (bf16[448,2048]{1,0:T(8,128)(2,1)}, bf16[448,2048]{1,0:T(8,128)(2,1)}) custom-call(s32[4]{0:T(128)} %pad_add_fusion.coords, bf16[3584,128]{1,0:T(8,128)(2,1)} %bitcast.72, bf16[3584,128]{1,0:T(8,128)(2,1)} %copy-done.9, bf16[3584,128]{1,0:T(8,128)(2,1)} %collective-permute-done.3.refs_2_, bf16[3584,128]{1,0:T(8,128)(2,1)} %copy-done.10, ...), custom_call_target="tpu_custom_call" | custom-call | flops 5500000256 | bytes 34000000 | tf_op jit(solution)/shard_map/part_product/pallas_call | solution.py:210
  247.2 7.0 %merge.1 = (f32[112,2048]{1,0:T(8,128)}, bf16[112,2048]{1,0:T(8,128)(2,1)}, bf16[112,2048]{1,0:T(8,128)(2,1)}, bf16[112,2048]{1,0:T(8,128)(2,1)}, f32[112,2048]{...) custom-call(bf16[448,2048]{1,0:T(8,128)(2,1)} %get-tuple-element.210.refs_0_, ...), custom_call_target="tpu_custom_call" | custom-call | flops 3849999872 | bytes 23800000 | tf_op jit(solution)/shard_map/merge/pallas_call | solution.py:310
  254.9 5.4 %all-to-all-start.7 = ((f32[8,8,128]{2,1,0:T(8,128)}), f32[8,8,128]{2,1,0:T(8,128)S(1)}, u32[]{:S(2)}, u32[]{:S(2)}) async-start(f32[8,8,128]{2,1,0:T(8,128)} %broadcast_in_dim.23), calls=%async_computation.8 | async-start | bytes 65536 | tf_op jit(solution)/shard_map/all_to_all | solution.py:418
  260.3 3.1 collective-permute-start.24
  264.2 1.2 collective-permute-start.26
  265.3 2.4 collective-permute-start.27
  269.0 1.2 collective-permute-start.28
  270.2 10.5 %broadcast_multiply_fusion = f32[1024,1792]{1,0:T(8,128)} fusion(f32[]{:T(128)} %bitcast.22, f32[1024,1792]{1,0:T(8,128)} %get-tuple-element.242, f32[1024,1792]{1,0:T(8,128)} %copy-done.3, f32[1792]{0:T(1024)S(1)} %broadcast_divide_fusion, bf16[1024,1792]{1,0:T(8,128)(2,1)} %copy-done.4), kind=kLoop, calls=%fused_computation.3 | loop fusion | flops 9175040 | bytes 25697284 | tf_op jit(solution)/shard_map/mul | solution.py:548
  280.7 3.5 %collective-permute-done.25.refs_3_ = bf16[112,2048]{1,0:T(8,128)(2,1)S(1)} collective-permute-done((bf16[112,2048]{1,0:T(8,128)(2,1)}, bf16[112,2048]{1,0:T(8,128)(2,1)S(1)}, u32[]{:S(2)}, u32[]{:S(2)}) %collective-permute-start.25) | collective-permute-done | bytes 458784 | tf_op jit(solution)/shard_map/ppermute | solution.py:370
  284.2 1.8 collective-permute-done.27.refs_6_
  286.0 2.9 collective-permute-done.28.refs_7_
  289.7 3.6 %finish.1 = f32[224,2048]{1,0:T(8,128)} custom-call(f32[112,2048]{1,0:T(8,128)} %get-tuple-element.230.refs_0_, bf16[112,2048]{1,0:T(8,128)(2,1)} %copy-done.21, bf16[112,2048]{1,0:T(8,128)(2,1)} %copy-done.22, bf16[112,2048]{1,0:T(8,128)(2,1)} %copy-done.23, f32[112,2048]{1,0:T(8,128)} %get-tuple-element.234.refs_4_, bf16[112,2048]{1,0:T(8,128)(2,1)} %copy-done.24, ...), custom_call_target="tpu_custom_call" | custom-call | flops 2200000000 | bytes 13600000 | tf_op jit(solution)/shard_map/finish/pallas_call | solution.py:345
  293.3 5.7 %reduce-scatter.2.cloned.1.call-done = bf16[64,2048]{1,0:T(8,128)(2,1)} async-done(((bf16[1024,2048]{1,0:T(8,128)(2,1)}), bf16[64,2048]{1,0:T(8,128)(2,1)}) %reduce-scatter.2.cloned.1.call-update) | async-done | bytes 262160 | tf_op jit(solution)/shard_map/reduce_scatter | solution.py:528
  299.0 1.8 convert_element_type.73
  (112 shorter events, 12.9 us)
Async XLA Ops:
  7.2 122.1 %copy-start = (f32[128,128]{1,0:T(8,128)S(1)}, f32[128,128]{1,0:T(8,128)}, u32[]{:S(2)}) copy-start(f32[128,128]{1,0:T(8,128)} %param.25) | copy-start | bytes 196612
  7.8 11.6 %copy-start.15 = (bf16[64,128]{1,0:T(8,128)(2,1)S(1)}, bf16[64,128]{1,0:T(8,128)(2,1)}, u32[]{:S(2)}) copy-start(bf16[64,128]{1,0:T(8,128)(2,1)} %param.23) | copy-start | bytes 49156
  14.0 52.5 %collective-permute-start = (bf16[3584,128]{1,0:T(8,128)(2,1)}, bf16[3584,128]{1,0:T(8,128)(2,1)S(1)}, u32[]{:S(2)}, u32[]{:S(2)}) collective-permute-start(bf16[3584,128]{1,0:T(8,128)(2,1)} %bitcast.81), channel_id=1, source_target_pairs={{0,8},{1,9},{4,12},{5,13},{8,0},{9,1},{12,4},{13,5},{2,10},{3,11},... | collective-permute-start | bytes 2752520 | tf_op jit(solution)/shard_map/ppermute | solution.py:382
  18.5 48.1 %collective-permute-start.1 = (bf16[3584,128]{1,0:T(8,128)(2,1)}, bf16[3584,128]{1,0:T(8,128)(2,1)S(1)}, u32[]{:S(2)}, u32[]{:S(2)}) collective-permute-start(bf16[3584,128]{1,0:T(8,128)(2,1)} %bitcast.80), channel_id=1, source_target_pairs={{0,9},{1,8},{4,13},{5,12},{8,1},{9,0},{12,5},{13,4},{2,11},{3,10},... | collective-permute-start | bytes 2752520 | tf_op jit(solution)/shard_map/ppermute | solution.py:382
  19.1 47.5 %collective-permute-start.2 = (bf16[3584,128]{1,0:T(8,128)(2,1)}, bf16[3584,128]{1,0:T(8,128)(2,1)S(1)}, u32[]{:S(2)}, u32[]{:S(2)}) collective-permute-start(bf16[3584,128]{1,0:T(8,128)(2,1)} %bitcast.79), channel_id=1, source_target_pairs={{0,1},{1,0},{4,5},{5,4},{8,9},{9,8},{12,13},{13,12},{2,3},{3,2},{6... | collective-permute-start | bytes 2752520 | tf_op jit(solution)/shard_map/ppermute | solution.py:382
  20.2 42.4 %all-to-all-start = ((bf16[16,64,128]{2,1,0:T(8,128)(2,1)}), bf16[16,64,128]{2,1,0:T(8,128)(2,1)S(1)}, u32[]{:S(2)}, u32[]{:S(2)}) async-start(bf16[16,64,128]{2,1,0:T(8,128)(2,1)} %broadcast_in_dim.16), calls=%async_computation | async-start | bytes 524288 | tf_op jit(solution)/shard_map/all_to_all | solution.py:418
  27.9 110.2 %all-gather.3.cloned.1.call-start = ((), (), s32[]{:S(2)}) async-start(), calls=%async_computation.10 | async-start | bytes 4718592 | tf_op jit(solution)/shard_map/all_gather | solution.py:472
  47.7 7.7 %copy-start.17 = (f32[1024]{0:T(1024)S(1)}, f32[1024]{0:T(1024)}, u32[]{:S(2)}) copy-start(f32[1024]{0:T(1024)} %param.21) | copy-start | bytes 12292
  47.7 7.7 %copy-start.14 = (bf16[224,128]{1,0:T(8,128)(2,1)S(1)}, bf16[224,128]{1,0:T(8,128)(2,1)}, u32[]{:S(2)}) copy-start(bf16[224,128]{1,0:T(8,128)(2,1)} %param.24) | copy-start | bytes 172036
  62.8 14.3 %copy-start.16 = (f32[1792]{0:T(1024)S(1)}, f32[1792]{0:T(1024)}, u32[]{:S(2)}) copy-start(f32[1792]{0:T(1024)} %param.22) | copy-start | bytes 21508
  66.6 16.5 %copy-start.7 = (bf16[3584,128]{1,0:T(8,128)(2,1)}, bf16[3584,128]{1,0:T(8,128)(2,1)S(1)}, u32[]{:S(2)}) copy-start(bf16[3584,128]{1,0:T(8,128)(2,1)S(1)} %collective-permute-done.refs_4_) | copy-start | bytes 2752516
  66.6 16.5 %copy-start.8 = (bf16[3584,128]{1,0:T(8,128)(2,1)}, bf16[3584,128]{1,0:T(8,128)(2,1)S(1)}, u32[]{:S(2)}) copy-start(bf16[3584,128]{1,0:T(8,128)(2,1)S(1)} %collective-permute-done.1.refs_5_) | copy-start | bytes 2752516
  66.6 16.5 %copy-start.9 = (bf16[3584,128]{1,0:T(8,128)(2,1)}, bf16[3584,128]{1,0:T(8,128)(2,1)S(1)}, u32[]{:S(2)}) copy-start(bf16[3584,128]{1,0:T(8,128)(2,1)S(1)} %collective-permute-done.2.refs_1_) | copy-start | bytes 2752516
  66.6 31.7 %collective-permute-start.3 = (bf16[3584,128]{1,0:T(8,128)(2,1)}, bf16[3584,128]{1,0:T(8,128)(2,1)}, u32[]{:S(2)}, u32[]{:S(2)}) collective-permute-start(bf16[3584,128]{1,0:T(8,128)(2,1)} %bitcast.78), channel_id=1, source_target_pairs={{0,4},{1,5},{4,8},{5,9},{8,12},{9,13},{12,0},{13,1},{2,6},{3,7},{6... | collective-permute-start | bytes 2752520 | tf_op jit(solution)/shard_map/ppermute | solution.py:382
  67.2 31.7 %collective-permute-start.4 = (bf16[3584,128]{1,0:T(8,128)(2,1)}, bf16[3584,128]{1,0:T(8,128)(2,1)}, u32[]{:S(2)}, u32[]{:S(2)}) collective-permute-start(bf16[3584,128]{1,0:T(8,128)(2,1)} %bitcast.77), channel_id=1, source_target_pairs={{0,12},{1,13},{4,0},{5,1},{8,4},{9,5},{12,8},{13,9},{2,14},{3,15},... | collective-permute-start | bytes 2752520 | tf_op jit(solution)/shard_map/ppermute | solution.py:382
  69.4 29.0 %all-to-all-start.1 = ((bf16[8,32,1792]{2,1,0:T(8,128)(2,1)}), bf16[8,32,1792]{2,1,0:T(8,128)(2,1)}, u32[]{:S(2)}, u32[]{:S(2)}) async-start(bf16[8,32,1792]{2,1,0:T(8,128)(2,1)} %pad_maximum_fusion.1), calls=%async_computation.1 | async-start | bytes 1835008 | tf_op jit(solution)/shard_map/all_to_all | solution.py:474
  74.4 23.9 %collective-permute-start.5 = (bf16[128,2048]{1,0:T(8,128)(2,1)}, bf16[128,2048]{1,0:T(8,128)(2,1)}, u32[]{:S(2)}, u32[]{:S(2)}) collective-permute-start(bf16[128,2048]{1,0:T(8,128)(2,1)} %sketch.3.refs_8_), channel_id=1, source_target_pairs={{0,2},{16,18},{2,0},{18,16},{1,3},{17,19},{3,1},{19,17},{4,6},{20,... | collective-permute-start | bytes 1572872 | tf_op jit(solution)/shard_map/ppermute | solution.py:370
  100.2 37.9 %collective-permute-start.8 = (bf16[128,2048]{1,0:T(8,128)(2,1)}, bf16[128,2048]{1,0:T(8,128)(2,1)}, u32[]{:S(2)}, u32[]{:S(2)}) collective-permute-start(bf16[128,2048]{1,0:T(8,128)(2,1)} %sketch.3.refs_8_), channel_id=1, source_target_pairs={{0,16},{16,2},{2,18},{18,0},{1,17},{17,3},{3,19},{19,1},{4,20},{20... | collective-permute-start | bytes 1572872 | tf_op jit(solution)/shard_map/ppermute | solution.py:370
  101.5 36.6 %collective-permute-start.9 = (bf16[128,2048]{1,0:T(8,128)(2,1)}, bf16[128,2048]{1,0:T(8,128)(2,1)}, u32[]{:S(2)}, u32[]{:S(2)}) collective-permute-start(bf16[128,2048]{1,0:T(8,128)(2,1)} %sketch.3.refs_8_), channel_id=1, source_target_pairs={{0,18},{16,0},{2,16},{18,2},{1,19},{17,1},{3,17},{19,3},{4,22},{20... | collective-permute-start | bytes 1572872 | tf_op jit(solution)/shard_map/ppermute | solution.py:370
  103.2 34.9 %collective-permute-start.6 = (bf16[3584,128]{1,0:T(8,128)(2,1)}, bf16[3584,128]{1,0:T(8,128)(2,1)S(1)}, u32[]{:S(2)}, u32[]{:S(2)}) collective-permute-start(bf16[3584,128]{1,0:T(8,128)(2,1)} %bitcast.76), channel_id=1, source_target_pairs={{0,5},{1,4},{4,9},{5,8},{8,13},{9,12},{12,1},{13,0},{2,7},{3,6},{6... | collective-permute-start | bytes 2752520 | tf_op jit(solution)/shard_map/ppermute | solution.py:382
  106.7 31.4 %collective-permute-start.7 = (bf16[3584,128]{1,0:T(8,128)(2,1)}, bf16[3584,128]{1,0:T(8,128)(2,1)}, u32[]{:S(2)}, u32[]{:S(2)}) collective-permute-start(bf16[3584,128]{1,0:T(8,128)(2,1)} %bitcast.75), channel_id=1, source_target_pairs={{0,13},{1,12},{4,1},{5,0},{8,5},{9,4},{12,9},{13,8},{2,15},{3,14},... | collective-permute-start | bytes 2752520 | tf_op jit(solution)/shard_map/ppermute | solution.py:382
  111.3 13.1 %all-to-all-start.2 = ((bf16[8,16,1792]{2,1,0:T(8,128)(2,1)}), bf16[8,16,1792]{2,1,0:T(8,128)(2,1)}, u32[]{:S(2)}, u32[]{:S(2)}) async-start(bf16[8,16,1792]{2,1,0:T(8,128)(2,1)} %broadcast_in_dim.21), calls=%async_computation.2 | async-start | bytes 917504 | tf_op jit(solution)/shard_map/all_to_all | solution.py:418
  124.4 29.7 %all-to-all-start.3 = ((bf16[8,16,64,128]{3,2,1,0:T(8,128)(2,1)}), bf16[8,16,64,128]{3,2,1,0:T(8,128)(2,1)S(1)}, u32[]{:S(2)}, u32[]{:S(2)}) async-start(bf16[8,16,64,128]{3,2,1,0:T(8,128)(2,1)} %turn_act.1), calls=%async_computation.3 | async-start | bytes 4194304 | tf_op jit(solution)/shard_map/all_to_all | solution.py:496
  130.9 2.0 copy-start.6
  132.9 3.3 %copy-start.11 = (bf16[1792,128]{1,0:T(8,128)(2,1)S(1)}, bf16[1792,128]{1,0:T(8,128)(2,1)}, u32[]{:S(2)}) copy-start(bf16[1792,128]{1,0:T(8,128)(2,1)} %multiply_convert_fusion) | copy-start | bytes 1376260
  134.5 1.8 copy-start.4
  138.1 3.5 %copy-start.10 = (bf16[3584,128]{1,0:T(8,128)(2,1)}, bf16[3584,128]{1,0:T(8,128)(2,1)S(1)}, u32[]{:S(2)}) copy-start(bf16[3584,128]{1,0:T(8,128)(2,1)S(1)} %collective-permute-done.6.refs_3_) | copy-start | bytes 2752516
  154.1 27.7 %copy-start.2 = (bf16[8,16,64,128]{3,2,1,0:T(8,128)(2,1)}, bf16[8,16,64,128]{3,2,1,0:T(8,128)(2,1)S(1)}, u32[]{:S(2)}) copy-start(bf16[8,16,64,128]{3,2,1,0:T(8,128)(2,1)S(1)} %all-to-all-done.3) | copy-start | bytes 6291460
  154.1 30.4 %collective-permute-start.14 = (bf16[512,2048]{1,0:T(8,128)(2,1)}, bf16[512,2048]{1,0:T(8,128)(2,1)}, u32[]{:S(2)}, u32[]{:S(2)}) collective-permute-start(bf16[512,2048]{1,0:T(8,128)(2,1)} %pad_maximum_fusion), channel_id=1, source_target_pairs={{0,1},{1,0},{2,3},{3,2},{4,5},{5,4},{6,7},{7,6},{8,9},{9,8},{10,11... | collective-permute-start | bytes 6291464 | tf_op jit(solution)/shard_map/ppermute | solution.py:377
  156.2 28.3 %collective-permute-start.10 = (bf16[224,2048]{1,0:T(8,128)(2,1)}, bf16[224,2048]{1,0:T(8,128)(2,1)S(1)}, u32[]{:S(2)}, u32[]{:S(2)}) collective-permute-start(bf16[224,2048]{1,0:T(8,128)(2,1)} %get-tuple-element.171), channel_id=1, source_target_pairs={{0,32},{32,64},{64,96},{96,0},{1,33},{33,65},{65,97},{97,1},{2,34}... | collective-permute-start | bytes 2752520 | tf_op jit(solution)/shard_map/ppermute | solution.py:373
  156.5 28.0 %collective-permute-start.11 = (bf16[224,2048]{1,0:T(8,128)(2,1)}, bf16[224,2048]{1,0:T(8,128)(2,1)}, u32[]{:S(2)}, u32[]{:S(2)}) collective-permute-start(bf16[224,2048]{1,0:T(8,128)(2,1)} %get-tuple-element.172), channel_id=1, source_target_pairs={{0,96},{32,0},{64,32},{96,64},{1,97},{33,1},{65,33},{97,65},{2,98}... | collective-permute-start | bytes 2752520 | tf_op jit(solution)/shard_map/ppermute | solution.py:373
  158.8 25.6 %collective-permute-start.12 = (bf16[224,2048]{1,0:T(8,128)(2,1)}, bf16[224,2048]{1,0:T(8,128)(2,1)}, u32[]{:S(2)}, u32[]{:S(2)}) collective-permute-start(bf16[224,2048]{1,0:T(8,128)(2,1)} %get-tuple-element.173), channel_id=1, source_target_pairs={{0,16},{16,2},{2,18},{18,0},{1,17},{17,3},{3,19},{19,1},{4,20},{20... | collective-permute-start | bytes 2752520 | tf_op jit(solution)/shard_map/ppermute | solution.py:370
  158.8 25.6 %collective-permute-start.13 = (bf16[224,2048]{1,0:T(8,128)(2,1)}, bf16[224,2048]{1,0:T(8,128)(2,1)}, u32[]{:S(2)}, u32[]{:S(2)}) collective-permute-start(bf16[224,2048]{1,0:T(8,128)(2,1)} %get-tuple-element.174), channel_id=1, source_target_pairs={{0,18},{16,0},{2,16},{18,2},{1,19},{17,1},{3,17},{19,3},{4,22},{20... | collective-permute-start | bytes 2752520 | tf_op jit(solution)/shard_map/ppermute | solution.py:370
  161.5 22.9 %all-to-all-start.4 = ((bf16[16,64,128]{2,1,0:T(8,128)(2,1)}), bf16[16,64,128]{2,1,0:T(8,128)(2,1)S(1)}, u32[]{:S(2)}, u32[]{:S(2)}) async-start(bf16[16,64,128]{2,1,0:T(8,128)(2,1)} %bitcast.20), calls=%async_computation.4 | async-start | bytes 524288 | tf_op jit(solution)/shard_map/all_to_all | solution.py:422
  185.4 31.1 %collective-permute-start.15 = (bf16[224,2048]{1,0:T(8,128)(2,1)}, bf16[224,2048]{1,0:T(8,128)(2,1)S(1)}, u32[]{:S(2)}, u32[]{:S(2)}) collective-permute-start(bf16[224,2048]{1,0:T(8,128)(2,1)} %get-tuple-element.187), channel_id=1, source_target_pairs={{0,32},{32,64},{64,96},{96,0},{1,33},{33,65},{65,97},{97,1},{2,34}... | collective-permute-start | bytes 2752520 | tf_op jit(solution)/shard_map/ppermute | solution.py:373
  185.4 31.1 %collective-permute-start.16 = (bf16[224,2048]{1,0:T(8,128)(2,1)}, bf16[224,2048]{1,0:T(8,128)(2,1)S(1)}, u32[]{:S(2)}, u32[]{:S(2)}) collective-permute-start(bf16[224,2048]{1,0:T(8,128)(2,1)} %get-tuple-element.188), channel_id=1, source_target_pairs={{0,96},{32,0},{64,32},{96,64},{1,97},{33,1},{65,33},{97,65},{2,98}... | collective-permute-start | bytes 2752520 | tf_op jit(solution)/shard_map/ppermute | solution.py:373
  188.1 28.4 %collective-permute-start.17 = (bf16[224,2048]{1,0:T(8,128)(2,1)}, bf16[224,2048]{1,0:T(8,128)(2,1)}, u32[]{:S(2)}, u32[]{:S(2)}) collective-permute-start(bf16[224,2048]{1,0:T(8,128)(2,1)} %get-tuple-element.189), channel_id=1, source_target_pairs={{0,16},{16,2},{2,18},{18,0},{1,17},{17,3},{3,19},{19,1},{4,20},{20... | collective-permute-start | bytes 2752520 | tf_op jit(solution)/shard_map/ppermute | solution.py:370
  189.5 27.0 %collective-permute-start.18 = (bf16[224,2048]{1,0:T(8,128)(2,1)}, bf16[224,2048]{1,0:T(8,128)(2,1)}, u32[]{:S(2)}, u32[]{:S(2)}) collective-permute-start(bf16[224,2048]{1,0:T(8,128)(2,1)} %get-tuple-element.190), channel_id=1, source_target_pairs={{0,18},{16,0},{2,16},{18,2},{1,19},{17,1},{3,17},{19,3},{4,22},{20... | collective-permute-start | bytes 2752520 | tf_op jit(solution)/shard_map/ppermute | solution.py:370
  191.5 24.9 %all-to-all-start.5 = ((bf16[16,64,128]{2,1,0:T(8,128)(2,1)}), bf16[16,64,128]{2,1,0:T(8,128)(2,1)S(1)}, u32[]{:S(2)}, u32[]{:S(2)}) async-start(bf16[16,64,128]{2,1,0:T(8,128)(2,1)} %broadcast_in_dim.22), calls=%async_computation.5 | async-start | bytes 524288 | tf_op jit(solution)/shard_map/all_to_all | solution.py:418
  196.6 102.4 %reduce-scatter.2.cloned.1.call-start = ((), (), s32[]{:S(2)}) async-start(), calls=%async_computation.9 | async-start | bytes 4456448 | tf_op jit(solution)/shard_map/reduce_scatter | solution.py:528
  211.0 10.9 %copy-start.13 = (f32[128,128]{1,0:T(8,128)S(1)}, f32[128,128]{1,0:T(8,128)}, u32[]{:S(2)}) copy-start(f32[128,128]{1,0:T(8,128)} %param.26) | copy-start | bytes 196612
  211.0 11.3 %copy-start.12 = (bf16[1792,128]{1,0:T(8,128)(2,1)S(1)}, bf16[1792,128]{1,0:T(8,128)(2,1)}, u32[]{:S(2)}) copy-start(bf16[1792,128]{1,0:T(8,128)(2,1)} %multiply_convert_fusion) | copy-start | bytes 1376260
  216.4 7.0 %copy-start.18 = (bf16[224,2048]{1,0:T(8,128)(2,1)}, bf16[224,2048]{1,0:T(8,128)(2,1)S(1)}, u32[]{:S(2)}) copy-start(bf16[224,2048]{1,0:T(8,128)(2,1)S(1)} %collective-permute-done.15.refs_2_) | copy-start | bytes 2752516
  216.5 7.0 %copy-start.19 = (bf16[224,2048]{1,0:T(8,128)(2,1)}, bf16[224,2048]{1,0:T(8,128)(2,1)S(1)}, u32[]{:S(2)}) copy-start(bf16[224,2048]{1,0:T(8,128)(2,1)S(1)} %collective-permute-done.16.refs_3_) | copy-start | bytes 2752516
  216.5 30.7 %collective-permute-start.19 = (bf16[224,2048]{1,0:T(8,128)(2,1)}, bf16[224,2048]{1,0:T(8,128)(2,1)}, u32[]{:S(2)}, u32[]{:S(2)}) collective-permute-start(bf16[224,2048]{1,0:T(8,128)(2,1)} %get-tuple-element.211), channel_id=1, source_target_pairs={{0,32},{32,64},{64,96},{96,0},{1,33},{33,65},{65,97},{97,1},{2,34}... | collective-permute-start | bytes 2752520 | tf_op jit(solution)/shard_map/ppermute | solution.py:373
  216.6 30.6 %collective-permute-start.20 = (bf16[224,2048]{1,0:T(8,128)(2,1)}, bf16[224,2048]{1,0:T(8,128)(2,1)}, u32[]{:S(2)}, u32[]{:S(2)}) collective-permute-start(bf16[224,2048]{1,0:T(8,128)(2,1)} %get-tuple-element.214), channel_id=1, source_target_pairs={{0,96},{32,0},{64,32},{96,64},{1,97},{33,1},{65,33},{97,65},{2,98}... | collective-permute-start | bytes 2752520 | tf_op jit(solution)/shard_map/ppermute | solution.py:373
  219.3 27.9 %collective-permute-start.21 = (bf16[224,2048]{1,0:T(8,128)(2,1)}, bf16[224,2048]{1,0:T(8,128)(2,1)}, u32[]{:S(2)}, u32[]{:S(2)}) collective-permute-start(bf16[224,2048]{1,0:T(8,128)(2,1)} %get-tuple-element.216), channel_id=1, source_target_pairs={{0,16},{16,2},{2,18},{18,0},{1,17},{17,3},{3,19},{19,1},{4,20},{20... | collective-permute-start | bytes 2752520 | tf_op jit(solution)/shard_map/ppermute | solution.py:370
  220.1 27.1 %collective-permute-start.22 = (bf16[224,2048]{1,0:T(8,128)(2,1)}, bf16[224,2048]{1,0:T(8,128)(2,1)}, u32[]{:S(2)}, u32[]{:S(2)}) collective-permute-start(bf16[224,2048]{1,0:T(8,128)(2,1)} %get-tuple-element.219), channel_id=1, source_target_pairs={{0,18},{16,0},{2,16},{18,2},{1,19},{17,1},{3,17},{19,3},{4,22},{20... | collective-permute-start | bytes 2752520 | tf_op jit(solution)/shard_map/ppermute | solution.py:370
  222.3 2.1 copy-start.5
  224.4 6.1 %copy-start.3 = (f32[1024,1792]{1,0:T(8,128)}, f32[1024,1792]{1,0:T(8,128)S(1)}, u32[]{:S(2)}) copy-start(f32[1024,1792]{1,0:T(8,128)S(1)} %fusion.2) | copy-start | bytes 22020100
  231.7 15.4 %all-to-all-start.6 = ((f32[16,8,128]{2,1,0:T(8,128)}), f32[16,8,128]{2,1,0:T(8,128)S(1)}, u32[]{:S(2)}, u32[]{:S(2)}) async-start(f32[16,8,128]{2,1,0:T(8,128)} %broadcast_in_dim_broadcast_in_dim_broadcast_in_dim.3), calls=%async_computation.7 | async-start | bytes 131072 | tf_op jit(solution)/shard_map/all_to_all | solution.py:418
  254.2 14.7 %collective-permute-start.23 = (bf16[112,2048]{1,0:T(8,128)(2,1)}, bf16[112,2048]{1,0:T(8,128)(2,1)S(1)}, u32[]{:S(2)}, u32[]{:S(2)}) collective-permute-start(bf16[112,2048]{1,0:T(8,128)(2,1)} %get-tuple-element.231), channel_id=1, source_target_pairs={{0,16},{16,2},{2,18},{18,0},{1,17},{17,3},{3,19},{19,1},{4,20},{20... | collective-permute-start | bytes 1376264 | tf_op jit(solution)/shard_map/ppermute | solution.py:370
  254.9 12.8 %all-to-all-start.7 = ((f32[8,8,128]{2,1,0:T(8,128)}), f32[8,8,128]{2,1,0:T(8,128)S(1)}, u32[]{:S(2)}, u32[]{:S(2)}) async-start(f32[8,8,128]{2,1,0:T(8,128)} %broadcast_in_dim.23), calls=%async_computation.8 | async-start | bytes 65536 | tf_op jit(solution)/shard_map/all_to_all | solution.py:418
  260.3 20.4 %collective-permute-start.24 = (bf16[112,2048]{1,0:T(8,128)(2,1)}, bf16[112,2048]{1,0:T(8,128)(2,1)S(1)}, u32[]{:S(2)}, u32[]{:S(2)}) collective-permute-start(bf16[112,2048]{1,0:T(8,128)(2,1)} %get-tuple-element.232), channel_id=1, source_target_pairs={{0,2},{16,18},{2,0},{18,16},{1,3},{17,19},{3,1},{19,17},{4,6},{20,... | collective-permute-start | bytes 1376264 | tf_op jit(solution)/shard_map/ppermute | solution.py:370
  263.4 20.9 %collective-permute-start.25 = (bf16[112,2048]{1,0:T(8,128)(2,1)}, bf16[112,2048]{1,0:T(8,128)(2,1)S(1)}, u32[]{:S(2)}, u32[]{:S(2)}) collective-permute-start(bf16[112,2048]{1,0:T(8,128)(2,1)} %get-tuple-element.233), channel_id=1, source_target_pairs={{0,18},{16,0},{2,16},{18,2},{1,19},{17,1},{3,17},{19,3},{4,22},{20... | collective-permute-start | bytes 1376264 | tf_op jit(solution)/shard_map/ppermute | solution.py:370
  264.2 20.1 %collective-permute-start.26 = (bf16[112,2048]{1,0:T(8,128)(2,1)}, bf16[112,2048]{1,0:T(8,128)(2,1)S(1)}, u32[]{:S(2)}, u32[]{:S(2)}) collective-permute-start(bf16[112,2048]{1,0:T(8,128)(2,1)} %get-tuple-element.235), channel_id=1, source_target_pairs={{0,32},{32,64},{64,96},{96,0},{1,33},{33,65},{65,97},{97,1},{2,34}... | collective-permute-start | bytes 1376264 | tf_op jit(solution)/shard_map/ppermute | solution.py:373
  265.3 20.7 %collective-permute-start.27 = (bf16[112,2048]{1,0:T(8,128)(2,1)}, bf16[112,2048]{1,0:T(8,128)(2,1)S(1)}, u32[]{:S(2)}, u32[]{:S(2)}) collective-permute-start(bf16[112,2048]{1,0:T(8,128)(2,1)} %get-tuple-element.236), channel_id=1, source_target_pairs={{0,64},{32,96},{64,0},{96,32},{1,65},{33,97},{65,1},{97,33},{2,66}... | collective-permute-start | bytes 1376264 | tf_op jit(solution)/shard_map/ppermute | solution.py:373
  269.0 11.7 %copy-start.21 = (bf16[112,2048]{1,0:T(8,128)(2,1)}, bf16[112,2048]{1,0:T(8,128)(2,1)S(1)}, u32[]{:S(2)}) copy-start(bf16[112,2048]{1,0:T(8,128)(2,1)S(1)} %collective-permute-done.23.refs_1_) | copy-start | bytes 1376260
  269.0 20.0 %collective-permute-start.28 = (bf16[112,2048]{1,0:T(8,128)(2,1)}, bf16[112,2048]{1,0:T(8,128)(2,1)S(1)}, u32[]{:S(2)}, u32[]{:S(2)}) collective-permute-start(bf16[112,2048]{1,0:T(8,128)(2,1)} %get-tuple-element.237), channel_id=1, source_target_pairs={{0,96},{32,0},{64,32},{96,64},{1,97},{33,1},{65,33},{97,65},{2,98}... | collective-permute-start | bytes 1376264 | tf_op jit(solution)/shard_map/ppermute | solution.py:373
  270.2 30.5 %copy-start.1 = (f32[128,128]{1,0:T(8,128)S(1)}, f32[128,128]{1,0:T(8,128)}, u32[]{:S(2)}) copy-start(f32[128,128]{1,0:T(8,128)} %param.25) | copy-start | bytes 196612
  280.7 8.2 %copy-start.22 = (bf16[112,2048]{1,0:T(8,128)(2,1)}, bf16[112,2048]{1,0:T(8,128)(2,1)S(1)}, u32[]{:S(2)}) copy-start(bf16[112,2048]{1,0:T(8,128)(2,1)S(1)} %collective-permute-done.24.refs_2_) | copy-start | bytes 1376260
  284.2 4.7 %copy-start.23 = (bf16[112,2048]{1,0:T(8,128)(2,1)}, bf16[112,2048]{1,0:T(8,128)(2,1)S(1)}, u32[]{:S(2)}) copy-start(bf16[112,2048]{1,0:T(8,128)(2,1)S(1)} %collective-permute-done.25.refs_3_) | copy-start | bytes 1376260
  284.2 4.7 %copy-start.24 = (bf16[112,2048]{1,0:T(8,128)(2,1)}, bf16[112,2048]{1,0:T(8,128)(2,1)S(1)}, u32[]{:S(2)}) copy-start(bf16[112,2048]{1,0:T(8,128)(2,1)S(1)} %collective-permute-done.26.refs_5_) | copy-start | bytes 1376260
  286.0 2.9 copy-start.25
  (2 other events, 1.7 us)
Sparse Core Ops, SparseCore 0:
  66.8 42.3 all-gather.2
  216.6 82.3 reduce-scatter.1

commit v2 on v1

--- a/solution.py
+++ b/solution.py
@@ -126,10 +126,12 @@
     tokens = grads.shape[0]
     wide = grads.shape[1] // 8
     part = wide // 32
-    first, last = shifts[0], shifts[-1]
 
     def slab(i, j, c):
-        return (0, ((c[2] + jnp.where(i == 0, first, last)) & 3) * 2 + j)
+        step = shifts[0]
+        for k in range(1, len(shifts)):
+            step = jnp.where(i >= k, shifts[k], step)
+        return (0, ((c[2] + step) & 3) * 2 + j)
 
     count = 2 * len(shifts)
     outs = pl.pallas_call(
@@ -449,14 +451,14 @@
     inv_act = 1.0 / damped_act
     inv_grad = 1.0 / damped_grad
 
-    here, here_away, two, two_away = turn(coords, out_grads, (0, 2))
-    (two, two_away, here_away, coords, panel_act, act_picks, grad_picks, gradient) = phase(
-        two, two_away, here_away, coords, panel_act, act_picks, grad_picks, gradient
-    )
-
-    got = [send(two, 2, 0), send(two_away, 2, 1), send(here_away, 0, 1)]
+    two, two_away = turn(coords, out_grads, (2,))
+    (two, two_away, coords, panel_act, act_picks, grad_picks, gradient) = phase(
+        two, two_away, coords, panel_act, act_picks, grad_picks, gradient
+    )
+
+    got = [send(two, 2, 0), send(two_away, 2, 1)]
     rows_act = share(panel_act, GROUP, n_group).reshape(rows, rank)
-    one, one_away, three, three_away = turn(coords, out_grads, (1, 3))
+    here, here_away, one, one_away, three, three_away = turn(coords, out_grads, (0, 1, 3))
     sketch_act = sketch(activations, act_signs, act_picks, table)
     sketch_grad = sketch(out_grads, grad_signs, grad_picks, table)
     scaled_act = (rows_act * inv_act[:, None]).astype(BF)
@@ -464,21 +466,20 @@
     left_part = left_part.reshape(n_data, rank // n_data, cols)
     panel = jnp.broadcast_to(panel_grad.reshape(1, -1, cols), (n_data, rank // n_data, cols))
     mixed = jnp.concatenate([left_part, panel], axis=1)
-    (got, one, one_away, three, three_away, mixed, sketch_grad, sketch_act, scaled_act, activations) = phase(
-        got, one, one_away, three, three_away, mixed, sketch_grad, sketch_act, scaled_act, activations
-    )
-    got_two, got_two_away, got_here_away = got
+    (got, here_away, one, one_away, three, three_away, mixed, sketch_grad, sketch_act, scaled_act, activations) = phase(
+        got, here_away, one, one_away, three, three_away, mixed, sketch_grad, sketch_act, scaled_act, activations
+    )
+    got_two, got_two_away = got
 
     keys_z = lax.all_gather(sketch_grad, ALONG_Z, axis=0)
-    got = [send(one, 1, 0), send(three, 3, 0), shift(sketch_act, "y", 2)]
+    got = [send(one, 1, 0), send(three, 3, 0), shift(sketch_act, "y", 2), send(here_away, 0, 1)]
     mixed = lax.all_to_all(mixed, DATA, 0, 0, tiled=True)
     for_y = turn_act(activations)
-    (got, one_away, three_away, mixed, for_y, sketch_act) = phase(
-        got, one_away, three_away, mixed, for_y, sketch_act
-    )
-    got_one, got_three, keys_two = got
+    (got, one_away, three_away, for_y, sketch_act) = phase(
+        got, one_away, three_away, for_y, sketch_act
+    )
+    got_one, got_three, keys_two, got_here_away = got
     left_sum = mixed[:, : rank // n_data].astype(F32).sum(0).astype(BF)
-    (left_sum, one_away, three_away, sketch_act) = phase(left_sum, one_away, three_away, sketch_act)
 
     got = [send(one_away, 1, 1), send(three_away, 3, 1)]
     got += [shift(sketch_act, "y", 1), shift(sketch_act, "y", 3)]

time: 309 us -> 305 us (0.987)
  waiting for transfers between devices: 55.4 us -> 51.6 us
    ppermute x7, waiting for transfers between devices: 0.6 us -> 20.2 us  [send(): return lax.ppermute(array, ALONG_Z, pairs)]
    ppermute x12, waiting for transfers between devices: 18.8 us -> 6.48 us  [shift(): lax.ppermute(array, RING_Y, [(spot(y), spot((y + step) % 4)) for y in ran...]
    all_to_all x5, waiting for transfers between devices: 20.4 us -> 8.49 us  [share(): return lax.all_to_all(copies, axes, 0, 0, tiled=True)]
  transfers between devices with their start and end apart: 39 -> 39, of which waited for: 11 -> 14; matrix products, arithmetic and copies ran while one was open for 13% -> 13% of each run, Pallas kernels for 31% -> 32%
where the time goes in v2:
time: 305 us; the launch traced here: 304 us
  Pallas kernels  100 us (33%)
  starting transfers between devices  89.8 us (29%)
  waiting for transfers between devices  51.6 us (17%)
  other arithmetic  19.8 us (6%)
  matrix products  16.4 us (5%)
  between operations  15.2 us (5%)
  local copies, waits for them, and re-layouts  10.4 us (3%)
    pallas_call x4, Pallas kernels, part_product(): pl.pallas_call(functools.partial(part_kernel, scale, split), grid_spec=pl...  45.3 us
    all_to_all x5, starting transfers between devices, share(): return lax.all_to_all(copies, axes, 0, 0, tiled=True)  26.9 us
    pallas_call x2, Pallas kernels, sketch(): pl.pallas_call(sketch_kernel, grid_spec=pltpu.PrefetchScalarGridSpec(num_...  21.4 us
    ppermute x7, waiting for transfers between devices, send(): return lax.ppermute(array, ALONG_Z, pairs)  20.2 us
    ppermute x12, starting transfers between devices, shift(): lax.ppermute(array, RING_Y, [(spot(y), spot((y + step) % 4)) for y in ran...  18.1 us
    ppermute x7, starting transfers between devices, send(): return lax.ppermute(array, ALONG_Z, pairs)  16.8 us
    ppermute x9, starting transfers between devices, shift(): return lax.ppermute(array, axis, [(i, (i + step) % 4) for i in range(4)])  13.3 us
    pallas_call x2, Pallas kernels, turn(): pl.pallas_call(functools.partial(turn_kernel, shifts), grid_spec=pltpu.Pr...  12.3 us
  transfers between devices with their start and end apart: 39, of which 14 were waited for; matrix products, arithmetic and copies ran while one was open for 13% of the time, Pallas kernels for 32%

profile of v2, /device:TPU:1, one launch (start us, length us, event | category | flops | bytes accessed | tf_op | source)
XLA Modules:
  0.0 303.5 jit_solution(16181084890445446969)
XLA Ops:
  7.8 3.9 %turn.2 = (bf16[32,112,128]{2,1,0:T(8,128)(2,1)}, bf16[32,112,128]{2,1,0:T(8,128)(2,1)}) custom-call(s32[4]{0:T(128)} %pad_add_fusion.coords, bf16[128,28672]{1,0:T(8,128)(2,1)} %x_ref.2), custom_call_target="tpu_custom_call" | custom-call | flops 3300000000 | bytes 20400000 | tf_op jit(solution)/shard_map/turn/pallas_call | solution.py:137
  11.7 4.4 %collective-permute-start = (bf16[3584,128]{1,0:T(8,128)(2,1)}, bf16[3584,128]{1,0:T(8,128)(2,1)S(1)}, u32[]{:S(2)}, u32[]{:S(2)}) collective-permute-start(bf16[3584,128]{1,0:T(8,128)(2,1)} %bitcast.81), channel_id=1, source_target_pairs={{0,8},{1,9},{4,12},{5,13},{8,0},{9,1},{12,4},{13,5},{2,10},{3,11},... | collective-permute-start | bytes 2752520 | tf_op jit(solution)/shard_map/ppermute | solution.py:384
  17.5 7.7 %all-to-all-start = ((bf16[16,64,128]{2,1,0:T(8,128)(2,1)}), bf16[16,64,128]{2,1,0:T(8,128)(2,1)S(1)}, u32[]{:S(2)}, u32[]{:S(2)}) async-start(bf16[16,64,128]{2,1,0:T(8,128)(2,1)} %broadcast_in_dim.16), calls=%async_computation | async-start | bytes 524288 | tf_op jit(solution)/shard_map/all_to_all | solution.py:420
  25.2 8.4 %turn.3 = (bf16[32,112,128]{2,1,0:T(8,128)(2,1)}, bf16[32,112,128]{2,1,0:T(8,128)(2,1)}, bf16[32,112,128]{2,1,0:T(8,128)(2,1)}, bf16[32,112,128]{2,1,0:T(8,128)(...) custom-call(s32[4]{0:T(128)} %pad_add_fusion.coords, bf16[128,28672]{1,0:T(8,128)(2,1)} %x_ref.2), custom_call_target="tpu_custom_call" | custom-call | flops 3300000000 | bytes 20400000 | tf_op jit(solution)/shard_map/turn/pallas_call | solution.py:137
  33.6 13.7 %sketch.2 = bf16[128,2048]{1,0:T(8,128)(2,1)} custom-call(s32[2048]{0:T(1024)} %picks, bf16[128,28672]{1,0:T(8,128)(2,1)} %x_ref.2, s32[1,28672]{1,0:T(1,128)} %bitcast.82, bf16[256,256]{1,0:T(8,128)(2,1)} %constant.41.clone.table_ref), custom_call_target="tpu_custom_call" | custom-call | flops 7150000128 | bytes 44200000 | tf_op jit(solution)/shard_map/sketch/pallas_call | solution.py:78
  47.3 7.7 %sketch.3.refs_8_ = bf16[128,2048]{1,0:T(8,128)(2,1)} custom-call(s32[2048]{0:T(1024)} %picks.1, bf16[128,8192]{1,0:T(8,128)(2,1)} %act_ref, s32[1,8192]{1,0:T(1,128)} %bitcast.83, bf16[256,256]{1,0:T(8,128)(2,1)} %constant.41.clone.table_ref), custom_call_target="tpu_custom_call" | custom-call | flops 2750000128 | bytes 17000000 | tf_op jit(solution)/shard_map/sketch/pallas_call | solution.py:78
  55.1 5.2 %all-to-all-done = bf16[16,64,128]{2,1,0:T(8,128)(2,1)S(1)} async-done(((bf16[16,64,128]{2,1,0:T(8,128)(2,1)}), bf16[16,64,128]{2,1,0:T(8,128)(2,1)S(1)}, u32[]{:S(2)}, u32[]{:S(2)}) %all-to-all-start) | async-done | bytes 262176 | tf_op jit(solution)/shard_map/all_to_all | solution.py:420
  60.5 2.7 convolution_convert_fusion
  64.3 5.1 %all-to-all-start.1 = ((bf16[8,32,1792]{2,1,0:T(8,128)(2,1)}), bf16[8,32,1792]{2,1,0:T(8,128)(2,1)}, u32[]{:S(2)}, u32[]{:S(2)}) async-start(bf16[8,32,1792]{2,1,0:T(8,128)(2,1)} %pad_maximum_fusion.1), calls=%async_computation.1 | async-start | bytes 1835008 | tf_op jit(solution)/shard_map/all_to_all | solution.py:476
  70.0 2.2 collective-permute-start.3
  72.1 2.6 collective-permute-start.4
  74.8 1.5 collective-permute-start.5
  76.2 6.0 %turn_act.1 = bf16[8,16,64,128]{3,2,1,0:T(8,128)(2,1)} custom-call(bf16[128,8192]{1,0:T(8,128)(2,1)} %act_ref), custom_call_target="tpu_custom_call" | custom-call | flops 3300000000 | bytes 20400000 | tf_op jit(solution)/shard_map/turn_act/pallas_call | solution.py:170
  82.2 1.1 all-to-all-done.1
  83.3 1.3 slice_convert_fusion
  85.4 4.1 %all-to-all-start.2 = ((bf16[8,16,1792]{2,1,0:T(8,128)(2,1)}), bf16[8,16,1792]{2,1,0:T(8,128)(2,1)}, u32[]{:S(2)}, u32[]{:S(2)}) async-start(bf16[8,16,1792]{2,1,0:T(8,128)(2,1)} %broadcast_in_dim.21), calls=%async_computation.2 | async-start | bytes 917504 | tf_op jit(solution)/shard_map/all_to_all | solution.py:420
  90.7 3.2 %collective-permute-done.4.refs_10_ = bf16[128,2048]{1,0:T(8,128)(2,1)} collective-permute-done((bf16[128,2048]{1,0:T(8,128)(2,1)}, bf16[128,2048]{1,0:T(8,128)(2,1)}, u32[]{:S(2)}, u32[]{:S(2)}) %collective-permute-start.4) | collective-permute-done | bytes 524320 | tf_op jit(solution)/shard_map/ppermute | solution.py:372
  93.9 11.1 %collective-permute-done.2.refs_2_ = bf16[3584,128]{1,0:T(8,128)(2,1)S(1)} collective-permute-done((bf16[3584,128]{1,0:T(8,128)(2,1)}, bf16[3584,128]{1,0:T(8,128)(2,1)S(1)}, u32[]{:S(2)}, u32[]{:S(2)}) %collective-permute-start.2) | collective-permute-done | bytes 917536 | tf_op jit(solution)/shard_map/ppermute | solution.py:384
  104.9 1.2 collective-permute-done.3.refs_6_
  107.0 1.8 collective-permute-start.9
  108.8 5.2 %collective-permute-start.6 = (bf16[3584,128]{1,0:T(8,128)(2,1)}, bf16[3584,128]{1,0:T(8,128)(2,1)S(1)}, u32[]{:S(2)}, u32[]{:S(2)}) collective-permute-start(bf16[3584,128]{1,0:T(8,128)(2,1)} %bitcast.76), channel_id=1, source_target_pairs={{0,5},{1,4},{4,9},{5,8},{8,13},{9,12},{12,1},{13,0},{2,7},{3,6},{6... | collective-permute-start | bytes 2752520 | tf_op jit(solution)/shard_map/ppermute | solution.py:384
  114.1 2.3 collective-permute-start.7
  116.4 3.7 %all-to-all-start.3 = ((bf16[8,16,64,128]{3,2,1,0:T(8,128)(2,1)}), bf16[8,16,64,128]{3,2,1,0:T(8,128)(2,1)S(1)}, u32[]{:S(2)}, u32[]{:S(2)}) async-start(bf16[8,16,64,128]{3,2,1,0:T(8,128)(2,1)} %turn_act.1), calls=%async_computation.3 | async-start | bytes 4194304 | tf_op jit(solution)/shard_map/all_to_all | solution.py:497
  120.2 1.6 convolution_bitcast_fusion
  121.8 1.1 fusion.1
  123.8 1.5 subtract_convert_fusion
  125.4 1.8 copy-done.4
  127.2 1.8 convolution_convert_fusion.1
  129.0 7.8 %collective-permute-done.6.refs_3_ = bf16[3584,128]{1,0:T(8,128)(2,1)S(1)} collective-permute-done((bf16[3584,128]{1,0:T(8,128)(2,1)}, bf16[3584,128]{1,0:T(8,128)(2,1)S(1)}, u32[]{:S(2)}, u32[]{:S(2)}) %collective-permute-start.6) | collective-permute-done | bytes 917536 | tf_op jit(solution)/shard_map/ppermute | solution.py:384
  136.9 3.3 %pad_maximum_fusion = bf16[512,2048]{1,0:T(8,128)(2,1)} fusion(bf16[128,2048]{1,0:T(8,128)(2,1)} %collective-permute-done.9.refs_11_, bf16[128,2048]{1,0:T(8,128)(2,1)} %collective-permute-done.4.refs_10_, bf16[128,2048]{1,0:T(8,128)(2,1)} %collective-permute-done.8.refs_9_, bf16[128,2048]{1,0:T(8,128)(2,1)} %sketch.3.refs_8_), kind=kLoop, calls=%fused_computation.6 | loop fusion | flops 8388608 | bytes 4194304 | tf_op jit(solution)/shard_map/concatenate | solution.py:498
  140.2 9.9 %part_product.4 = (bf16[224,2048]{1,0:T(8,128)(2,1)}, bf16[224,2048]{1,0:T(8,128)(2,1)}, bf16[224,2048]{1,0:T(8,128)(2,1)}, bf16[224,2048]{1,0:T(8,128)(2,1)}) custom-call(s32[4]{0:T(128)} %pad_add_fusion.coords, bf16[3584,128]{1,0:T(8,128)(2,1)} %bitcast.70, bf16[3584,128]{1,0:T(8,128)(2,1)} %collective-permute-done.5.refs_1_, bf16[3584,128]{1,0:T(8,128)(2,1)} %copy-done.9, ...), custom_call_target="tpu_custom_call" | custom-call | flops 5500000256 | bytes 34000000 | tf_op jit(solution)/shard_map/part_product/pallas_call | solution.py:212
  150.2 1.8 collective-permute-start.10
  152.1 1.2 collective-permute-start.11
  153.5 2.4 collective-permute-start.13
  156.0 5.8 %all-to-all-start.4 = ((bf16[16,64,128]{2,1,0:T(8,128)(2,1)}), bf16[16,64,128]{2,1,0:T(8,128)(2,1)S(1)}, u32[]{:S(2)}, u32[]{:S(2)}) async-start(bf16[16,64,128]{2,1,0:T(8,128)(2,1)} %bitcast.20), calls=%async_computation.4 | async-start | bytes 524288 | tf_op jit(solution)/shard_map/all_to_all | solution.py:424
  161.8 15.8 %part_product.5 = (bf16[224,2048]{1,0:T(8,128)(2,1)}, bf16[224,2048]{1,0:T(8,128)(2,1)}, bf16[224,2048]{1,0:T(8,128)(2,1)}, bf16[224,2048]{1,0:T(8,128)(2,1)}, b...) custom-call(s32[4]{0:T(128)} %pad_add_fusion.coords, ...), custom_call_target="tpu_custom_call" | custom-call | flops 8800000000 | bytes 54400000 | tf_op jit(solution)/shard_map/part_product/pallas_call | solution.py:212
  177.6 4.2 %all-to-all-done.4 = bf16[16,64,128]{2,1,0:T(8,128)(2,1)S(1)} async-done(((bf16[16,64,128]{2,1,0:T(8,128)(2,1)}), bf16[16,64,128]{2,1,0:T(8,128)(2,1)S(1)}, u32[]{:S(2)}, u32[]{:S(2)}) %all-to-all-start.4) | async-done | bytes 262176 | tf_op jit(solution)/shard_map/all_to_all | solution.py:424
  182.9 2.6 collective-permute-start.16
  186.4 1.8 collective-permute-start.18
  189.0 5.8 %all-to-all-start.5 = ((bf16[16,64,128]{2,1,0:T(8,128)(2,1)}), bf16[16,64,128]{2,1,0:T(8,128)(2,1)S(1)}, u32[]{:S(2)}, u32[]{:S(2)}) async-start(bf16[16,64,128]{2,1,0:T(8,128)(2,1)} %broadcast_in_dim.22), calls=%async_computation.5 | async-start | bytes 524288 | tf_op jit(solution)/shard_map/all_to_all | solution.py:420
  194.8 9.7 %part_product.6 = bf16[1024,2048]{1,0:T(8,128)(2,1)} custom-call(s32[4]{0:T(128)} %pad_add_fusion.coords, bf16[8,1024,128]{2,1,0:T(8,128)(2,1)} %bitcast.62, bf16[8,1024,128]{2,1,0:T(8,128)(2,1)} %bitcast.63, bf16[8,1024,128]{2,1,0:T(8,128)(2,1)} %bitcast.64, bf16[8,1024,128]{2,1,0:T(8,128)(2,1)} %bitcast.65, bf16[8,1024,128]{2,1,0:T(8,128)(2,1)} %bitcast.66, ...), custom_call_target="tpu_custom_call" | custom-call | flops 6049999872 | bytes 37400000 | tf_op jit(solution)/shard_map/part_product/pallas_call | solution.py:212
  204.5 4.7 %add_terms.1 = (bf16[224,2048]{1,0:T(8,128)(2,1)}, bf16[224,2048]{1,0:T(8,128)(2,1)}, bf16[224,2048]{1,0:T(8,128)(2,1)}, bf16[224,2048]{1,0:T(8,128)(2,1)}) custom-call(bf16[224,2048]{1,0:T(8,128)(2,1)} %get-tuple-element.181.refs_0_, bf16[224,2048]{1,0:T(8,128)(2,1)} %get-tuple-element.182.refs_1_, bf16[224,2048]{1,0:T(8,128)(2,1)} %get-tuple-element.183.refs_2_, ...), custom_call_target="tpu_custom_call" | custom-call | flops 2750000128 | bytes 17000000 | tf_op jit(solution)/shard_map/add_terms/pallas_call | solution.py:282
  209.2 3.3 %all-to-all-done.5 = bf16[16,64,128]{2,1,0:T(8,128)(2,1)S(1)} async-done(((bf16[16,64,128]{2,1,0:T(8,128)(2,1)}), bf16[16,64,128]{2,1,0:T(8,128)(2,1)S(1)}, u32[]{:S(2)}, u32[]{:S(2)}) %all-to-all-start.5) | async-done | bytes 262176 | tf_op jit(solution)/shard_map/all_to_all | solution.py:420
  212.7 2.7 collective-permute-start.20
  216.2 1.8 collective-permute-start.22
  218.4 1.1 fusion.2
  220.6 6.1 %multiply_reduce_fusion = (f32[]{:T(128)}, f32[1024,1792]{1,0:T(8,128)}) fusion(f32[1024,1792]{1,0:T(8,128)S(1)} %fusion.2, f32[1792]{0:T(1024)S(1)} %broadcast_divide_fusion, bf16[1024,1792]{1,0:T(8,128)(2,1)S(1)} %copy-done.5, bf16[1792,128]{1,0:T(8,128)(2,1)S(1)} %copy-done.12, f32[1024,128]{1,0:T(8,128)S(1)} %fusion.8), kind=kOutput, calls=%fused_computation | convolution fusion | flops 480903168 | bytes 19340292 | tf_op jit(solution)/shard_map/dot_general | solution.py:413
  226.7 1.3 broadcast_in_dim_broadcast_in_dim_broadcast_in_dim.3
  228.0 5.0 %all-to-all-start.6 = ((f32[16,8,128]{2,1,0:T(8,128)}), f32[16,8,128]{2,1,0:T(8,128)S(1)}, u32[]{:S(2)}, u32[]{:S(2)}) async-start(f32[16,8,128]{2,1,0:T(8,128)} %broadcast_in_dim_broadcast_in_dim_broadcast_in_dim.3), calls=%async_computation.7 | async-start | bytes 131072 | tf_op jit(solution)/shard_map/all_to_all | solution.py:420
  233.0 9.9 %part_product.7 = (bf16[448,2048]{1,0:T(8,128)(2,1)}, bf16[448,2048]{1,0:T(8,128)(2,1)}) custom-call(s32[4]{0:T(128)} %pad_add_fusion.coords, bf16[3584,128]{1,0:T(8,128)(2,1)} %bitcast.72, bf16[3584,128]{1,0:T(8,128)(2,1)} %collective-permute-done.5.refs_1_, bf16[3584,128]{1,0:T(8,128)(2,1)} %copy-done.9, bf16[3584,128]{1,0:T(8,128)(2,1)} %copy-done.10, ...), custom_call_target="tpu_custom_call" | custom-call | flops 5500000256 | bytes 34000000 | tf_op jit(solution)/shard_map/part_product/pallas_call | solution.py:212
  243.4 7.1 %merge.1 = (f32[112,2048]{1,0:T(8,128)}, bf16[112,2048]{1,0:T(8,128)(2,1)}, bf16[112,2048]{1,0:T(8,128)(2,1)}, bf16[112,2048]{1,0:T(8,128)(2,1)}, f32[112,2048]{...) custom-call(bf16[448,2048]{1,0:T(8,128)(2,1)} %get-tuple-element.200.refs_0_, ...), custom_call_target="tpu_custom_call" | custom-call | flops 3849999872 | bytes 23800000 | tf_op jit(solution)/shard_map/merge/pallas_call | solution.py:312
  252.0 4.3 %all-to-all-start.7 = ((f32[8,8,128]{2,1,0:T(8,128)}), f32[8,8,128]{2,1,0:T(8,128)S(1)}, u32[]{:S(2)}, u32[]{:S(2)}) async-start(f32[8,8,128]{2,1,0:T(8,128)} %broadcast_in_dim.23), calls=%async_computation.8 | async-start | bytes 65536 | tf_op jit(solution)/shard_map/all_to_all | solution.py:420
  256.3 2.8 collective-permute-start.24
  259.1 1.1 collective-permute-start.25
  260.1 1.2 collective-permute-start.26
  261.3 2.4 collective-permute-start.27
  265.0 1.2 collective-permute-start.28
  266.2 10.5 %broadcast_multiply_fusion = f32[1024,1792]{1,0:T(8,128)} fusion(f32[]{:T(128)} %bitcast.22, f32[1024,1792]{1,0:T(8,128)} %get-tuple-element.232, f32[1024,1792]{1,0:T(8,128)} %copy-done.3, f32[1792]{0:T(1024)S(1)} %broadcast_divide_fusion, bf16[1024,1792]{1,0:T(8,128)(2,1)} %copy-done.4), kind=kLoop, calls=%fused_computation.3 | loop fusion | flops 9175040 | bytes 25697284 | tf_op jit(solution)/shard_map/mul | solution.py:549
  276.7 3.3 %collective-permute-done.25.refs_3_ = bf16[112,2048]{1,0:T(8,128)(2,1)S(1)} collective-permute-done((bf16[112,2048]{1,0:T(8,128)(2,1)}, bf16[112,2048]{1,0:T(8,128)(2,1)S(1)}, u32[]{:S(2)}, u32[]{:S(2)}) %collective-permute-start.25) | collective-permute-done | bytes 458784 | tf_op jit(solution)/shard_map/ppermute | solution.py:372
  280.0 2.8 collective-permute-done.27.refs_6_
  282.7 2.9 collective-permute-done.28.refs_7_
  286.4 3.6 %finish.1 = f32[224,2048]{1,0:T(8,128)} custom-call(f32[112,2048]{1,0:T(8,128)} %get-tuple-element.220.refs_0_, bf16[112,2048]{1,0:T(8,128)(2,1)} %copy-done.21, bf16[112,2048]{1,0:T(8,128)(2,1)} %copy-done.22, bf16[112,2048]{1,0:T(8,128)(2,1)} %copy-done.23, f32[112,2048]{1,0:T(8,128)} %get-tuple-element.224.refs_4_, bf16[112,2048]{1,0:T(8,128)(2,1)} %copy-done.24, ...), custom_call_target="tpu_custom_call" | custom-call | flops 2200000000 | bytes 13600000 | tf_op jit(solution)/shard_map/finish/pallas_call | solution.py:347
  290.0 4.9 %reduce-scatter.2.cloned.1.call-done = bf16[64,2048]{1,0:T(8,128)(2,1)} async-done(((bf16[1024,2048]{1,0:T(8,128)(2,1)}), bf16[64,2048]{1,0:T(8,128)(2,1)}) %reduce-scatter.2.cloned.1.call-update) | async-done | bytes 262160 | tf_op jit(solution)/shard_map/reduce_scatter | solution.py:529
  294.9 1.8 convert_element_type.73
  (112 shorter events, 16.6 us)
Async XLA Ops:
  7.2 113.0 %copy-start = (f32[128,128]{1,0:T(8,128)S(1)}, f32[128,128]{1,0:T(8,128)}, u32[]{:S(2)}) copy-start(f32[128,128]{1,0:T(8,128)} %param.25) | copy-start | bytes 196612
  7.8 9.0 %copy-start.15 = (bf16[64,128]{1,0:T(8,128)(2,1)S(1)}, bf16[64,128]{1,0:T(8,128)(2,1)}, u32[]{:S(2)}) copy-start(bf16[64,128]{1,0:T(8,128)(2,1)} %param.23) | copy-start | bytes 49156
  11.7 52.5 %collective-permute-start = (bf16[3584,128]{1,0:T(8,128)(2,1)}, bf16[3584,128]{1,0:T(8,128)(2,1)S(1)}, u32[]{:S(2)}, u32[]{:S(2)}) collective-permute-start(bf16[3584,128]{1,0:T(8,128)(2,1)} %bitcast.81), channel_id=1, source_target_pairs={{0,8},{1,9},{4,12},{5,13},{8,0},{9,1},{12,4},{13,5},{2,10},{3,11},... | collective-permute-start | bytes 2752520 | tf_op jit(solution)/shard_map/ppermute | solution.py:384
  16.2 48.1 %collective-permute-start.1 = (bf16[3584,128]{1,0:T(8,128)(2,1)}, bf16[3584,128]{1,0:T(8,128)(2,1)S(1)}, u32[]{:S(2)}, u32[]{:S(2)}) collective-permute-start(bf16[3584,128]{1,0:T(8,128)(2,1)} %bitcast.80), channel_id=1, source_target_pairs={{0,9},{1,8},{4,13},{5,12},{8,1},{9,0},{12,5},{13,4},{2,11},{3,10},... | collective-permute-start | bytes 2752520 | tf_op jit(solution)/shard_map/ppermute | solution.py:384
  17.5 42.8 %all-to-all-start = ((bf16[16,64,128]{2,1,0:T(8,128)(2,1)}), bf16[16,64,128]{2,1,0:T(8,128)(2,1)S(1)}, u32[]{:S(2)}, u32[]{:S(2)}) async-start(bf16[16,64,128]{2,1,0:T(8,128)(2,1)} %broadcast_in_dim.16), calls=%async_computation | async-start | bytes 524288 | tf_op jit(solution)/shard_map/all_to_all | solution.py:420
  25.2 111.7 %all-gather.3.cloned.1.call-start = ((), (), s32[]{:S(2)}) async-start(), calls=%async_computation.10 | async-start | bytes 4718592 | tf_op jit(solution)/shard_map/all_gather | solution.py:474
  47.3 7.7 %copy-start.17 = (f32[1024]{0:T(1024)S(1)}, f32[1024]{0:T(1024)}, u32[]{:S(2)}) copy-start(f32[1024]{0:T(1024)} %param.21) | copy-start | bytes 12292
  47.3 7.7 %copy-start.14 = (bf16[224,128]{1,0:T(8,128)(2,1)S(1)}, bf16[224,128]{1,0:T(8,128)(2,1)}, u32[]{:S(2)}) copy-start(bf16[224,128]{1,0:T(8,128)(2,1)} %param.24) | copy-start | bytes 172036
  60.5 8.9 %copy-start.16 = (f32[1792]{0:T(1024)S(1)}, f32[1792]{0:T(1024)}, u32[]{:S(2)}) copy-start(f32[1792]{0:T(1024)} %param.22) | copy-start | bytes 21508
  64.3 18.0 %copy-start.7 = (bf16[3584,128]{1,0:T(8,128)(2,1)}, bf16[3584,128]{1,0:T(8,128)(2,1)S(1)}, u32[]{:S(2)}) copy-start(bf16[3584,128]{1,0:T(8,128)(2,1)S(1)} %collective-permute-done.refs_4_) | copy-start | bytes 2752516
  64.3 18.0 %copy-start.8 = (bf16[3584,128]{1,0:T(8,128)(2,1)}, bf16[3584,128]{1,0:T(8,128)(2,1)S(1)}, u32[]{:S(2)}) copy-start(bf16[3584,128]{1,0:T(8,128)(2,1)S(1)} %collective-permute-done.1.refs_5_) | copy-start | bytes 2752516
  64.3 19.0 %all-to-all-start.1 = ((bf16[8,32,1792]{2,1,0:T(8,128)(2,1)}), bf16[8,32,1792]{2,1,0:T(8,128)(2,1)}, u32[]{:S(2)}, u32[]{:S(2)}) async-start(bf16[8,32,1792]{2,1,0:T(8,128)(2,1)} %pad_maximum_fusion.1), calls=%async_computation.1 | async-start | bytes 1835008 | tf_op jit(solution)/shard_map/all_to_all | solution.py:476
  69.4 35.5 %collective-permute-start.2 = (bf16[3584,128]{1,0:T(8,128)(2,1)}, bf16[3584,128]{1,0:T(8,128)(2,1)S(1)}, u32[]{:S(2)}, u32[]{:S(2)}) collective-permute-start(bf16[3584,128]{1,0:T(8,128)(2,1)} %bitcast.79), channel_id=1, source_target_pairs={{0,4},{1,5},{4,8},{5,9},{8,12},{9,13},{12,0},{13,1},{2,6},{3,7},{6... | collective-permute-start | bytes 2752520 | tf_op jit(solution)/shard_map/ppermute | solution.py:384
  70.0 36.2 %collective-permute-start.3 = (bf16[3584,128]{1,0:T(8,128)(2,1)}, bf16[3584,128]{1,0:T(8,128)(2,1)}, u32[]{:S(2)}, u32[]{:S(2)}) collective-permute-start(bf16[3584,128]{1,0:T(8,128)(2,1)} %bitcast.78), channel_id=1, source_target_pairs={{0,12},{1,13},{4,0},{5,1},{8,4},{9,5},{12,8},{13,9},{2,14},{3,15},... | collective-permute-start | bytes 2752520 | tf_op jit(solution)/shard_map/ppermute | solution.py:384
  72.1 21.7 %collective-permute-start.4 = (bf16[128,2048]{1,0:T(8,128)(2,1)}, bf16[128,2048]{1,0:T(8,128)(2,1)}, u32[]{:S(2)}, u32[]{:S(2)}) collective-permute-start(bf16[128,2048]{1,0:T(8,128)(2,1)} %sketch.3.refs_8_), channel_id=1, source_target_pairs={{0,2},{16,18},{2,0},{18,16},{1,3},{17,19},{3,1},{19,17},{4,6},{20,... | collective-permute-start | bytes 1572872 | tf_op jit(solution)/shard_map/ppermute | solution.py:372
  74.8 31.4 %collective-permute-start.5 = (bf16[3584,128]{1,0:T(8,128)(2,1)}, bf16[3584,128]{1,0:T(8,128)(2,1)}, u32[]{:S(2)}, u32[]{:S(2)}) collective-permute-start(bf16[3584,128]{1,0:T(8,128)(2,1)} %bitcast.77), channel_id=1, source_target_pairs={{0,1},{1,0},{4,5},{5,4},{8,9},{9,8},{12,13},{13,12},{2,3},{3,2},{6... | collective-permute-start | bytes 2752520 | tf_op jit(solution)/shard_map/ppermute | solution.py:384
  85.4 31.0 %all-to-all-start.2 = ((bf16[8,16,1792]{2,1,0:T(8,128)(2,1)}), bf16[8,16,1792]{2,1,0:T(8,128)(2,1)}, u32[]{:S(2)}, u32[]{:S(2)}) async-start(bf16[8,16,1792]{2,1,0:T(8,128)(2,1)} %broadcast_in_dim.21), calls=%async_computation.2 | async-start | bytes 917504 | tf_op jit(solution)/shard_map/all_to_all | solution.py:420
  104.9 11.5 %copy-start.9 = (bf16[3584,128]{1,0:T(8,128)(2,1)}, bf16[3584,128]{1,0:T(8,128)(2,1)S(1)}, u32[]{:S(2)}) copy-start(bf16[3584,128]{1,0:T(8,128)(2,1)S(1)} %collective-permute-done.2.refs_2_) | copy-start | bytes 2752516
  106.2 22.9 %collective-permute-start.8 = (bf16[128,2048]{1,0:T(8,128)(2,1)}, bf16[128,2048]{1,0:T(8,128)(2,1)}, u32[]{:S(2)}, u32[]{:S(2)}) collective-permute-start(bf16[128,2048]{1,0:T(8,128)(2,1)} %sketch.3.refs_8_), channel_id=1, source_target_pairs={{0,16},{16,2},{2,18},{18,0},{1,17},{17,3},{3,19},{19,1},{4,20},{20... | collective-permute-start | bytes 1572872 | tf_op jit(solution)/shard_map/ppermute | solution.py:372
  107.0 22.0 %collective-permute-start.9 = (bf16[128,2048]{1,0:T(8,128)(2,1)}, bf16[128,2048]{1,0:T(8,128)(2,1)}, u32[]{:S(2)}, u32[]{:S(2)}) collective-permute-start(bf16[128,2048]{1,0:T(8,128)(2,1)} %sketch.3.refs_8_), channel_id=1, source_target_pairs={{0,18},{16,0},{2,16},{18,2},{1,19},{17,1},{3,17},{19,3},{4,22},{20... | collective-permute-start | bytes 1572872 | tf_op jit(solution)/shard_map/ppermute | solution.py:372
  108.8 28.0 %collective-permute-start.6 = (bf16[3584,128]{1,0:T(8,128)(2,1)}, bf16[3584,128]{1,0:T(8,128)(2,1)S(1)}, u32[]{:S(2)}, u32[]{:S(2)}) collective-permute-start(bf16[3584,128]{1,0:T(8,128)(2,1)} %bitcast.76), channel_id=1, source_target_pairs={{0,5},{1,4},{4,9},{5,8},{8,13},{9,12},{12,1},{13,0},{2,7},{3,6},{6... | collective-permute-start | bytes 2752520 | tf_op jit(solution)/shard_map/ppermute | solution.py:384
  114.1 22.8 %collective-permute-start.7 = (bf16[3584,128]{1,0:T(8,128)(2,1)}, bf16[3584,128]{1,0:T(8,128)(2,1)}, u32[]{:S(2)}, u32[]{:S(2)}) collective-permute-start(bf16[3584,128]{1,0:T(8,128)(2,1)} %bitcast.75), channel_id=1, source_target_pairs={{0,13},{1,12},{4,1},{5,0},{8,5},{9,4},{12,9},{13,8},{2,15},{3,14},... | collective-permute-start | bytes 2752520 | tf_op jit(solution)/shard_map/ppermute | solution.py:384
  116.4 33.7 %all-to-all-start.3 = ((bf16[8,16,64,128]{3,2,1,0:T(8,128)(2,1)}), bf16[8,16,64,128]{3,2,1,0:T(8,128)(2,1)S(1)}, u32[]{:S(2)}, u32[]{:S(2)}) async-start(bf16[8,16,64,128]{3,2,1,0:T(8,128)(2,1)} %turn_act.1), calls=%async_computation.3 | async-start | bytes 4194304 | tf_op jit(solution)/shard_map/all_to_all | solution.py:497
  121.8 2.0 copy-start.6
  123.8 3.3 %copy-start.11 = (bf16[1792,128]{1,0:T(8,128)(2,1)S(1)}, bf16[1792,128]{1,0:T(8,128)(2,1)}, u32[]{:S(2)}) copy-start(bf16[1792,128]{1,0:T(8,128)(2,1)} %multiply_convert_fusion) | copy-start | bytes 1376260
  125.4 1.8 copy-start.4
  136.8 3.4 %copy-start.10 = (bf16[3584,128]{1,0:T(8,128)(2,1)}, bf16[3584,128]{1,0:T(8,128)(2,1)S(1)}, u32[]{:S(2)}) copy-start(bf16[3584,128]{1,0:T(8,128)(2,1)S(1)} %collective-permute-done.6.refs_3_) | copy-start | bytes 2752516
  150.1 27.5 %copy-start.2 = (bf16[8,16,64,128]{3,2,1,0:T(8,128)(2,1)}, bf16[8,16,64,128]{3,2,1,0:T(8,128)(2,1)S(1)}, u32[]{:S(2)}) copy-start(bf16[8,16,64,128]{3,2,1,0:T(8,128)(2,1)S(1)} %all-to-all-done.3) | copy-start | bytes 6291460
  150.1 31.8 %collective-permute-start.14 = (bf16[512,2048]{1,0:T(8,128)(2,1)}, bf16[512,2048]{1,0:T(8,128)(2,1)}, u32[]{:S(2)}, u32[]{:S(2)}) collective-permute-start(bf16[512,2048]{1,0:T(8,128)(2,1)} %pad_maximum_fusion), channel_id=1, source_target_pairs={{0,1},{1,0},{2,3},{3,2},{4,5},{5,4},{6,7},{7,6},{8,9},{9,8},{10,11... | collective-permute-start | bytes 6291464 | tf_op jit(solution)/shard_map/ppermute | solution.py:379
  150.2 31.7 %collective-permute-start.10 = (bf16[224,2048]{1,0:T(8,128)(2,1)}, bf16[224,2048]{1,0:T(8,128)(2,1)S(1)}, u32[]{:S(2)}, u32[]{:S(2)}) collective-permute-start(bf16[224,2048]{1,0:T(8,128)(2,1)} %get-tuple-element.161), channel_id=1, source_target_pairs={{0,32},{32,64},{64,96},{96,0},{1,33},{33,65},{65,97},{97,1},{2,34}... | collective-permute-start | bytes 2752520 | tf_op jit(solution)/shard_map/ppermute | solution.py:375
  152.1 29.8 %collective-permute-start.11 = (bf16[224,2048]{1,0:T(8,128)(2,1)}, bf16[224,2048]{1,0:T(8,128)(2,1)}, u32[]{:S(2)}, u32[]{:S(2)}) collective-permute-start(bf16[224,2048]{1,0:T(8,128)(2,1)} %get-tuple-element.162), channel_id=1, source_target_pairs={{0,96},{32,0},{64,32},{96,64},{1,97},{33,1},{65,33},{97,65},{2,98}... | collective-permute-start | bytes 2752520 | tf_op jit(solution)/shard_map/ppermute | solution.py:375
  153.3 28.6 %collective-permute-start.12 = (bf16[224,2048]{1,0:T(8,128)(2,1)}, bf16[224,2048]{1,0:T(8,128)(2,1)}, u32[]{:S(2)}, u32[]{:S(2)}) collective-permute-start(bf16[224,2048]{1,0:T(8,128)(2,1)} %get-tuple-element.163), channel_id=1, source_target_pairs={{0,16},{16,2},{2,18},{18,0},{1,17},{17,3},{3,19},{19,1},{4,20},{20... | collective-permute-start | bytes 2752520 | tf_op jit(solution)/shard_map/ppermute | solution.py:372
  153.5 28.4 %collective-permute-start.13 = (bf16[224,2048]{1,0:T(8,128)(2,1)}, bf16[224,2048]{1,0:T(8,128)(2,1)}, u32[]{:S(2)}, u32[]{:S(2)}) collective-permute-start(bf16[224,2048]{1,0:T(8,128)(2,1)} %get-tuple-element.164), channel_id=1, source_target_pairs={{0,18},{16,0},{2,16},{18,2},{1,19},{17,1},{3,17},{19,3},{4,22},{20... | collective-permute-start | bytes 2752520 | tf_op jit(solution)/shard_map/ppermute | solution.py:372
  156.0 25.9 %all-to-all-start.4 = ((bf16[16,64,128]{2,1,0:T(8,128)(2,1)}), bf16[16,64,128]{2,1,0:T(8,128)(2,1)S(1)}, u32[]{:S(2)}, u32[]{:S(2)}) async-start(bf16[16,64,128]{2,1,0:T(8,128)(2,1)} %bitcast.20), calls=%async_computation.4 | async-start | bytes 524288 | tf_op jit(solution)/shard_map/all_to_all | solution.py:424
  182.8 29.7 %collective-permute-start.15 = (bf16[224,2048]{1,0:T(8,128)(2,1)}, bf16[224,2048]{1,0:T(8,128)(2,1)S(1)}, u32[]{:S(2)}, u32[]{:S(2)}) collective-permute-start(bf16[224,2048]{1,0:T(8,128)(2,1)} %get-tuple-element.177), channel_id=1, source_target_pairs={{0,32},{32,64},{64,96},{96,0},{1,33},{33,65},{65,97},{97,1},{2,34}... | collective-permute-start | bytes 2752520 | tf_op jit(solution)/shard_map/ppermute | solution.py:375
  182.9 29.7 %collective-permute-start.16 = (bf16[224,2048]{1,0:T(8,128)(2,1)}, bf16[224,2048]{1,0:T(8,128)(2,1)S(1)}, u32[]{:S(2)}, u32[]{:S(2)}) collective-permute-start(bf16[224,2048]{1,0:T(8,128)(2,1)} %get-tuple-element.178), channel_id=1, source_target_pairs={{0,96},{32,0},{64,32},{96,64},{1,97},{33,1},{65,33},{97,65},{2,98}... | collective-permute-start | bytes 2752520 | tf_op jit(solution)/shard_map/ppermute | solution.py:375
  185.5 27.1 %collective-permute-start.17 = (bf16[224,2048]{1,0:T(8,128)(2,1)}, bf16[224,2048]{1,0:T(8,128)(2,1)}, u32[]{:S(2)}, u32[]{:S(2)}) collective-permute-start(bf16[224,2048]{1,0:T(8,128)(2,1)} %get-tuple-element.179), channel_id=1, source_target_pairs={{0,16},{16,2},{2,18},{18,0},{1,17},{17,3},{3,19},{19,1},{4,20},{20... | collective-permute-start | bytes 2752520 | tf_op jit(solution)/shard_map/ppermute | solution.py:372
  186.4 26.2 %collective-permute-start.18 = (bf16[224,2048]{1,0:T(8,128)(2,1)}, bf16[224,2048]{1,0:T(8,128)(2,1)}, u32[]{:S(2)}, u32[]{:S(2)}) collective-permute-start(bf16[224,2048]{1,0:T(8,128)(2,1)} %get-tuple-element.180), channel_id=1, source_target_pairs={{0,18},{16,0},{2,16},{18,2},{1,19},{17,1},{3,17},{19,3},{4,22},{20... | collective-permute-start | bytes 2752520 | tf_op jit(solution)/shard_map/ppermute | solution.py:372
  189.0 23.6 %all-to-all-start.5 = ((bf16[16,64,128]{2,1,0:T(8,128)(2,1)}), bf16[16,64,128]{2,1,0:T(8,128)(2,1)S(1)}, u32[]{:S(2)}, u32[]{:S(2)}) async-start(bf16[16,64,128]{2,1,0:T(8,128)(2,1)} %broadcast_in_dim.22), calls=%async_computation.5 | async-start | bytes 524288 | tf_op jit(solution)/shard_map/all_to_all | solution.py:420
  194.8 100.1 %reduce-scatter.2.cloned.1.call-start = ((), (), s32[]{:S(2)}) async-start(), calls=%async_computation.9 | async-start | bytes 4456448 | tf_op jit(solution)/shard_map/reduce_scatter | solution.py:529
  209.2 8.8 %copy-start.13 = (f32[128,128]{1,0:T(8,128)S(1)}, f32[128,128]{1,0:T(8,128)}, u32[]{:S(2)}) copy-start(f32[128,128]{1,0:T(8,128)} %param.26) | copy-start | bytes 196612
  209.2 9.2 %copy-start.12 = (bf16[1792,128]{1,0:T(8,128)(2,1)S(1)}, bf16[1792,128]{1,0:T(8,128)(2,1)}, u32[]{:S(2)}) copy-start(bf16[1792,128]{1,0:T(8,128)(2,1)} %multiply_convert_fusion) | copy-start | bytes 1376260
  212.6 7.0 %copy-start.18 = (bf16[224,2048]{1,0:T(8,128)(2,1)}, bf16[224,2048]{1,0:T(8,128)(2,1)S(1)}, u32[]{:S(2)}) copy-start(bf16[224,2048]{1,0:T(8,128)(2,1)S(1)} %collective-permute-done.15.refs_2_) | copy-start | bytes 2752516
  212.6 7.0 %copy-start.19 = (bf16[224,2048]{1,0:T(8,128)(2,1)}, bf16[224,2048]{1,0:T(8,128)(2,1)S(1)}, u32[]{:S(2)}) copy-start(bf16[224,2048]{1,0:T(8,128)(2,1)S(1)} %collective-permute-done.16.refs_3_) | copy-start | bytes 2752516
  212.6 30.8 %collective-permute-start.19 = (bf16[224,2048]{1,0:T(8,128)(2,1)}, bf16[224,2048]{1,0:T(8,128)(2,1)}, u32[]{:S(2)}, u32[]{:S(2)}) collective-permute-start(bf16[224,2048]{1,0:T(8,128)(2,1)} %get-tuple-element.201), channel_id=1, source_target_pairs={{0,32},{32,64},{64,96},{96,0},{1,33},{33,65},{65,97},{97,1},{2,34}... | collective-permute-start | bytes 2752520 | tf_op jit(solution)/shard_map/ppermute | solution.py:375
  212.7 30.7 %collective-permute-start.20 = (bf16[224,2048]{1,0:T(8,128)(2,1)}, bf16[224,2048]{1,0:T(8,128)(2,1)}, u32[]{:S(2)}, u32[]{:S(2)}) collective-permute-start(bf16[224,2048]{1,0:T(8,128)(2,1)} %get-tuple-element.204), channel_id=1, source_target_pairs={{0,96},{32,0},{64,32},{96,64},{1,97},{33,1},{65,33},{97,65},{2,98}... | collective-permute-start | bytes 2752520 | tf_op jit(solution)/shard_map/ppermute | solution.py:375
  215.4 28.1 %collective-permute-start.21 = (bf16[224,2048]{1,0:T(8,128)(2,1)}, bf16[224,2048]{1,0:T(8,128)(2,1)}, u32[]{:S(2)}, u32[]{:S(2)}) collective-permute-start(bf16[224,2048]{1,0:T(8,128)(2,1)} %get-tuple-element.206), channel_id=1, source_target_pairs={{0,16},{16,2},{2,18},{18,0},{1,17},{17,3},{3,19},{19,1},{4,20},{20... | collective-permute-start | bytes 2752520 | tf_op jit(solution)/shard_map/ppermute | solution.py:372
  216.2 27.2 %collective-permute-start.22 = (bf16[224,2048]{1,0:T(8,128)(2,1)}, bf16[224,2048]{1,0:T(8,128)(2,1)}, u32[]{:S(2)}, u32[]{:S(2)}) collective-permute-start(bf16[224,2048]{1,0:T(8,128)(2,1)} %get-tuple-element.209), channel_id=1, source_target_pairs={{0,18},{16,0},{2,16},{18,2},{1,19},{17,1},{3,17},{19,3},{4,22},{20... | collective-permute-start | bytes 2752520 | tf_op jit(solution)/shard_map/ppermute | solution.py:372
  218.4 2.2 copy-start.5
  220.6 6.1 %copy-start.3 = (f32[1024,1792]{1,0:T(8,128)}, f32[1024,1792]{1,0:T(8,128)S(1)}, u32[]{:S(2)}) copy-start(f32[1024,1792]{1,0:T(8,128)S(1)} %fusion.2) | copy-start | bytes 22020100
  228.0 14.9 %all-to-all-start.6 = ((f32[16,8,128]{2,1,0:T(8,128)}), f32[16,8,128]{2,1,0:T(8,128)S(1)}, u32[]{:S(2)}, u32[]{:S(2)}) async-start(f32[16,8,128]{2,1,0:T(8,128)} %broadcast_in_dim_broadcast_in_dim_broadcast_in_dim.3), calls=%async_computation.7 | async-start | bytes 131072 | tf_op jit(solution)/shard_map/all_to_all | solution.py:420
  250.5 14.4 %collective-permute-start.23 = (bf16[112,2048]{1,0:T(8,128)(2,1)}, bf16[112,2048]{1,0:T(8,128)(2,1)S(1)}, u32[]{:S(2)}, u32[]{:S(2)}) collective-permute-start(bf16[112,2048]{1,0:T(8,128)(2,1)} %get-tuple-element.221), channel_id=1, source_target_pairs={{0,16},{16,2},{2,18},{18,0},{1,17},{17,3},{3,19},{19,1},{4,20},{20... | collective-permute-start | bytes 1376264 | tf_op jit(solution)/shard_map/ppermute | solution.py:372
  252.0 11.7 %all-to-all-start.7 = ((f32[8,8,128]{2,1,0:T(8,128)}), f32[8,8,128]{2,1,0:T(8,128)S(1)}, u32[]{:S(2)}, u32[]{:S(2)}) async-start(f32[8,8,128]{2,1,0:T(8,128)} %broadcast_in_dim.23), calls=%async_computation.8 | async-start | bytes 65536 | tf_op jit(solution)/shard_map/all_to_all | solution.py:420
  256.3 20.4 %collective-permute-start.24 = (bf16[112,2048]{1,0:T(8,128)(2,1)}, bf16[112,2048]{1,0:T(8,128)(2,1)S(1)}, u32[]{:S(2)}, u32[]{:S(2)}) collective-permute-start(bf16[112,2048]{1,0:T(8,128)(2,1)} %get-tuple-element.222), channel_id=1, source_target_pairs={{0,2},{16,18},{2,0},{18,16},{1,3},{17,19},{3,1},{19,17},{4,6},{20,... | collective-permute-start | bytes 1376264 | tf_op jit(solution)/shard_map/ppermute | solution.py:372
  259.1 20.9 %collective-permute-start.25 = (bf16[112,2048]{1,0:T(8,128)(2,1)}, bf16[112,2048]{1,0:T(8,128)(2,1)S(1)}, u32[]{:S(2)}, u32[]{:S(2)}) collective-permute-start(bf16[112,2048]{1,0:T(8,128)(2,1)} %get-tuple-element.223), channel_id=1, source_target_pairs={{0,18},{16,0},{2,16},{18,2},{1,19},{17,1},{3,17},{19,3},{4,22},{20... | collective-permute-start | bytes 1376264 | tf_op jit(solution)/shard_map/ppermute | solution.py:372
  260.1 19.8 %collective-permute-start.26 = (bf16[112,2048]{1,0:T(8,128)(2,1)}, bf16[112,2048]{1,0:T(8,128)(2,1)S(1)}, u32[]{:S(2)}, u32[]{:S(2)}) collective-permute-start(bf16[112,2048]{1,0:T(8,128)(2,1)} %get-tuple-element.225), channel_id=1, source_target_pairs={{0,32},{32,64},{64,96},{96,0},{1,33},{33,65},{65,97},{97,1},{2,34}... | collective-permute-start | bytes 1376264 | tf_op jit(solution)/shard_map/ppermute | solution.py:375
  261.3 21.4 %collective-permute-start.27 = (bf16[112,2048]{1,0:T(8,128)(2,1)}, bf16[112,2048]{1,0:T(8,128)(2,1)S(1)}, u32[]{:S(2)}, u32[]{:S(2)}) collective-permute-start(bf16[112,2048]{1,0:T(8,128)(2,1)} %get-tuple-element.226), channel_id=1, source_target_pairs={{0,64},{32,96},{64,0},{96,32},{1,65},{33,97},{65,1},{97,33},{2,66}... | collective-permute-start | bytes 1376264 | tf_op jit(solution)/shard_map/ppermute | solution.py:375
  264.9 11.7 %copy-start.21 = (bf16[112,2048]{1,0:T(8,128)(2,1)}, bf16[112,2048]{1,0:T(8,128)(2,1)S(1)}, u32[]{:S(2)}) copy-start(bf16[112,2048]{1,0:T(8,128)(2,1)S(1)} %collective-permute-done.23.refs_1_) | copy-start | bytes 1376260
  265.0 20.6 %collective-permute-start.28 = (bf16[112,2048]{1,0:T(8,128)(2,1)}, bf16[112,2048]{1,0:T(8,128)(2,1)S(1)}, u32[]{:S(2)}, u32[]{:S(2)}) collective-permute-start(bf16[112,2048]{1,0:T(8,128)(2,1)} %get-tuple-element.227), channel_id=1, source_target_pairs={{0,96},{32,0},{64,32},{96,64},{1,97},{33,1},{65,33},{97,65},{2,98}... | collective-permute-start | bytes 1376264 | tf_op jit(solution)/shard_map/ppermute | solution.py:375
  266.2 30.5 %copy-start.1 = (f32[128,128]{1,0:T(8,128)S(1)}, f32[128,128]{1,0:T(8,128)}, u32[]{:S(2)}) copy-start(f32[128,128]{1,0:T(8,128)} %param.25) | copy-start | bytes 196612
  276.7 8.9 %copy-start.22 = (bf16[112,2048]{1,0:T(8,128)(2,1)}, bf16[112,2048]{1,0:T(8,128)(2,1)S(1)}, u32[]{:S(2)}) copy-start(bf16[112,2048]{1,0:T(8,128)(2,1)S(1)} %collective-permute-done.24.refs_2_) | copy-start | bytes 1376260
  280.0 5.6 %copy-start.23 = (bf16[112,2048]{1,0:T(8,128)(2,1)}, bf16[112,2048]{1,0:T(8,128)(2,1)S(1)}, u32[]{:S(2)}) copy-start(bf16[112,2048]{1,0:T(8,128)(2,1)S(1)} %collective-permute-done.25.refs_3_) | copy-start | bytes 1376260
  280.0 5.6 %copy-start.24 = (bf16[112,2048]{1,0:T(8,128)(2,1)}, bf16[112,2048]{1,0:T(8,128)(2,1)S(1)}, u32[]{:S(2)}) copy-start(bf16[112,2048]{1,0:T(8,128)(2,1)S(1)} %collective-permute-done.26.refs_5_) | copy-start | bytes 1376260
  282.7 2.9 copy-start.25
  (2 other events, 1.7 us)
Sparse Core Ops, SparseCore 0:
  64.4 47.4 all-gather.2
  212.7 82.0 reduce-scatter.1

commit v3 on v2

--- a/solution.py
+++ b/solution.py
@@ -523,10 +523,10 @@
     held = add_terms(held, via)
     right_sum = share(right_sum, GROUP, n_group).reshape(rows, rank)
     partial = part_act(coords, rows_y, keys_y, keys_sib, token_scale)
+    factor_act = lax.psum_scatter(partial, ("x", "z"), scatter_dimension=0, tiled=True).astype(F32)
     (got_free, held, right_sum, partial, left, keys_z) = phase(
         got_free, held, right_sum, partial, left, keys_z
     )
-    factor_act = lax.psum_scatter(partial, ("x", "z"), scatter_dimension=0, tiled=True).astype(F32)
 
     got_held = [shift(h, *way) for h, way in zip(held, ways)]
     right_core = jnp.dot(right_sum.astype(F32), core_grad, precision=lax.Precision.HIGHEST)

time: 305 us -> 316 us (1.036)
  waiting for transfers between devices: 51.6 us -> 61.3 us
    ppermute x7, waiting for transfers between devices: 20.2 us -> 33.2 us  [send(): return lax.ppermute(array, ALONG_Z, pairs)]
    all_to_all x5, starting transfers between devices: 26.9 us -> 32.5 us  [share(): return lax.all_to_all(copies, axes, 0, 0, tiled=True)]
    ppermute x7, starting transfers between devices: 16.8 us -> 11.5 us  [send(): return lax.ppermute(array, ALONG_Z, pairs)]
    reduce_scatter x1, waiting for transfers between devices: 4.92 us -> 0.01 us  [local(): lax.psum_scatter(partial, ('x', 'z'), scatter_dimension=0, tiled=True)]
    all_to_all x5, waiting for transfers between devices: 8.49 us -> 13.1 us  [share(): return lax.all_to_all(copies, axes, 0, 0, tiled=True)]
  transfers between devices with their start and end apart: 39 -> 39, of which waited for: 14 -> 10; matrix products, arithmetic and copies ran while one was open for 13% -> 12% of each run, Pallas kernels for 32% -> 28%
where the time goes in v3:
time: 316 us; the launch traced here: 312 us
  Pallas kernels  100 us (32%)
  starting transfers between devices  90.1 us (29%)
  waiting for transfers between devices  61.3 us (19%)
  other arithmetic  19.9 us (6%)
  matrix products  16.3 us (5%)
  between operations  15.2 us (5%)
  local copies, waits for them, and re-layouts  9.42 us (3%)
    pallas_call x4, Pallas kernels, part_product(): pl.pallas_call(functools.partial(part_kernel, scale, split), grid_spec=pl...  45.3 us
    ppermute x7, waiting for transfers between devices, send(): return lax.ppermute(array, ALONG_Z, pairs)  33.2 us
    all_to_all x5, starting transfers between devices, share(): return lax.all_to_all(copies, axes, 0, 0, tiled=True)  32.5 us
    pallas_call x2, Pallas kernels, sketch(): pl.pallas_call(sketch_kernel, grid_spec=pltpu.PrefetchScalarGridSpec(num_...  21.4 us
    ppermute x12, starting transfers between devices, shift(): lax.ppermute(array, RING_Y, [(spot(y), spot((y + step) % 4)) for y in ran...  16.9 us
    ppermute x9, starting transfers between devices, shift(): return lax.ppermute(array, axis, [(i, (i + step) % 4) for i in range(4)])  13.2 us
    all_to_all x5, waiting for transfers between devices, share(): return lax.all_to_all(copies, axes, 0, 0, tiled=True)  13.1 us
    pallas_call x2, Pallas kernels, turn(): pl.pallas_call(functools.partial(turn_kernel, shifts), grid_spec=pltpu.Pr...  12.3 us
  transfers between devices with their start and end apart: 39, of which 10 were waited for; matrix products, arithmetic and copies ran while one was open for 12% of the time, Pallas kernels for 28%

profile of v3, /device:TPU:1, one launch (start us, length us, event | category | flops | bytes accessed | tf_op | source)
XLA Modules:
  0.0 312.4 jit_solution(1700305759407683615)
XLA Ops:
  7.8 3.9 %turn.2 = (bf16[32,112,128]{2,1,0:T(8,128)(2,1)}, bf16[32,112,128]{2,1,0:T(8,128)(2,1)}) custom-call(s32[4]{0:T(128)} %pad_add_fusion.coords, bf16[128,28672]{1,0:T(8,128)(2,1)} %x_ref.2), custom_call_target="tpu_custom_call" | custom-call | flops 3300000000 | bytes 20400000 | tf_op jit(solution)/shard_map/turn/pallas_call | solution.py:137
  12.5 9.5 %all-to-all-start = ((bf16[16,64,128]{2,1,0:T(8,128)(2,1)}), bf16[16,64,128]{2,1,0:T(8,128)(2,1)S(1)}, u32[]{:S(2)}, u32[]{:S(2)}) async-start(bf16[16,64,128]{2,1,0:T(8,128)(2,1)} %broadcast_in_dim.16), calls=%async_computation | async-start | bytes 524288 | tf_op jit(solution)/shard_map/all_to_all | solution.py:420
  22.0 3.0 collective-permute-start
  25.3 8.3 %turn.3 = (bf16[32,112,128]{2,1,0:T(8,128)(2,1)}, bf16[32,112,128]{2,1,0:T(8,128)(2,1)}, bf16[32,112,128]{2,1,0:T(8,128)(2,1)}, bf16[32,112,128]{2,1,0:T(8,128)(...) custom-call(s32[4]{0:T(128)} %pad_add_fusion.coords, bf16[128,28672]{1,0:T(8,128)(2,1)} %x_ref.2), custom_call_target="tpu_custom_call" | custom-call | flops 3300000000 | bytes 20400000 | tf_op jit(solution)/shard_map/turn/pallas_call | solution.py:137
  33.7 13.7 %sketch.2 = bf16[128,2048]{1,0:T(8,128)(2,1)} custom-call(s32[2048]{0:T(1024)} %picks, bf16[128,28672]{1,0:T(8,128)(2,1)} %x_ref.2, s32[1,28672]{1,0:T(1,128)} %bitcast.82, bf16[256,256]{1,0:T(8,128)(2,1)} %constant.41.clone.table_ref), custom_call_target="tpu_custom_call" | custom-call | flops 7150000128 | bytes 44200000 | tf_op jit(solution)/shard_map/sketch/pallas_call | solution.py:78
  47.4 7.7 %sketch.3.refs_8_ = bf16[128,2048]{1,0:T(8,128)(2,1)} custom-call(s32[2048]{0:T(1024)} %picks.1, bf16[128,8192]{1,0:T(8,128)(2,1)} %act_ref, s32[1,8192]{1,0:T(1,128)} %bitcast.83, bf16[256,256]{1,0:T(8,128)(2,1)} %constant.41.clone.table_ref), custom_call_target="tpu_custom_call" | custom-call | flops 2750000128 | bytes 17000000 | tf_op jit(solution)/shard_map/sketch/pallas_call | solution.py:78
  55.4 2.7 convolution_convert_fusion
  58.2 1.0 pad_maximum_fusion.1
  59.2 8.9 %collective-permute-done.1.refs_5_ = bf16[3584,128]{1,0:T(8,128)(2,1)S(1)} collective-permute-done((bf16[3584,128]{1,0:T(8,128)(2,1)}, bf16[3584,128]{1,0:T(8,128)(2,1)S(1)}, u32[]{:S(2)}, u32[]{:S(2)}) %collective-permute-start.1) | collective-permute-done | bytes 917536 | tf_op jit(solution)/shard_map/ppermute | solution.py:384
  68.2 4.2 %all-to-all-start.1 = ((bf16[8,32,1792]{2,1,0:T(8,128)(2,1)}), bf16[8,32,1792]{2,1,0:T(8,128)(2,1)}, u32[]{:S(2)}, u32[]{:S(2)}) async-start(bf16[8,32,1792]{2,1,0:T(8,128)(2,1)} %pad_maximum_fusion.1), calls=%async_computation.1 | async-start | bytes 1835008 | tf_op jit(solution)/shard_map/all_to_all | solution.py:476
  72.4 3.4 %collective-permute-start.4 = (bf16[128,2048]{1,0:T(8,128)(2,1)}, bf16[128,2048]{1,0:T(8,128)(2,1)}, u32[]{:S(2)}, u32[]{:S(2)}) collective-permute-start(bf16[128,2048]{1,0:T(8,128)(2,1)} %sketch.3.refs_8_), channel_id=1, source_target_pairs={{0,2},{16,18},{2,0},{18,16},{1,3},{17,19},{3,1},{19,17},{4,6},{20,... | collective-permute-start | bytes 1572872 | tf_op jit(solution)/shard_map/ppermute | solution.py:372
  76.0 2.5 collective-permute-start.3
  78.5 1.5 collective-permute-start.5
  80.0 6.0 %turn_act.1 = bf16[8,16,64,128]{3,2,1,0:T(8,128)(2,1)} custom-call(bf16[128,8192]{1,0:T(8,128)(2,1)} %act_ref), custom_call_target="tpu_custom_call" | custom-call | flops 3300000000 | bytes 20400000 | tf_op jit(solution)/shard_map/turn_act/pallas_call | solution.py:170
  86.5 1.3 slice_convert_fusion
  88.7 4.3 %all-to-all-start.2 = ((bf16[8,16,1792]{2,1,0:T(8,128)(2,1)}), bf16[8,16,1792]{2,1,0:T(8,128)(2,1)}, u32[]{:S(2)}, u32[]{:S(2)}) async-start(bf16[8,16,1792]{2,1,0:T(8,128)(2,1)} %broadcast_in_dim.21), calls=%async_computation.2 | async-start | bytes 917504 | tf_op jit(solution)/shard_map/all_to_all | solution.py:420
  92.9 1.1 multiply_convert_fusion
  94.0 3.5 %collective-permute-done.4.refs_10_ = bf16[128,2048]{1,0:T(8,128)(2,1)} collective-permute-done((bf16[128,2048]{1,0:T(8,128)(2,1)}, bf16[128,2048]{1,0:T(8,128)(2,1)}, u32[]{:S(2)}, u32[]{:S(2)}) %collective-permute-start.4) | collective-permute-done | bytes 524320 | tf_op jit(solution)/shard_map/ppermute | solution.py:372
  97.5 17.4 %collective-permute-done.2.refs_2_ = bf16[3584,128]{1,0:T(8,128)(2,1)S(1)} collective-permute-done((bf16[3584,128]{1,0:T(8,128)(2,1)}, bf16[3584,128]{1,0:T(8,128)(2,1)S(1)}, u32[]{:S(2)}, u32[]{:S(2)}) %collective-permute-start.2) | collective-permute-done | bytes 917536 | tf_op jit(solution)/shard_map/ppermute | solution.py:384
  115.1 1.4 collective-permute-start.8
  116.4 1.4 collective-permute-start.6
  117.9 2.6 collective-permute-start.7
  120.4 5.0 %all-to-all-start.3 = ((bf16[8,16,64,128]{3,2,1,0:T(8,128)(2,1)}), bf16[8,16,64,128]{3,2,1,0:T(8,128)(2,1)S(1)}, u32[]{:S(2)}, u32[]{:S(2)}) async-start(bf16[8,16,64,128]{3,2,1,0:T(8,128)(2,1)} %turn_act.1), calls=%async_computation.3 | async-start | bytes 4194304 | tf_op jit(solution)/shard_map/all_to_all | solution.py:497
  125.4 1.6 convolution_bitcast_fusion
  127.1 1.1 fusion.1
  129.1 1.5 subtract_convert_fusion
  130.6 1.8 copy-done.4
  132.4 1.8 convolution_convert_fusion.1
  134.3 6.9 %collective-permute-done.6.refs_3_ = bf16[3584,128]{1,0:T(8,128)(2,1)S(1)} collective-permute-done((bf16[3584,128]{1,0:T(8,128)(2,1)}, bf16[3584,128]{1,0:T(8,128)(2,1)S(1)}, u32[]{:S(2)}, u32[]{:S(2)}) %collective-permute-start.6) | collective-permute-done | bytes 917536 | tf_op jit(solution)/shard_map/ppermute | solution.py:384
  141.1 3.4 %pad_maximum_fusion = bf16[512,2048]{1,0:T(8,128)(2,1)} fusion(bf16[128,2048]{1,0:T(8,128)(2,1)} %collective-permute-done.9.refs_11_, bf16[128,2048]{1,0:T(8,128)(2,1)} %collective-permute-done.4.refs_10_, bf16[128,2048]{1,0:T(8,128)(2,1)} %collective-permute-done.8.refs_9_, bf16[128,2048]{1,0:T(8,128)(2,1)} %sketch.3.refs_8_), kind=kLoop, calls=%fused_computation.6 | loop fusion | flops 8388608 | bytes 4194304 | tf_op jit(solution)/shard_map/concatenate | solution.py:498
  144.6 9.8 %part_product.4 = (bf16[224,2048]{1,0:T(8,128)(2,1)}, bf16[224,2048]{1,0:T(8,128)(2,1)}, bf16[224,2048]{1,0:T(8,128)(2,1)}, bf16[224,2048]{1,0:T(8,128)(2,1)}) custom-call(s32[4]{0:T(128)} %pad_add_fusion.coords, bf16[3584,128]{1,0:T(8,128)(2,1)} %bitcast.70, bf16[3584,128]{1,0:T(8,128)(2,1)} %collective-permute-done.5.refs_1_, bf16[3584,128]{1,0:T(8,128)(2,1)} %copy-done.9, ...), custom_call_target="tpu_custom_call" | custom-call | flops 5500000256 | bytes 34000000 | tf_op jit(solution)/shard_map/part_product/pallas_call | solution.py:212
  154.4 1.2 collective-permute-start.14
  155.6 1.4 collective-permute-start.10
  157.0 1.2 collective-permute-start.11
  158.3 1.4 collective-permute-start.12
  159.7 1.2 collective-permute-start.13
  161.0 5.5 %all-to-all-start.4 = ((bf16[16,64,128]{2,1,0:T(8,128)(2,1)}), bf16[16,64,128]{2,1,0:T(8,128)(2,1)S(1)}, u32[]{:S(2)}, u32[]{:S(2)}) async-start(bf16[16,64,128]{2,1,0:T(8,128)(2,1)} %bitcast.20), calls=%async_computation.4 | async-start | bytes 524288 | tf_op jit(solution)/shard_map/all_to_all | solution.py:424
  166.6 15.9 %part_product.5 = (bf16[224,2048]{1,0:T(8,128)(2,1)}, bf16[224,2048]{1,0:T(8,128)(2,1)}, bf16[224,2048]{1,0:T(8,128)(2,1)}, bf16[224,2048]{1,0:T(8,128)(2,1)}, b...) custom-call(s32[4]{0:T(128)} %pad_add_fusion.coords, ...), custom_call_target="tpu_custom_call" | custom-call | flops 8800000000 | bytes 54400000 | tf_op jit(solution)/shard_map/part_product/pallas_call | solution.py:212
  182.5 4.1 %all-to-all-done.4 = bf16[16,64,128]{2,1,0:T(8,128)(2,1)S(1)} async-done(((bf16[16,64,128]{2,1,0:T(8,128)(2,1)}), bf16[16,64,128]{2,1,0:T(8,128)(2,1)S(1)}, u32[]{:S(2)}, u32[]{:S(2)}) %all-to-all-start.4) | async-done | bytes 262176 | tf_op jit(solution)/shard_map/all_to_all | solution.py:424
  186.7 9.7 %part_product.6 = bf16[1024,2048]{1,0:T(8,128)(2,1)} custom-call(s32[4]{0:T(128)} %pad_add_fusion.coords, bf16[8,1024,128]{2,1,0:T(8,128)(2,1)} %bitcast.62, bf16[8,1024,128]{2,1,0:T(8,128)(2,1)} %bitcast.63, bf16[8,1024,128]{2,1,0:T(8,128)(2,1)} %bitcast.64, bf16[8,1024,128]{2,1,0:T(8,128)(2,1)} %bitcast.65, bf16[8,1024,128]{2,1,0:T(8,128)(2,1)} %bitcast.66, ...), custom_call_target="tpu_custom_call" | custom-call | flops 6049999872 | bytes 37400000 | tf_op jit(solution)/shard_map/part_product/pallas_call | solution.py:212
  196.7 2.7 collective-permute-start.16
  200.3 1.8 collective-permute-start.18
  202.8 5.8 %all-to-all-start.5 = ((bf16[16,64,128]{2,1,0:T(8,128)(2,1)}), bf16[16,64,128]{2,1,0:T(8,128)(2,1)S(1)}, u32[]{:S(2)}, u32[]{:S(2)}) async-start(bf16[16,64,128]{2,1,0:T(8,128)(2,1)} %broadcast_in_dim.22), calls=%async_computation.6 | async-start | bytes 524288 | tf_op jit(solution)/shard_map/all_to_all | solution.py:420
  208.7 4.8 %add_terms.1 = (bf16[224,2048]{1,0:T(8,128)(2,1)}, bf16[224,2048]{1,0:T(8,128)(2,1)}, bf16[224,2048]{1,0:T(8,128)(2,1)}, bf16[224,2048]{1,0:T(8,128)(2,1)}) custom-call(bf16[224,2048]{1,0:T(8,128)(2,1)} %get-tuple-element.182.refs_0_, bf16[224,2048]{1,0:T(8,128)(2,1)} %get-tuple-element.183.refs_1_, bf16[224,2048]{1,0:T(8,128)(2,1)} %get-tuple-element.184.refs_2_, ...), custom_call_target="tpu_custom_call" | custom-call | flops 2750000128 | bytes 17000000 | tf_op jit(solution)/shard_map/add_terms/pallas_call | solution.py:282
  213.5 13.1 %all-to-all-done.5 = bf16[16,64,128]{2,1,0:T(8,128)(2,1)S(1)} async-done(((bf16[16,64,128]{2,1,0:T(8,128)(2,1)}), bf16[16,64,128]{2,1,0:T(8,128)(2,1)S(1)}, u32[]{:S(2)}, u32[]{:S(2)}) %all-to-all-start.5) | async-done | bytes 262176 | tf_op jit(solution)/shard_map/all_to_all | solution.py:420
  226.7 2.7 collective-permute-start.20
  230.1 1.9 collective-permute-start.22
  232.4 1.1 fusion.2
  234.5 6.1 %multiply_reduce_fusion = (f32[]{:T(128)}, f32[1024,1792]{1,0:T(8,128)}) fusion(f32[1024,1792]{1,0:T(8,128)S(1)} %fusion.2, f32[1792]{0:T(1024)S(1)} %broadcast_divide_fusion, bf16[1024,1792]{1,0:T(8,128)(2,1)S(1)} %copy-done.5, bf16[1792,128]{1,0:T(8,128)(2,1)S(1)} %copy-done.12, f32[1024,128]{1,0:T(8,128)S(1)} %fusion.8), kind=kOutput, calls=%fused_computation | convolution fusion | flops 480903168 | bytes 19340292 | tf_op jit(solution)/shard_map/dot_general | solution.py:413
  240.5 1.3 broadcast_in_dim_broadcast_in_dim_broadcast_in_dim.3
  241.8 7.6 %all-to-all-start.6 = ((f32[16,8,128]{2,1,0:T(8,128)}), f32[16,8,128]{2,1,0:T(8,128)S(1)}, u32[]{:S(2)}, u32[]{:S(2)}) async-start(f32[16,8,128]{2,1,0:T(8,128)} %broadcast_in_dim_broadcast_in_dim_broadcast_in_dim.3), calls=%async_computation.7 | async-start | bytes 131072 | tf_op jit(solution)/shard_map/all_to_all | solution.py:420
  249.4 9.9 %part_product.7 = (bf16[448,2048]{1,0:T(8,128)(2,1)}, bf16[448,2048]{1,0:T(8,128)(2,1)}) custom-call(s32[4]{0:T(128)} %pad_add_fusion.coords, bf16[3584,128]{1,0:T(8,128)(2,1)} %bitcast.72, bf16[3584,128]{1,0:T(8,128)(2,1)} %collective-permute-done.5.refs_1_, bf16[3584,128]{1,0:T(8,128)(2,1)} %copy-done.9, bf16[3584,128]{1,0:T(8,128)(2,1)} %copy-done.10, ...), custom_call_target="tpu_custom_call" | custom-call | flops 5500000256 | bytes 34000000 | tf_op jit(solution)/shard_map/part_product/pallas_call | solution.py:212
  259.3 6.9 %merge.1 = (f32[112,2048]{1,0:T(8,128)}, bf16[112,2048]{1,0:T(8,128)(2,1)}, bf16[112,2048]{1,0:T(8,128)(2,1)}, bf16[112,2048]{1,0:T(8,128)(2,1)}, f32[112,2048]{...) custom-call(bf16[448,2048]{1,0:T(8,128)(2,1)} %get-tuple-element.198.refs_0_, ...), custom_call_target="tpu_custom_call" | custom-call | flops 3849999872 | bytes 23800000 | tf_op jit(solution)/shard_map/merge/pallas_call | solution.py:312
  266.9 5.3 %all-to-all-start.7 = ((f32[8,8,128]{2,1,0:T(8,128)}), f32[8,8,128]{2,1,0:T(8,128)S(1)}, u32[]{:S(2)}, u32[]{:S(2)}) async-start(f32[8,8,128]{2,1,0:T(8,128)} %broadcast_in_dim.23), calls=%async_computation.8 | async-start | bytes 65536 | tf_op jit(solution)/shard_map/all_to_all | solution.py:420
  272.2 1.3 collective-permute-start.24
  273.6 2.5 collective-permute-start.25
  276.1 1.2 collective-permute-start.26
  277.3 2.4 collective-permute-start.27
  280.9 1.2 collective-permute-start.28
  282.2 10.5 %broadcast_multiply_fusion = f32[1024,1792]{1,0:T(8,128)} fusion(f32[]{:T(128)} %bitcast.22, f32[1024,1792]{1,0:T(8,128)} %get-tuple-element.230, f32[1024,1792]{1,0:T(8,128)} %copy-done.3, f32[1792]{0:T(1024)S(1)} %broadcast_divide_fusion, bf16[1024,1792]{1,0:T(8,128)(2,1)} %copy-done.4), kind=kLoop, calls=%fused_computation.3 | loop fusion | flops 9175040 | bytes 25697284 | tf_op jit(solution)/shard_map/mul | solution.py:549
  292.7 2.0 collective-permute-done.25.refs_3_
  294.7 3.8 %collective-permute-done.27.refs_6_ = bf16[112,2048]{1,0:T(8,128)(2,1)S(1)} collective-permute-done((bf16[112,2048]{1,0:T(8,128)(2,1)}, bf16[112,2048]{1,0:T(8,128)(2,1)S(1)}, u32[]{:S(2)}, u32[]{:S(2)}) %collective-permute-start.27) | collective-permute-done | bytes 458784 | tf_op jit(solution)/shard_map/ppermute | solution.py:375
  300.3 3.5 %finish.1 = f32[224,2048]{1,0:T(8,128)} custom-call(f32[112,2048]{1,0:T(8,128)} %get-tuple-element.218.refs_0_, bf16[112,2048]{1,0:T(8,128)(2,1)} %copy-done.21, bf16[112,2048]{1,0:T(8,128)(2,1)} %copy-done.22, bf16[112,2048]{1,0:T(8,128)(2,1)} %copy-done.23, f32[112,2048]{1,0:T(8,128)} %get-tuple-element.222.refs_4_, bf16[112,2048]{1,0:T(8,128)(2,1)} %copy-done.24, ...), custom_call_target="tpu_custom_call" | custom-call | flops 2200000000 | bytes 13600000 | tf_op jit(solution)/shard_map/finish/pallas_call | solution.py:347
  303.8 1.8 convert_element_type.73
  (112 shorter events, 12.1 us)
Async XLA Ops:
  7.2 118.3 %copy-start = (f32[128,128]{1,0:T(8,128)S(1)}, f32[128,128]{1,0:T(8,128)}, u32[]{:S(2)}) copy-start(f32[128,128]{1,0:T(8,128)} %param.25) | copy-start | bytes 196612
  7.8 3.9 %copy-start.15 = (bf16[64,128]{1,0:T(8,128)(2,1)S(1)}, bf16[64,128]{1,0:T(8,128)(2,1)}, u32[]{:S(2)}) copy-start(bf16[64,128]{1,0:T(8,128)(2,1)} %param.23) | copy-start | bytes 49156
  12.5 42.7 %all-to-all-start = ((bf16[16,64,128]{2,1,0:T(8,128)(2,1)}), bf16[16,64,128]{2,1,0:T(8,128)(2,1)S(1)}, u32[]{:S(2)}, u32[]{:S(2)}) async-start(bf16[16,64,128]{2,1,0:T(8,128)(2,1)} %broadcast_in_dim.16), calls=%async_computation | async-start | bytes 524288 | tf_op jit(solution)/shard_map/all_to_all | solution.py:420
  22.0 119.2 %all-gather.3.cloned.1.call-start = ((), (), s32[]{:S(2)}) async-start(), calls=%async_computation.10 | async-start | bytes 4718592 | tf_op jit(solution)/shard_map/all_gather | solution.py:474
  22.0 37.2 %collective-permute-start = (bf16[3584,128]{1,0:T(8,128)(2,1)}, bf16[3584,128]{1,0:T(8,128)(2,1)S(1)}, u32[]{:S(2)}, u32[]{:S(2)}) collective-permute-start(bf16[3584,128]{1,0:T(8,128)(2,1)} %bitcast.81), channel_id=1, source_target_pairs={{0,8},{1,9},{4,12},{5,13},{8,0},{9,1},{12,4},{13,5},{2,10},{3,11},... | collective-permute-start | bytes 2752520 | tf_op jit(solution)/shard_map/ppermute | solution.py:384
  25.0 43.2 %collective-permute-start.1 = (bf16[3584,128]{1,0:T(8,128)(2,1)}, bf16[3584,128]{1,0:T(8,128)(2,1)S(1)}, u32[]{:S(2)}, u32[]{:S(2)}) collective-permute-start(bf16[3584,128]{1,0:T(8,128)(2,1)} %bitcast.80), channel_id=1, source_target_pairs={{0,9},{1,8},{4,13},{5,12},{8,1},{9,0},{12,5},{13,4},{2,11},{3,10},... | collective-permute-start | bytes 2752520 | tf_op jit(solution)/shard_map/ppermute | solution.py:384
  47.4 7.7 %copy-start.17 = (f32[1024]{0:T(1024)S(1)}, f32[1024]{0:T(1024)}, u32[]{:S(2)}) copy-start(f32[1024]{0:T(1024)} %param.21) | copy-start | bytes 12292
  47.4 7.7 %copy-start.14 = (bf16[224,128]{1,0:T(8,128)(2,1)S(1)}, bf16[224,128]{1,0:T(8,128)(2,1)}, u32[]{:S(2)}) copy-start(bf16[224,128]{1,0:T(8,128)(2,1)} %param.24) | copy-start | bytes 172036
  55.4 17.0 %copy-start.16 = (f32[1792]{0:T(1024)S(1)}, f32[1792]{0:T(1024)}, u32[]{:S(2)}) copy-start(f32[1792]{0:T(1024)} %param.22) | copy-start | bytes 21508
  59.2 26.8 %copy-start.7 = (bf16[3584,128]{1,0:T(8,128)(2,1)}, bf16[3584,128]{1,0:T(8,128)(2,1)S(1)}, u32[]{:S(2)}) copy-start(bf16[3584,128]{1,0:T(8,128)(2,1)S(1)} %collective-permute-done.refs_4_) | copy-start | bytes 2752516
  68.1 17.8 %copy-start.8 = (bf16[3584,128]{1,0:T(8,128)(2,1)}, bf16[3584,128]{1,0:T(8,128)(2,1)S(1)}, u32[]{:S(2)}) copy-start(bf16[3584,128]{1,0:T(8,128)(2,1)S(1)} %collective-permute-done.1.refs_5_) | copy-start | bytes 2752516
  68.2 18.4 %all-to-all-start.1 = ((bf16[8,32,1792]{2,1,0:T(8,128)(2,1)}), bf16[8,32,1792]{2,1,0:T(8,128)(2,1)}, u32[]{:S(2)}, u32[]{:S(2)}) async-start(bf16[8,32,1792]{2,1,0:T(8,128)(2,1)} %pad_maximum_fusion.1), calls=%async_computation.1 | async-start | bytes 1835008 | tf_op jit(solution)/shard_map/all_to_all | solution.py:476
  72.4 25.1 %collective-permute-start.4 = (bf16[128,2048]{1,0:T(8,128)(2,1)}, bf16[128,2048]{1,0:T(8,128)(2,1)}, u32[]{:S(2)}, u32[]{:S(2)}) collective-permute-start(bf16[128,2048]{1,0:T(8,128)(2,1)} %sketch.3.refs_8_), channel_id=1, source_target_pairs={{0,2},{16,18},{2,0},{18,16},{1,3},{17,19},{3,1},{19,17},{4,6},{20,... | collective-permute-start | bytes 1572872 | tf_op jit(solution)/shard_map/ppermute | solution.py:372
  75.8 39.1 %collective-permute-start.2 = (bf16[3584,128]{1,0:T(8,128)(2,1)}, bf16[3584,128]{1,0:T(8,128)(2,1)S(1)}, u32[]{:S(2)}, u32[]{:S(2)}) collective-permute-start(bf16[3584,128]{1,0:T(8,128)(2,1)} %bitcast.79), channel_id=1, source_target_pairs={{0,4},{1,5},{4,8},{5,9},{8,12},{9,13},{12,0},{13,1},{2,6},{3,7},{6... | collective-permute-start | bytes 2752520 | tf_op jit(solution)/shard_map/ppermute | solution.py:384
  76.0 38.9 %collective-permute-start.3 = (bf16[3584,128]{1,0:T(8,128)(2,1)}, bf16[3584,128]{1,0:T(8,128)(2,1)}, u32[]{:S(2)}, u32[]{:S(2)}) collective-permute-start(bf16[3584,128]{1,0:T(8,128)(2,1)} %bitcast.78), channel_id=1, source_target_pairs={{0,12},{1,13},{4,0},{5,1},{8,4},{9,5},{12,8},{13,9},{2,14},{3,15},... | collective-permute-start | bytes 2752520 | tf_op jit(solution)/shard_map/ppermute | solution.py:384
  78.5 36.4 %collective-permute-start.5 = (bf16[3584,128]{1,0:T(8,128)(2,1)}, bf16[3584,128]{1,0:T(8,128)(2,1)}, u32[]{:S(2)}, u32[]{:S(2)}) collective-permute-start(bf16[3584,128]{1,0:T(8,128)(2,1)} %bitcast.77), channel_id=1, source_target_pairs={{0,1},{1,0},{4,5},{5,4},{8,9},{9,8},{12,13},{13,12},{2,3},{3,2},{6... | collective-permute-start | bytes 2752520 | tf_op jit(solution)/shard_map/ppermute | solution.py:384
  88.7 31.8 %all-to-all-start.2 = ((bf16[8,16,1792]{2,1,0:T(8,128)(2,1)}), bf16[8,16,1792]{2,1,0:T(8,128)(2,1)}, u32[]{:S(2)}, u32[]{:S(2)}) async-start(bf16[8,16,1792]{2,1,0:T(8,128)(2,1)} %broadcast_in_dim.21), calls=%async_computation.2 | async-start | bytes 917504 | tf_op jit(solution)/shard_map/all_to_all | solution.py:420
  114.9 5.5 %copy-start.9 = (bf16[3584,128]{1,0:T(8,128)(2,1)}, bf16[3584,128]{1,0:T(8,128)(2,1)S(1)}, u32[]{:S(2)}) copy-start(bf16[3584,128]{1,0:T(8,128)(2,1)S(1)} %collective-permute-done.2.refs_2_) | copy-start | bytes 2752516
  114.9 19.3 %collective-permute-start.9 = (bf16[128,2048]{1,0:T(8,128)(2,1)}, bf16[128,2048]{1,0:T(8,128)(2,1)}, u32[]{:S(2)}, u32[]{:S(2)}) collective-permute-start(bf16[128,2048]{1,0:T(8,128)(2,1)} %sketch.3.refs_8_), channel_id=1, source_target_pairs={{0,18},{16,0},{2,16},{18,2},{1,19},{17,1},{3,17},{19,3},{4,22},{20... | collective-permute-start | bytes 1572872 | tf_op jit(solution)/shard_map/ppermute | solution.py:372
  115.1 19.2 %collective-permute-start.8 = (bf16[128,2048]{1,0:T(8,128)(2,1)}, bf16[128,2048]{1,0:T(8,128)(2,1)}, u32[]{:S(2)}, u32[]{:S(2)}) collective-permute-start(bf16[128,2048]{1,0:T(8,128)(2,1)} %sketch.3.refs_8_), channel_id=1, source_target_pairs={{0,16},{16,2},{2,18},{18,0},{1,17},{17,3},{3,19},{19,1},{4,20},{20... | collective-permute-start | bytes 1572872 | tf_op jit(solution)/shard_map/ppermute | solution.py:372
  116.4 24.7 %collective-permute-start.6 = (bf16[3584,128]{1,0:T(8,128)(2,1)}, bf16[3584,128]{1,0:T(8,128)(2,1)S(1)}, u32[]{:S(2)}, u32[]{:S(2)}) collective-permute-start(bf16[3584,128]{1,0:T(8,128)(2,1)} %bitcast.76), channel_id=1, source_target_pairs={{0,5},{1,4},{4,9},{5,8},{8,13},{9,12},{12,1},{13,0},{2,7},{3,6},{6... | collective-permute-start | bytes 2752520 | tf_op jit(solution)/shard_map/ppermute | solution.py:384
  117.9 23.3 %collective-permute-start.7 = (bf16[3584,128]{1,0:T(8,128)(2,1)}, bf16[3584,128]{1,0:T(8,128)(2,1)}, u32[]{:S(2)}, u32[]{:S(2)}) collective-permute-start(bf16[3584,128]{1,0:T(8,128)(2,1)} %bitcast.75), channel_id=1, source_target_pairs={{0,13},{1,12},{4,1},{5,0},{8,5},{9,4},{12,9},{13,8},{2,15},{3,14},... | collective-permute-start | bytes 2752520 | tf_op jit(solution)/shard_map/ppermute | solution.py:384
  120.4 33.9 %all-to-all-start.3 = ((bf16[8,16,64,128]{3,2,1,0:T(8,128)(2,1)}), bf16[8,16,64,128]{3,2,1,0:T(8,128)(2,1)S(1)}, u32[]{:S(2)}, u32[]{:S(2)}) async-start(bf16[8,16,64,128]{3,2,1,0:T(8,128)(2,1)} %turn_act.1), calls=%async_computation.3 | async-start | bytes 4194304 | tf_op jit(solution)/shard_map/all_to_all | solution.py:497
  127.0 2.0 copy-start.6
  129.1 3.3 %copy-start.11 = (bf16[1792,128]{1,0:T(8,128)(2,1)S(1)}, bf16[1792,128]{1,0:T(8,128)(2,1)}, u32[]{:S(2)}) copy-start(bf16[1792,128]{1,0:T(8,128)(2,1)} %multiply_convert_fusion) | copy-start | bytes 1376260
  130.6 1.8 copy-start.4
  141.1 3.4 %copy-start.10 = (bf16[3584,128]{1,0:T(8,128)(2,1)}, bf16[3584,128]{1,0:T(8,128)(2,1)S(1)}, u32[]{:S(2)}) copy-start(bf16[3584,128]{1,0:T(8,128)(2,1)S(1)} %collective-permute-done.6.refs_3_) | copy-start | bytes 2752516
  154.4 28.1 %copy-start.2 = (bf16[8,16,64,128]{3,2,1,0:T(8,128)(2,1)}, bf16[8,16,64,128]{3,2,1,0:T(8,128)(2,1)S(1)}, u32[]{:S(2)}) copy-start(bf16[8,16,64,128]{3,2,1,0:T(8,128)(2,1)S(1)} %all-to-all-done.3) | copy-start | bytes 6291460
  154.4 32.3 %collective-permute-start.14 = (bf16[512,2048]{1,0:T(8,128)(2,1)}, bf16[512,2048]{1,0:T(8,128)(2,1)}, u32[]{:S(2)}, u32[]{:S(2)}) collective-permute-start(bf16[512,2048]{1,0:T(8,128)(2,1)} %pad_maximum_fusion), channel_id=1, source_target_pairs={{0,1},{1,0},{2,3},{3,2},{4,5},{5,4},{6,7},{7,6},{8,9},{9,8},{10,11... | collective-permute-start | bytes 6291464 | tf_op jit(solution)/shard_map/ppermute | solution.py:379
  155.6 31.1 %collective-permute-start.10 = (bf16[224,2048]{1,0:T(8,128)(2,1)}, bf16[224,2048]{1,0:T(8,128)(2,1)S(1)}, u32[]{:S(2)}, u32[]{:S(2)}) collective-permute-start(bf16[224,2048]{1,0:T(8,128)(2,1)} %get-tuple-element.160), channel_id=1, source_target_pairs={{0,32},{32,64},{64,96},{96,0},{1,33},{33,65},{65,97},{97,1},{2,34}... | collective-permute-start | bytes 2752520 | tf_op jit(solution)/shard_map/ppermute | solution.py:375
  157.0 29.6 %collective-permute-start.11 = (bf16[224,2048]{1,0:T(8,128)(2,1)}, bf16[224,2048]{1,0:T(8,128)(2,1)}, u32[]{:S(2)}, u32[]{:S(2)}) collective-permute-start(bf16[224,2048]{1,0:T(8,128)(2,1)} %get-tuple-element.161), channel_id=1, source_target_pairs={{0,96},{32,0},{64,32},{96,64},{1,97},{33,1},{65,33},{97,65},{2,98}... | collective-permute-start | bytes 2752520 | tf_op jit(solution)/shard_map/ppermute | solution.py:375
  158.3 28.4 %collective-permute-start.12 = (bf16[224,2048]{1,0:T(8,128)(2,1)}, bf16[224,2048]{1,0:T(8,128)(2,1)}, u32[]{:S(2)}, u32[]{:S(2)}) collective-permute-start(bf16[224,2048]{1,0:T(8,128)(2,1)} %get-tuple-element.162), channel_id=1, source_target_pairs={{0,16},{16,2},{2,18},{18,0},{1,17},{17,3},{3,19},{19,1},{4,20},{20... | collective-permute-start | bytes 2752520 | tf_op jit(solution)/shard_map/ppermute | solution.py:372
  159.7 27.0 %collective-permute-start.13 = (bf16[224,2048]{1,0:T(8,128)(2,1)}, bf16[224,2048]{1,0:T(8,128)(2,1)}, u32[]{:S(2)}, u32[]{:S(2)}) collective-permute-start(bf16[224,2048]{1,0:T(8,128)(2,1)} %get-tuple-element.163), channel_id=1, source_target_pairs={{0,18},{16,0},{2,16},{18,2},{1,19},{17,1},{3,17},{19,3},{4,22},{20... | collective-permute-start | bytes 2752520 | tf_op jit(solution)/shard_map/ppermute | solution.py:372
  161.0 25.6 %all-to-all-start.4 = ((bf16[16,64,128]{2,1,0:T(8,128)(2,1)}), bf16[16,64,128]{2,1,0:T(8,128)(2,1)S(1)}, u32[]{:S(2)}, u32[]{:S(2)}) async-start(bf16[16,64,128]{2,1,0:T(8,128)(2,1)} %bitcast.20), calls=%async_computation.4 | async-start | bytes 524288 | tf_op jit(solution)/shard_map/all_to_all | solution.py:424
  166.5 137.3 %reduce-scatter.2.cloned.1.call-start = ((), (), s32[]{:S(2)}) async-start(), calls=%async_computation.9 | async-start | bytes 4456448 | tf_op jit(solution)/shard_map/reduce_scatter | solution.py:526
  186.7 9.7 %copy-start.20 = (bf16[224,2048]{1,0:T(8,128)(2,1)}, bf16[224,2048]{1,0:T(8,128)(2,1)S(1)}, u32[]{:S(2)}) copy-start(bf16[224,2048]{1,0:T(8,128)(2,1)S(1)} %collective-permute-done.10.refs_4_) | copy-start | bytes 2752516
  196.4 30.1 %collective-permute-start.15 = (bf16[224,2048]{1,0:T(8,128)(2,1)}, bf16[224,2048]{1,0:T(8,128)(2,1)S(1)}, u32[]{:S(2)}, u32[]{:S(2)}) collective-permute-start(bf16[224,2048]{1,0:T(8,128)(2,1)} %get-tuple-element.178), channel_id=1, source_target_pairs={{0,32},{32,64},{64,96},{96,0},{1,33},{33,65},{65,97},{97,1},{2,34}... | collective-permute-start | bytes 2752520 | tf_op jit(solution)/shard_map/ppermute | solution.py:375
  196.7 29.8 %collective-permute-start.16 = (bf16[224,2048]{1,0:T(8,128)(2,1)}, bf16[224,2048]{1,0:T(8,128)(2,1)S(1)}, u32[]{:S(2)}, u32[]{:S(2)}) collective-permute-start(bf16[224,2048]{1,0:T(8,128)(2,1)} %get-tuple-element.179), channel_id=1, source_target_pairs={{0,96},{32,0},{64,32},{96,64},{1,97},{33,1},{65,33},{97,65},{2,98}... | collective-permute-start | bytes 2752520 | tf_op jit(solution)/shard_map/ppermute | solution.py:375
  199.4 27.2 %collective-permute-start.17 = (bf16[224,2048]{1,0:T(8,128)(2,1)}, bf16[224,2048]{1,0:T(8,128)(2,1)}, u32[]{:S(2)}, u32[]{:S(2)}) collective-permute-start(bf16[224,2048]{1,0:T(8,128)(2,1)} %get-tuple-element.180), channel_id=1, source_target_pairs={{0,16},{16,2},{2,18},{18,0},{1,17},{17,3},{3,19},{19,1},{4,20},{20... | collective-permute-start | bytes 2752520 | tf_op jit(solution)/shard_map/ppermute | solution.py:372
  200.3 26.3 %collective-permute-start.18 = (bf16[224,2048]{1,0:T(8,128)(2,1)}, bf16[224,2048]{1,0:T(8,128)(2,1)}, u32[]{:S(2)}, u32[]{:S(2)}) collective-permute-start(bf16[224,2048]{1,0:T(8,128)(2,1)} %get-tuple-element.181), channel_id=1, source_target_pairs={{0,18},{16,0},{2,16},{18,2},{1,19},{17,1},{3,17},{19,3},{4,22},{20... | collective-permute-start | bytes 2752520 | tf_op jit(solution)/shard_map/ppermute | solution.py:372
  202.8 23.7 %all-to-all-start.5 = ((bf16[16,64,128]{2,1,0:T(8,128)(2,1)}), bf16[16,64,128]{2,1,0:T(8,128)(2,1)S(1)}, u32[]{:S(2)}, u32[]{:S(2)}) async-start(bf16[16,64,128]{2,1,0:T(8,128)(2,1)} %broadcast_in_dim.22), calls=%async_computation.6 | async-start | bytes 524288 | tf_op jit(solution)/shard_map/all_to_all | solution.py:420
  208.7 23.3 %copy-start.13 = (f32[128,128]{1,0:T(8,128)S(1)}, f32[128,128]{1,0:T(8,128)}, u32[]{:S(2)}) copy-start(f32[128,128]{1,0:T(8,128)} %param.26) | copy-start | bytes 196612
  208.7 23.7 %copy-start.12 = (bf16[1792,128]{1,0:T(8,128)(2,1)S(1)}, bf16[1792,128]{1,0:T(8,128)(2,1)}, u32[]{:S(2)}) copy-start(bf16[1792,128]{1,0:T(8,128)(2,1)} %multiply_convert_fusion) | copy-start | bytes 1376260
  226.5 7.0 %copy-start.18 = (bf16[224,2048]{1,0:T(8,128)(2,1)}, bf16[224,2048]{1,0:T(8,128)(2,1)S(1)}, u32[]{:S(2)}) copy-start(bf16[224,2048]{1,0:T(8,128)(2,1)S(1)} %collective-permute-done.15.refs_2_) | copy-start | bytes 2752516
  226.6 7.0 %copy-start.19 = (bf16[224,2048]{1,0:T(8,128)(2,1)}, bf16[224,2048]{1,0:T(8,128)(2,1)S(1)}, u32[]{:S(2)}) copy-start(bf16[224,2048]{1,0:T(8,128)(2,1)S(1)} %collective-permute-done.16.refs_3_) | copy-start | bytes 2752516
  226.6 32.7 %collective-permute-start.19 = (bf16[224,2048]{1,0:T(8,128)(2,1)}, bf16[224,2048]{1,0:T(8,128)(2,1)}, u32[]{:S(2)}, u32[]{:S(2)}) collective-permute-start(bf16[224,2048]{1,0:T(8,128)(2,1)} %get-tuple-element.199), channel_id=1, source_target_pairs={{0,32},{32,64},{64,96},{96,0},{1,33},{33,65},{65,97},{97,1},{2,34}... | collective-permute-start | bytes 2752520 | tf_op jit(solution)/shard_map/ppermute | solution.py:375
  226.7 32.6 %collective-permute-start.20 = (bf16[224,2048]{1,0:T(8,128)(2,1)}, bf16[224,2048]{1,0:T(8,128)(2,1)}, u32[]{:S(2)}, u32[]{:S(2)}) collective-permute-start(bf16[224,2048]{1,0:T(8,128)(2,1)} %get-tuple-element.202), channel_id=1, source_target_pairs={{0,96},{32,0},{64,32},{96,64},{1,97},{33,1},{65,33},{97,65},{2,98}... | collective-permute-start | bytes 2752520 | tf_op jit(solution)/shard_map/ppermute | solution.py:375
  229.3 30.0 %collective-permute-start.21 = (bf16[224,2048]{1,0:T(8,128)(2,1)}, bf16[224,2048]{1,0:T(8,128)(2,1)}, u32[]{:S(2)}, u32[]{:S(2)}) collective-permute-start(bf16[224,2048]{1,0:T(8,128)(2,1)} %get-tuple-element.204), channel_id=1, source_target_pairs={{0,16},{16,2},{2,18},{18,0},{1,17},{17,3},{3,19},{19,1},{4,20},{20... | collective-permute-start | bytes 2752520 | tf_op jit(solution)/shard_map/ppermute | solution.py:372
  230.1 29.2 %collective-permute-start.22 = (bf16[224,2048]{1,0:T(8,128)(2,1)}, bf16[224,2048]{1,0:T(8,128)(2,1)}, u32[]{:S(2)}, u32[]{:S(2)}) collective-permute-start(bf16[224,2048]{1,0:T(8,128)(2,1)} %get-tuple-element.207), channel_id=1, source_target_pairs={{0,18},{16,0},{2,16},{18,2},{1,19},{17,1},{3,17},{19,3},{4,22},{20... | collective-permute-start | bytes 2752520 | tf_op jit(solution)/shard_map/ppermute | solution.py:372
  232.4 2.1 copy-start.5
  234.5 6.1 %copy-start.3 = (f32[1024,1792]{1,0:T(8,128)}, f32[1024,1792]{1,0:T(8,128)S(1)}, u32[]{:S(2)}) copy-start(f32[1024,1792]{1,0:T(8,128)S(1)} %fusion.2) | copy-start | bytes 22020100
  241.8 17.4 %all-to-all-start.6 = ((f32[16,8,128]{2,1,0:T(8,128)}), f32[16,8,128]{2,1,0:T(8,128)S(1)}, u32[]{:S(2)}, u32[]{:S(2)}) async-start(f32[16,8,128]{2,1,0:T(8,128)} %broadcast_in_dim_broadcast_in_dim_broadcast_in_dim.3), calls=%async_computation.7 | async-start | bytes 131072 | tf_op jit(solution)/shard_map/all_to_all | solution.py:420
  266.2 14.7 %collective-permute-start.23 = (bf16[112,2048]{1,0:T(8,128)(2,1)}, bf16[112,2048]{1,0:T(8,128)(2,1)S(1)}, u32[]{:S(2)}, u32[]{:S(2)}) collective-permute-start(bf16[112,2048]{1,0:T(8,128)(2,1)} %get-tuple-element.219), channel_id=1, source_target_pairs={{0,16},{16,2},{2,18},{18,0},{1,17},{17,3},{3,19},{19,1},{4,20},{20... | collective-permute-start | bytes 1376264 | tf_op jit(solution)/shard_map/ppermute | solution.py:372
  266.9 12.8 %all-to-all-start.7 = ((f32[8,8,128]{2,1,0:T(8,128)}), f32[8,8,128]{2,1,0:T(8,128)S(1)}, u32[]{:S(2)}, u32[]{:S(2)}) async-start(f32[8,8,128]{2,1,0:T(8,128)} %broadcast_in_dim.23), calls=%async_computation.8 | async-start | bytes 65536 | tf_op jit(solution)/shard_map/all_to_all | solution.py:420
  272.2 20.4 %collective-permute-start.24 = (bf16[112,2048]{1,0:T(8,128)(2,1)}, bf16[112,2048]{1,0:T(8,128)(2,1)S(1)}, u32[]{:S(2)}, u32[]{:S(2)}) collective-permute-start(bf16[112,2048]{1,0:T(8,128)(2,1)} %get-tuple-element.220), channel_id=1, source_target_pairs={{0,2},{16,18},{2,0},{18,16},{1,3},{17,19},{3,1},{19,17},{4,6},{20,... | collective-permute-start | bytes 1376264 | tf_op jit(solution)/shard_map/ppermute | solution.py:372
  273.6 21.1 %collective-permute-start.25 = (bf16[112,2048]{1,0:T(8,128)(2,1)}, bf16[112,2048]{1,0:T(8,128)(2,1)S(1)}, u32[]{:S(2)}, u32[]{:S(2)}) collective-permute-start(bf16[112,2048]{1,0:T(8,128)(2,1)} %get-tuple-element.221), channel_id=1, source_target_pairs={{0,18},{16,0},{2,16},{18,2},{1,19},{17,1},{3,17},{19,3},{4,22},{20... | collective-permute-start | bytes 1376264 | tf_op jit(solution)/shard_map/ppermute | solution.py:372
  276.1 18.6 %collective-permute-start.26 = (bf16[112,2048]{1,0:T(8,128)(2,1)}, bf16[112,2048]{1,0:T(8,128)(2,1)S(1)}, u32[]{:S(2)}, u32[]{:S(2)}) collective-permute-start(bf16[112,2048]{1,0:T(8,128)(2,1)} %get-tuple-element.223), channel_id=1, source_target_pairs={{0,32},{32,64},{64,96},{96,0},{1,33},{33,65},{65,97},{97,1},{2,34}... | collective-permute-start | bytes 1376264 | tf_op jit(solution)/shard_map/ppermute | solution.py:375
  277.3 21.2 %collective-permute-start.27 = (bf16[112,2048]{1,0:T(8,128)(2,1)}, bf16[112,2048]{1,0:T(8,128)(2,1)S(1)}, u32[]{:S(2)}, u32[]{:S(2)}) collective-permute-start(bf16[112,2048]{1,0:T(8,128)(2,1)} %get-tuple-element.224), channel_id=1, source_target_pairs={{0,64},{32,96},{64,0},{96,32},{1,65},{33,97},{65,1},{97,33},{2,66}... | collective-permute-start | bytes 1376264 | tf_op jit(solution)/shard_map/ppermute | solution.py:375
  280.9 11.7 %copy-start.21 = (bf16[112,2048]{1,0:T(8,128)(2,1)}, bf16[112,2048]{1,0:T(8,128)(2,1)S(1)}, u32[]{:S(2)}) copy-start(bf16[112,2048]{1,0:T(8,128)(2,1)S(1)} %collective-permute-done.23.refs_1_) | copy-start | bytes 1376260
  280.9 18.5 %collective-permute-start.28 = (bf16[112,2048]{1,0:T(8,128)(2,1)}, bf16[112,2048]{1,0:T(8,128)(2,1)S(1)}, u32[]{:S(2)}, u32[]{:S(2)}) collective-permute-start(bf16[112,2048]{1,0:T(8,128)(2,1)} %get-tuple-element.225), channel_id=1, source_target_pairs={{0,96},{32,0},{64,32},{96,64},{1,97},{33,1},{65,33},{97,65},{2,98}... | collective-permute-start | bytes 1376264 | tf_op jit(solution)/shard_map/ppermute | solution.py:375
  282.2 23.4 %copy-start.1 = (f32[128,128]{1,0:T(8,128)S(1)}, f32[128,128]{1,0:T(8,128)}, u32[]{:S(2)}) copy-start(f32[128,128]{1,0:T(8,128)} %param.25) | copy-start | bytes 196612
  292.7 6.8 %copy-start.22 = (bf16[112,2048]{1,0:T(8,128)(2,1)}, bf16[112,2048]{1,0:T(8,128)(2,1)S(1)}, u32[]{:S(2)}) copy-start(bf16[112,2048]{1,0:T(8,128)(2,1)S(1)} %collective-permute-done.24.refs_2_) | copy-start | bytes 1376260
  294.7 4.8 %copy-start.23 = (bf16[112,2048]{1,0:T(8,128)(2,1)}, bf16[112,2048]{1,0:T(8,128)(2,1)S(1)}, u32[]{:S(2)}) copy-start(bf16[112,2048]{1,0:T(8,128)(2,1)S(1)} %collective-permute-done.25.refs_3_) | copy-start | bytes 1376260
  294.7 4.8 %copy-start.24 = (bf16[112,2048]{1,0:T(8,128)(2,1)}, bf16[112,2048]{1,0:T(8,128)(2,1)S(1)}, u32[]{:S(2)}) copy-start(bf16[112,2048]{1,0:T(8,128)(2,1)S(1)} %collective-permute-done.26.refs_5_) | copy-start | bytes 1376260
  (2 other events, 1.8 us)
Sparse Core Ops, SparseCore 0:
  68.3 48.5 all-gather.2
  196.6 78.4 reduce-scatter.1
